TPU v7x, 32 devices: a whole 2x2x4 slice. The times are simulated.
32 devices in a mesh: wide: 8 (over z, x), narrow: 4 (over y, core).
Axes of the slice: x: 2, y: 2, z: 4, core: 2. Of those that a mesh axis runs over, the one named last changes fastest.
Arguments:
- tokens: bfloat16 [64, 1024, 768], P(('wide', 'narrow')), may hold values from -6 to 6
- cotangent: bfloat16 [64, 1024, 768], P(('wide', 'narrow')), may hold values from -6 to 6
- row_kind: int32 [64], P(('wide', 'narrow')), may hold values from 0 to 1
- grad_mask: int32 [64, 1024], P(('wide', 'narrow')), may hold values 0 or 1
- w_qkv: bfloat16 [768, 2304], P('wide'), may hold values from -0.3125 to 0.3125
- w_out: bfloat16 [768, 768], P('wide'), may hold values from -0.625 to 0.625
- w_in: bfloat16 [768, 3072], P('wide'), may hold values from -0.21875 to 0.21875
- w_back: bfloat16 [3072, 768], P('wide'), may hold values from -0.109375 to 0.109375
- norm_gain: bfloat16 [2, 768], P(None, 'wide'), may hold values from 0.5 to 1.5
- norm_shift: bfloat16 [2, 768], P(None, 'wide'), may hold values from -1 to 1
- proj_bias: bfloat16 [4, 768], P(None, 'wide'), may hold values from -1 to 1
- ffn_bias: bfloat16 [3072], P('wide'), may hold values from -1 to 1
Outputs:
- layer_out: bfloat16 [64, 1024, 768], P(('wide', 'narrow'))
- input_grad: float32 [64, 1024, 768], P(('wide', 'narrow'))
- grad_qkv: float32 [768, 2304], P('wide')
- grad_out: float32 [768, 768], P('wide')
- grad_in: float32 [768, 3072], P('wide')
- grad_back: float32 [3072, 768], P('wide')
- grad_gain: float32 [2, 768], P(None, 'wide')
- grad_shift: float32 [2, 768], P(None, 'wide')
- grad_proj_bias: float32 [4, 768], P(None, 'wide')
- grad_ffn_bias: float32 [3072], P('wide')
All inputs are finite; a program needn't handle non-finite values. No bound on the sum of `grad_mask` on one device may be relied on, other than what follows from the above.
Results may differ from a plain program's by a relative error of at most 0.02.
Values may be sent and summed in bfloat16 or wider, within the bound.
No kernel may reach another device: no remote copies, remote signals or barrier semaphores. Data moves between devices by JAX's collectives and lax.ppermute only.
A program may use at most 384 MiB of HBM per device.

v0:
```python
import jax
import jax.numpy as jnp
from jax import lax
from jax.sharding import PartitionSpec as P

HEADS = 12


EPSILON = 1e-05
ROOT_TWO_PI = 0.7978845608028654
CUBIC = 0.044715


def normalize(values, gain, shift):
    centre = jnp.mean(values, axis=-1, keepdims=True)
    centred = values - centre
    variance = jnp.mean(centred * centred, axis=-1, keepdims=True)
    inv_std = lax.rsqrt(variance + EPSILON)
    scaled = centred * inv_std
    return (scaled, inv_std, scaled * gain + shift)


def smooth_gate(values):
    return (
        0.5 * values * (1.0 + jnp.tanh(ROOT_TWO_PI * (values + CUBIC * values * values * values)))
    )


def gate_slope(values):
    bent = jnp.tanh(ROOT_TWO_PI * (values + CUBIC * values * values * values))
    return 0.5 * (1.0 + bent) + 0.5 * values * (1.0 - bent * bent) * ROOT_TWO_PI * (
        1.0 + 3.0 * CUBIC * values * values
    )


def norm_back(grad_norm, scaled, inv_std, gain):
    grad_scaled = grad_norm * gain
    first_mean = jnp.mean(grad_scaled, axis=-1, keepdims=True)
    second_mean = jnp.mean(grad_scaled * scaled, axis=-1, keepdims=True)
    return inv_std * (grad_scaled - first_mean - scaled * second_mean)


def attend(query, keys, value):
    length = query.shape[0]
    block = min(512, length)
    factor = query.shape[2] ** (-0.5)
    outputs = []
    logsums = []
    for first in range(0, length, block):
        part = query[first : first + block]
        scores = jnp.einsum("qhd,khd->hqk", part, keys, preferred_element_type=jnp.float32) * factor
        peak = jnp.max(scores, axis=-1, keepdims=True)
        expo = jnp.exp(scores - peak)
        totals = jnp.sum(expo, axis=-1, keepdims=True)
        probs = (expo / totals).astype(jnp.bfloat16)
        outputs.append(jnp.einsum("hqk,khd->qhd", probs, value, preferred_element_type=jnp.float32))
        logsums.append(peak + jnp.log(totals))
    return (jnp.concatenate(outputs, axis=0), jnp.concatenate(logsums, axis=1))


def attend_back(query, keys, value, grad_mixed, logsum):
    length = query.shape[0]
    block = min(512, length)
    factor = query.shape[2] ** (-0.5)
    grad_query = []
    grad_keys = jnp.zeros(keys.shape, jnp.float32)
    grad_value = jnp.zeros(value.shape, jnp.float32)
    for first in range(0, length, block):
        part = query[first : first + block]
        grad_part = grad_mixed[first : first + block]
        scores = jnp.einsum("qhd,khd->hqk", part, keys, preferred_element_type=jnp.float32) * factor
        probs = jnp.exp(scores - logsum[:, first : first + block])
        rounded = probs.astype(jnp.bfloat16)
        grad_probs = jnp.einsum(
            "qhd,khd->hqk", grad_part, value, preferred_element_type=jnp.float32
        )
        inner = jnp.sum(probs * grad_probs, axis=-1, keepdims=True)
        grad_scores = (probs * (grad_probs - inner)).astype(jnp.bfloat16)
        grad_query.append(
            jnp.einsum("hqk,khd->qhd", grad_scores, keys, preferred_element_type=jnp.float32)
            * factor
        )
        grad_keys = (
            grad_keys
            + jnp.einsum("hqk,qhd->khd", grad_scores, part, preferred_element_type=jnp.float32)
            * factor
        )
        grad_value = grad_value + jnp.einsum(
            "hqk,qhd->khd", rounded, grad_part, preferred_element_type=jnp.float32
        )
    return (jnp.concatenate(grad_query, axis=0), grad_keys, grad_value)


def body(
    tokens,
    cotangent,
    row_kind,
    grad_mask,
    w_qkv,
    w_out,
    w_in,
    w_back,
    norm_gain,
    norm_shift,
    proj_bias,
    ffn_bias,
):
    rows, length, width = tokens.shape
    count = rows * length
    head_size = width // HEADS
    qkv_full, out_full, gain_full, shift_full, bias_full = (
        lax.all_gather(w_qkv, "wide", axis=0, tiled=True),
        lax.all_gather(w_out, "wide", axis=0, tiled=True),
        lax.all_gather(norm_gain, "wide", axis=1, tiled=True),
        lax.all_gather(norm_shift, "wide", axis=1, tiled=True),
        lax.all_gather(proj_bias, "wide", axis=1, tiled=True),
    )
    gains = gain_full.astype(jnp.float32)
    shifts = shift_full.astype(jnp.float32)
    biases = bias_full.astype(jnp.float32)
    inputs = tokens.reshape(count, width).astype(jnp.float32)
    scaled_one, inv_one, normed = normalize(inputs, gains[0], shifts[0])
    normed_one = normed.astype(jnp.bfloat16)
    zero_bias = jnp.zeros((width,), jnp.float32)
    qkv_bias = jnp.concatenate([biases[0], zero_bias, biases[1]])
    projected = jnp.dot(normed_one, qkv_full, preferred_element_type=jnp.float32) + qkv_bias
    split_heads = projected.astype(jnp.bfloat16).reshape(rows, length, 3, HEADS, head_size)
    query = split_heads[:, :, 0]
    keys = split_heads[:, :, 1]
    value = split_heads[:, :, 2]
    mixed, logsum = lax.map(
        lambda members: attend(members[0], members[1], members[2]), (query, keys, value)
    )
    mixed_low = mixed.reshape(count, width).astype(jnp.bfloat16)
    hidden = inputs + jnp.dot(mixed_low, out_full, preferred_element_type=jnp.float32) + biases[2]
    in_full, back_full, ffn_bias_full = (
        lax.all_gather(w_in, "wide", axis=0, tiled=True),
        lax.all_gather(w_back, "wide", axis=0, tiled=True),
        lax.all_gather(ffn_bias, "wide", axis=0, tiled=True),
    )
    scaled_two, inv_two, normed = normalize(hidden, gains[1], shifts[1])
    normed_two = normed.astype(jnp.bfloat16)
    pre_act = jnp.dot(
        normed_two, in_full, preferred_element_type=jnp.float32
    ) + ffn_bias_full.astype(jnp.float32)
    active = smooth_gate(pre_act).astype(jnp.bfloat16)
    result = hidden + jnp.dot(active, back_full, preferred_element_type=jnp.float32) + biases[3]
    layer_out = result.astype(jnp.bfloat16).reshape(rows, length, width)
    keep = jnp.where(
        row_kind[:, None] == 1,
        jnp.ones(grad_mask.shape, jnp.float32),
        grad_mask.astype(jnp.float32),
    )
    grad_result = (cotangent.astype(jnp.float32) * keep[:, :, None]).reshape(count, width)
    in_back, back_back = (
        lax.all_gather(w_in, "wide", axis=0, tiled=True),
        lax.all_gather(w_back, "wide", axis=0, tiled=True),
    )
    grad_ffn = grad_result.astype(jnp.bfloat16)
    grad_back = jnp.einsum("nf,nd->fd", active, grad_ffn, preferred_element_type=jnp.float32)
    bias_four = jnp.sum(grad_ffn.astype(jnp.float32), axis=0)
    grad_active = jnp.einsum("nd,fd->nf", grad_ffn, back_back, preferred_element_type=jnp.float32)
    grad_pre = (grad_active * gate_slope(pre_act)).astype(jnp.bfloat16)
    grad_in = jnp.einsum("nd,nf->df", normed_two, grad_pre, preferred_element_type=jnp.float32)
    grad_ffn_bias = jnp.sum(grad_pre.astype(jnp.float32), axis=0)
    grad_two = jnp.einsum("nf,df->nd", grad_pre, in_back, preferred_element_type=jnp.float32)
    gain_two = jnp.sum(grad_two * scaled_two, axis=0)
    shift_two = jnp.sum(grad_two, axis=0)
    grad_hidden = grad_result + norm_back(grad_two, scaled_two, inv_two, gains[1])
    ffn_shares = (
        lax.psum_scatter(
            grad_in.astype(jnp.bfloat16), "wide", scatter_dimension=0, tiled=True
        ).astype(jnp.float32),
        lax.psum_scatter(
            grad_back.astype(jnp.bfloat16), "wide", scatter_dimension=0, tiled=True
        ).astype(jnp.float32),
        lax.psum_scatter(
            grad_ffn_bias.astype(jnp.bfloat16), "wide", scatter_dimension=0, tiled=True
        ).astype(jnp.float32),
    )
    ffn_summed = (
        lax.psum(ffn_shares[0].astype(jnp.bfloat16), "narrow").astype(jnp.float32),
        lax.psum(ffn_shares[1].astype(jnp.bfloat16), "narrow").astype(jnp.float32),
        lax.psum(ffn_shares[2].astype(jnp.bfloat16), "narrow").astype(jnp.float32),
    )
    qkv_back, out_back = (
        lax.all_gather(w_qkv, "wide", axis=0, tiled=True),
        lax.all_gather(w_out, "wide", axis=0, tiled=True),
    )
    grad_attn = grad_hidden.astype(jnp.bfloat16)
    grad_out = jnp.einsum("nc,nd->cd", mixed_low, grad_attn, preferred_element_type=jnp.float32)
    bias_three = jnp.sum(grad_attn.astype(jnp.float32), axis=0)
    grad_mixed = jnp.einsum("nd,cd->nc", grad_attn, out_back, preferred_element_type=jnp.float32)
    grad_mixed = grad_mixed.astype(jnp.bfloat16).reshape(rows, length, HEADS, head_size)
    grad_query, grad_keys, grad_value = lax.map(
        lambda members: attend_back(members[0], members[1], members[2], members[3], members[4]),
        (query, keys, value, grad_mixed, logsum),
    )
    grad_proj = (
        jnp.stack([grad_query, grad_keys, grad_value], axis=2)
        .reshape(count, 3 * width)
        .astype(jnp.bfloat16)
    )
    grad_qkv = jnp.einsum("nd,ne->de", normed_one, grad_proj, preferred_element_type=jnp.float32)
    column_sums = jnp.sum(grad_proj.astype(jnp.float32), axis=0)
    grad_one = jnp.einsum("ne,de->nd", grad_proj, qkv_back, preferred_element_type=jnp.float32)
    gain_one = jnp.sum(grad_one * scaled_one, axis=0)
    shift_one = jnp.sum(grad_one, axis=0)
    input_grad = grad_hidden + norm_back(grad_one, scaled_one, inv_one, gains[0])
    grad_gain = jnp.stack([gain_one, gain_two])
    grad_shift = jnp.stack([shift_one, shift_two])
    grad_bias = jnp.stack([column_sums[:width], column_sums[2 * width :], bias_three, bias_four])
    attn_shares = (
        lax.psum_scatter(
            grad_qkv.astype(jnp.bfloat16), "wide", scatter_dimension=0, tiled=True
        ).astype(jnp.float32),
        lax.psum_scatter(
            grad_out.astype(jnp.bfloat16), "wide", scatter_dimension=0, tiled=True
        ).astype(jnp.float32),
        lax.psum_scatter(
            grad_gain.astype(jnp.bfloat16), "wide", scatter_dimension=1, tiled=True
        ).astype(jnp.float32),
        lax.psum_scatter(
            grad_shift.astype(jnp.bfloat16), "wide", scatter_dimension=1, tiled=True
        ).astype(jnp.float32),
        lax.psum_scatter(
            grad_bias.astype(jnp.bfloat16), "wide", scatter_dimension=1, tiled=True
        ).astype(jnp.float32),
    )
    attn_summed = (
        lax.psum(attn_shares[0].astype(jnp.bfloat16), "narrow").astype(jnp.float32),
        lax.psum(attn_shares[1].astype(jnp.bfloat16), "narrow").astype(jnp.float32),
        lax.psum(attn_shares[2].astype(jnp.bfloat16), "narrow").astype(jnp.float32),
        lax.psum(attn_shares[3].astype(jnp.bfloat16), "narrow").astype(jnp.float32),
        lax.psum(attn_shares[4].astype(jnp.bfloat16), "narrow").astype(jnp.float32),
    )
    return (
        layer_out,
        input_grad.reshape(rows, length, width),
        attn_summed[0],
        attn_summed[1],
        ffn_summed[0],
        ffn_summed[1],
        attn_summed[2],
        attn_summed[3],
        attn_summed[4],
        ffn_summed[2],
    )


def solution(mesh):
    in_specs = (
        P(("wide", "narrow"), None, None),
        P(("wide", "narrow"), None, None),
        P(("wide", "narrow")),
        P(("wide", "narrow"), None),
        P("wide", None),
        P("wide", None),
        P("wide", None),
        P("wide", None),
        P(None, "wide"),
        P(None, "wide"),
        P(None, "wide"),
        P("wide"),
    )
    out_specs = (
        P(("wide", "narrow"), None, None),
        P(("wide", "narrow"), None, None),
        P("wide", None),
        P("wide", None),
        P("wide", None),
        P("wide", None),
        P(None, "wide"),
        P(None, "wide"),
        P(None, "wide"),
        P("wide"),
    )
    return jax.shard_map(body, mesh=mesh, in_specs=in_specs, out_specs=out_specs, check_vma=False)
```

profile of v0, /device:TPU:1, one launch (start us, length us, event | category | flops | bytes accessed | tf_op | source)
XLA Modules:
  0.0 1352.5 jit_solution(1113022227522957068)
XLA Ops:
  11.4 18.0 %all-gather = bf16[8,96,2]{1,2,0:T(2,128)(2,1)S(1)} all-gather(bf16[1,96,2]{1,2,0:T(2,128)(2,1)} %bitcast.323), channel_id=1, replica_groups=mesh['wide'=8,'narrow'=4] {'wide'}, dimensions={0}, use_global_device_ids=true | all-gather | bytes 3456 | tf_op jit(solution)/shard_map/all_gather | solution.py:114
  30.1 12.9 all-gather.1
  43.7 14.8 %all-gather.2 = bf16[8,96,4]{1,2,0:T(4,128)(2,1)S(1)} all-gather(bf16[1,96,4]{1,2,0:T(4,128)(2,1)} %bitcast.322), channel_id=1, replica_groups=mesh['wide'=8,'narrow'=4] {'wide'}, dimensions={0}, use_global_device_ids=true | all-gather | bytes 6912 | tf_op jit(solution)/shard_map/all_gather | solution.py:116
  63.0 22.3 %all-gather.3 = bf16[8,1,384]{2,1,0:T(2,128)(2,1)S(1)} all-gather(bf16[1,1,384]{2,1,0:T(2,128)(2,1)S(1)} %reshape.200), channel_id=1, replica_groups=mesh['wide'=8,'narrow'=4] {'wide'}, dimensions={0}, use_global_device_ids=true | all-gather | bytes 6912 | tf_op jit(solution)/shard_map/all_gather | solution.py:139
  94.3 12.3 add_convert_fusion
  106.6 12.7 copy.57
  119.4 16.3 %reshape.188 = bf16[2,1024,3,12,64]{1,0,4,3,2:T(2,128)(2,1)} reshape(bf16[2048,2304]{0,1:T(8,128)(2,1)} %copy.57) | data formatting | bytes 18874368 | tf_op jit(solution)/shard_map/reshape | solution.py:127
  135.6 8.6 slice_bitcast_fusion.2
  152.6 145.6 %while.26 = (s32[]{:T(128)}, bf16[2,1024,12,64]{1,3,2,0:T(8,128)(2,1)S(1)}, f32[2,12,1024,1]{2,1,3,0:T(8,128)S(1)}, bf16[2,1024,12,64]{1,3,2,0:T(8,128)(2,1)}, b...) while((s32[]{:T(128)}, ...), condition=%wide.region_7.8_spmd, body=%wide.region_2.7_spmd.sunk | while | flops 3337617408 | bytes 164104816 | solution.py:131
  152.8 13.5 multiply_reduce_fusion.13
  166.4 11.0 fusion.160
  177.4 11.6 fusion.161
  188.9 13.4 multiply_reduce_fusion.14
  202.4 11.2 fusion.162
  213.6 11.5 fusion.163
  225.3 14.0 %multiply_reduce_fusion.13 = (f32[12,512]{1,0:T(8,128)S(1)}, f32[12,512,1024]{2,1,0:T(8,128)}) fusion(bf16[2,1024,12,64]{1,3,2,0:T(8,128)(2,1)} %get-tuple-element.385, s32[]{:T(128)S(6)} %copy.91, bf16[2,1024,12,64]{1,3,2,0:T(8,128)(2,1)} %get-tuple-element.384, s32[]{:T(128)S(6)} %add.307), kind=kOutput, calls=%fused_computation.4.clone.1 | convolution fusion | flops 817883136 | bytes 27551232 | tf_op jit(solution)/shard_map/while/body/eval_jaxpr/qhd,khd->hqk/dot_general | solution.py:51
  239.4 11.0 fusion.160
  250.3 11.4 fusion.161
  261.8 13.4 multiply_reduce_fusion.14
  275.2 11.0 fusion.162
  286.2 11.4 fusion.163
  307.8 5.4 fusion.109
  316.9 24.1 %multiply_convert_fusion.2 = (bf16[2048,3072]{1,0:T(8,128)(2,1)}, f32[2048,3072]{1,0:T(8,128)}) fusion(f32[3072]{0:T(1024)S(1)} %bitcast.320, bf16[768,3072]{1,0:T(8,128)(2,1)} %all-gather.13.cloned.1.call-done, f32[2048,768]{1,0:T(8,128)} %copy-done.4, f32[768]{0:T(1024)S(1)} %copy-done.33, f32[768]{0:T(1024)S(1)} %copy-done.26, ...), kind=kOutput, calls=%fused_computation.103 | convolution fusion | flops 9734455296 | bytes 48793600 | tf_op jit(solution)/shard_map/dot_general | solution.py:143
  341.0 32.4 %fusion.110 = (bf16[3072]{0:T(1024)(128)(2,1)}, bf16[2048,3072]{1,0:T(8,128)(2,1)}) fusion(f32[2048,3072]{1,0:T(8,128)} %get-tuple-element.235, f32[3072]{0:T(1024)S(1)} %bitcast.321, bf16[2048,768]{1,0:T(8,128)(2,1)} %bitcast_convert_fusion, bf16[3072,768]{1,0:T(8,128)(2,1)} %all-gather.15.cloned.1.call-done), kind=kOutput, calls=%fused_computation.185 | convolution fusion | flops 9795793920 | bytes 45631488 | tf_op jit(solution)/shard_map/nd,fd->nf/dot_general | solution.py:162
  373.4 17.5 %multiply_reduce_fusion.4 = (bf16[768]{0:T(1024)(128)(2,1)}, f32[2048]{0:T(1024)S(1)}, f32[2048]{0:T(1024)S(1)}, bf16[768]{0:T(1024)(128)(2,1)}, f32[2048,768]{1,0:T(8,128)}) fusion(f32[2048,768]{1,0:T(8,128)} %copy-done.4, f32[2048]{0:T(1024)S(1)} %add_rsqrt_fusion, f32[2048]{0:T(1024)S(1)} %broadcast_multiply_fusion.4, f32[768]{0:T(1024)S(1)} %copy-done.26, ...), kind=kOutput, calls=%fused_computation.131 | convolution fusion | flops 9677826048 | bytes 29923328 | tf_op jit(solution)/shard_map/nf,df->nd/dot_general | solution.py:166
  391.0 6.9 convert_reduce_fusion.2
  404.3 7.1 convolution_convert_fusion.3
  429.2 340.7 %while.27 = (s32[]{:T(128)}, bf16[2,1024,12,64]{1,3,2,0:T(8,128)(2,1)}, bf16[2,1024,12,64]{1,3,2,0:T(8,128)(2,1)}, bf16[2,1024,12,64]{1,3,2,0:T(8,128)(2,1)}, bf...) while((s32[]{:T(128)}, ...), condition=%wide.region_15.16_spmd, body=%wide.region_12.15_spmd.sunk | while | flops 8211124224 | bytes 505339744 | solution.py:195
  448.1 13.5 fusion.177
  461.6 13.6 %fusion.176 = f32[12,512,1024]{2,1,0:T(8,128)} fusion(bf16[2,1024,12,64]{1,3,2,0:T(8,128)(2,1)} %get-tuple-element.417, s32[]{:T(128)S(6)} %copy.101, bf16[2,1024,12,64]{1,3,2,0:T(8,128)(2,1)} %get-tuple-element.418, s32[]{:T(128)S(6)} %add.311), kind=kOutput, calls=%fused_computation.60.clone.1 | convolution fusion | flops 805306368 | bytes 27526656 | tf_op jit(solution)/shard_map/while/body/eval_jaxpr/qhd,khd->hqk/dot_general | solution.py:71
  475.2 10.8 fusion.180
  486.0 12.3 bitcast_dynamic-update-slice_fusion.5
  498.3 16.8 %multiply_reduce_fusion.15 = (f32[12,512]{1,0:T(8,128)S(1)}, f32[12,512,1024]{2,1,0:T(8,128)}) fusion(f32[12,512,1024]{2,1,0:T(8,128)} %fusion.176, f32[12,512]{1,0:T(8,128)S(1)} %get-tuple-element.354, bf16[2,1024,12,64]{1,3,2,0:T(8,128)(2,1)} %get-tuple-element.421, s32[]{:T(128)S(6)} %copy.101, bf16[2,1024,12,64]{1,3,2,0:T(8,128)(2,1)} %get-tuple-element.420, ...), kind=kOutput, calls=%fused_computation.37.clone.1 | convolution fusion | flops 830466048 | bytes 52741632 | tf_op jit(solution)/shard_map/while/body/eval_jaxpr/qhd,khd->hqk/dot_general | solution.py:74
  515.1 16.8 %multiply_reduce_fusion.16 = (f32[12,512]{1,0:T(8,128)S(1)}, f32[12,512,1024]{2,1,0:T(8,128)}) fusion(f32[12,512,1024]{2,1,0:T(8,128)} %fusion.177, f32[12,512]{1,0:T(8,128)S(1)} %get-tuple-element.357, bf16[2,1024,12,64]{1,3,2,0:T(8,128)(2,1)} %get-tuple-element.421, s32[]{:T(128)S(6)} %copy.101, bf16[2,1024,12,64]{1,3,2,0:T(8,128)(2,1)} %get-tuple-element.420), kind=kOutput, calls=%fused_computation.40.clone.1 | convolution fusion | flops 830466048 | bytes 52741120 | tf_op jit(solution)/shard_map/while/body/eval_jaxpr/qhd,khd->hqk/dot_general | solution.py:74
  531.9 41.4 %multiply_convert_fusion.4 = (bf16[12,512,1024]{2,1,0:T(8,128)(2,1)}, bf16[12,512,1024]{2,1,0:T(8,128)(2,1)}) fusion(f32[12,512,1024]{2,1,0:T(8,128)} %get-tuple-element.355, f32[12,512,1024]{2,1,0:T(8,128)} %fusion.176, f32[12,512]{1,0:T(8,128)S(1)} %get-tuple-element.356, f32[12,512]{1,0:T(8,128)S(1)} %get-tuple-element.354, ...), kind=kLoop, calls=%fused_computation.36.clone.1 | loop fusion | flops 62914560 | bytes 125927424 | tf_op jit(solution)/shard_map/while/body/eval_jaxpr/convert_element_type | solution.py:78
  573.3 9.0 multiply_bitcast_fusion.4
  582.3 9.1 multiply_bitcast_fusion.5
  591.5 7.3 fusion.179
  605.8 13.4 fusion.177
  619.2 13.4 fusion.176
  632.6 10.7 fusion.180
  643.4 12.3 bitcast_dynamic-update-slice_fusion.5
  655.7 16.8 %multiply_reduce_fusion.15 = (f32[12,512]{1,0:T(8,128)S(1)}, f32[12,512,1024]{2,1,0:T(8,128)}) fusion(f32[12,512,1024]{2,1,0:T(8,128)} %fusion.176, f32[12,512]{1,0:T(8,128)S(1)} %get-tuple-element.354, bf16[2,1024,12,64]{1,3,2,0:T(8,128)(2,1)} %get-tuple-element.421, s32[]{:T(128)S(6)} %copy.101, bf16[2,1024,12,64]{1,3,2,0:T(8,128)(2,1)} %get-tuple-element.420, ...), kind=kOutput, calls=%fused_computation.37.clone.1 | convolution fusion | flops 830466048 | bytes 52741632 | tf_op jit(solution)/shard_map/while/body/eval_jaxpr/qhd,khd->hqk/dot_general | solution.py:74
  672.5 16.8 %multiply_reduce_fusion.16 = (f32[12,512]{1,0:T(8,128)S(1)}, f32[12,512,1024]{2,1,0:T(8,128)}) fusion(f32[12,512,1024]{2,1,0:T(8,128)} %fusion.177, f32[12,512]{1,0:T(8,128)S(1)} %get-tuple-element.357, bf16[2,1024,12,64]{1,3,2,0:T(8,128)(2,1)} %get-tuple-element.421, s32[]{:T(128)S(6)} %copy.101, bf16[2,1024,12,64]{1,3,2,0:T(8,128)(2,1)} %get-tuple-element.420), kind=kOutput, calls=%fused_computation.40.clone.1 | convolution fusion | flops 830466048 | bytes 52741120 | tf_op jit(solution)/shard_map/while/body/eval_jaxpr/qhd,khd->hqk/dot_general | solution.py:74
  689.3 41.4 %multiply_convert_fusion.4 = (bf16[12,512,1024]{2,1,0:T(8,128)(2,1)}, bf16[12,512,1024]{2,1,0:T(8,128)(2,1)}) fusion(f32[12,512,1024]{2,1,0:T(8,128)} %get-tuple-element.355, f32[12,512,1024]{2,1,0:T(8,128)} %fusion.176, f32[12,512]{1,0:T(8,128)S(1)} %get-tuple-element.356, f32[12,512]{1,0:T(8,128)S(1)} %get-tuple-element.354, ...), kind=kLoop, calls=%fused_computation.36.clone.1 | loop fusion | flops 62914560 | bytes 125927424 | tf_op jit(solution)/shard_map/while/body/eval_jaxpr/convert_element_type | solution.py:78
  730.6 9.0 multiply_bitcast_fusion.4
  739.7 9.1 multiply_bitcast_fusion.5
  748.8 7.3 fusion.179
  774.9 8.7 copy.67
  783.6 11.5 copy.77
  795.1 12.8 convolution_convert_fusion.2
  808.0 15.6 %convolution_convert_fusion = bf16[3072,768]{1,0:T(8,128)(2,1)} fusion(bf16[2048,3072]{1,0:T(8,128)(2,1)} %get-tuple-element.234, bf16[2048,768]{1,0:T(8,128)(2,1)} %bitcast_convert_fusion), kind=kOutput, calls=%fused_computation.140 | convolution fusion | flops 9666035712 | bytes 20447232 | tf_op jit(solution)/shard_map/nf,nd->fd/dot_general | solution.py:160
  823.8 18.1 %convolution_convert_fusion.1 = bf16[768,3072]{1,0:T(8,128)(2,1)} fusion(bf16[2048,3072]{1,0:T(8,128)(2,1)} %get-tuple-element.239, f32[2048,768]{1,0:T(8,128)} %copy-done.4, f32[768]{0:T(1024)S(1)} %copy-done.34, f32[768]{0:T(1024)S(1)} %copy-done.27, f32[2048]{0:T(1024)S(1)} %copy-done.25, f32[2048]{0:T(1024)S(1)} %copy-done.15), kind=kOutput, calls=%fused_computation.141 | convolution fusion | flops 9673900032 | bytes 23615488 | tf_op jit(solution)/shard_map/nd,nf->df/dot_general | solution.py:164
  846.2 14.7 %fusion.100 = (bf16[768]{0:T(1024)(128)(2,1)S(1)}, f32[2048]{0:T(1024)S(1)}, f32[2048]{0:T(1024)S(1)}, bf16[768]{0:T(1024)(128)(2,1)S(1)}, f32[2048,768]{1,0:T(8,128)}) fusion(bf16[2,1024,768]{2,1,0:T(8,128)(2,1)S(1)} %copy-done.2, f32[2048]{0:T(1024)S(1)} %copy-done.17, f32[2048]{0:T(1024)S(1)} %copy-done.19, f32[768]{0:T(1024)S(1)} %copy-done.23, ...), kind=kOutput, calls=%fused_computation.129 | convolution fusion | flops 7263479808 | bytes 22452224 | tf_op jit(solution)/shard_map/ne,de->nd/dot_general | solution.py:206
  864.0 16.5 %add_convert_fusion.1 = bf16[2048,768]{1,0:T(8,128)(2,1)} fusion(f32[2048,768]{1,0:T(8,128)} %copy-done.4, bf16[2048,3072]{1,0:T(8,128)(2,1)} %get-tuple-element.234, bf16[3072,768]{1,0:T(8,128)(2,1)} %all-gather.15.cloned.1.call-done, f32[768]{0:T(1024)S(1)} %copy-done.32), kind=kOutput, calls=%fused_computation.134 | convolution fusion | flops 9668395008 | bytes 26741760 | tf_op jit(solution)/shard_map/dot_general | solution.py:147
  880.5 14.8 %all-reduce = bf16[3072]{0:T(1024)(128)(2,1)S(1)} all-reduce(bf16[3072]{0:T(1024)(128)(2,1)S(1)} %copy-done.31), channel_id=9, replica_groups=mesh['wide'=8,'narrow'=4] {'wide'}, use_global_device_ids=true, to_apply=%region_40.41.clone | all-reduce | flops 3072 | bytes 12288
  898.7 99.3 %reduce-scatter.20.cloned.1.call-done = bf16[384,768]{1,0:T(8,128)(2,1)} async-done(((bf16[3072,768]{1,0:T(8,128)(2,1)}), bf16[384,768]{1,0:T(8,128)(2,1)}) %reduce-scatter.20.cloned.1.call-update) | async-done | bytes 589840 | tf_op jit(solution)/shard_map/reduce_scatter | solution.py:174
  998.0 98.9 %reduce-scatter.18.cloned.1.call-done = bf16[96,3072]{1,0:T(8,128)(2,1)} async-done(((bf16[768,3072]{1,0:T(8,128)(2,1)}), bf16[96,3072]{1,0:T(8,128)(2,1)}) %reduce-scatter.18.cloned.1.call-update) | async-done | bytes 589840 | tf_op jit(solution)/shard_map/reduce_scatter | solution.py:171
  1096.9 7.3 fusion.99
  1104.2 55.5 %reduce-scatter.24.cloned.1.call-done = bf16[96,2]{1,0:T(8,128)(2,1)} async-done(((bf16[768,2]{1,0:T(8,128)(2,1)}), bf16[96,2]{1,0:T(8,128)(2,1)}) %reduce-scatter.24.cloned.1.call-update) | async-done | bytes 400
  1160.5 63.0 %reduce-scatter.22.cloned.1.call-done = bf16[96,2]{1,0:T(8,128)(2,1)} async-done(((bf16[768,2]{1,0:T(8,128)(2,1)}), bf16[96,2]{1,0:T(8,128)(2,1)}) %reduce-scatter.22.cloned.1.call-update) | async-done | bytes 400
  1224.3 63.2 %reduce-scatter.26.cloned.1.call-done = bf16[96,4]{1,0:T(8,128)(2,1)} async-done(((bf16[768,4]{1,0:T(8,128)(2,1)}), bf16[96,4]{1,0:T(8,128)(2,1)}) %reduce-scatter.26.cloned.1.call-update) | async-done | bytes 784
  1288.3 7.6 all-reduce.1
  1298.2 39.3 %all-reduce.5.cloned.1.call-done = (bf16[96,2304]{1,0:T(8,128)(2,1)}, bf16[96,768]{1,0:T(8,128)(2,1)}, bf16[96,3072]{1,0:T(8,128)(2,1)}, bf16[384,768]{1,0:T(8,128)(2,1)}) async-done(((bf16[96,2304]{1,0:T(8,128)(2,1)}, bf16[96,768]{1,0:T(8,128)(2,1)}, bf16[96,3072]{1,0:T(8,128)(2,1)}, bf16[384,768]{1,0:T(8,128)(2,1)}), (bf16[96,2304]{1,0:T(8,128)(2,1)}, bf16[96,768]{1,0:T(8,128)(2,1)}, ...) | async-done | bytes 1769488 | tf_op jit(solution)/shard_map/psum | solution.py:231
  (228 shorter events, 106.9 us)
Async XLA Ops:
  7.2 54.8 %copy-start = (bf16[2,1024,768]{2,1,0:T(8,128)(2,1)S(1)}, bf16[2,1024,768]{2,1,0:T(8,128)(2,1)}, u32[]{:S(2)}) copy-start(bf16[2,1024,768]{2,1,0:T(8,128)(2,1)} %param.16) | copy-start | bytes 9437188
  7.2 78.8 %copy-start.30 = (s32[2,1024]{1,0:T(2,128)S(1)}, s32[2,1024]{1,0:T(2,128)}, u32[]{:S(2)}) copy-start(s32[2,1024]{1,0:T(2,128)} %param.19) | copy-start | bytes 24580
  7.2 87.1 %all-gather.9.cloned.1.call-start = ((), (), s32[]{:S(2)}) async-start(), calls=%async_computation.7 | async-start | bytes 3981312 | tf_op jit(solution)/shard_map/all_gather | solution.py:112
  7.9 299.9 %all-gather.11.cloned.1.call-start = ((), (), s32[]{:S(2)}) async-start(), calls=%async_computation.8 | async-start | bytes 1327104 | tf_op jit(solution)/shard_map/all_gather | solution.py:113
  8.7 308.2 %all-gather.13.cloned.1.call-start = ((), (), s32[]{:S(2)}) async-start(), calls=%async_computation.9 | async-start | bytes 5308416 | tf_op jit(solution)/shard_map/all_gather | solution.py:137
  9.4 331.6 %all-gather.15.cloned.1.call-start = ((), (), s32[]{:S(2)}) async-start(), calls=%async_computation.10 | async-start | bytes 5308416 | tf_op jit(solution)/shard_map/all_gather | solution.py:138
  10.0 885.4 %reduce-scatter.16.cloned.1.call-start = ((), (), s32[]{:S(2)}) async-start(), calls=%async_computation.12 | async-start | bytes 1327104 | tf_op jit(solution)/shard_map/reduce_scatter | solution.py:217
  30.1 61.8 %copy-start.22 = (f32[768]{0:T(1024)}, f32[768]{0:T(1024)S(1)}, u32[]{:S(2)}) copy-start(f32[768]{0:T(1024)S(1)} %get-tuple-element.164) | copy-start | bytes 9220
  58.6 28.0 %copy-start.11 = (bf16[2,1024,768]{2,1,0:T(8,128)(2,1)S(1)}, bf16[2,1024,768]{2,1,0:T(8,128)(2,1)}, u32[]{:S(2)}) copy-start(bf16[2,1024,768]{2,1,0:T(8,128)(2,1)} %param.17) | copy-start | bytes 9437188
  87.2 4.7 copy-start.3
  89.4 4.9 copy-start.16
  89.4 4.9 copy-start.18
  298.2 1.7 copy-start.10
  299.9 8.0 copy-start.1
  299.9 8.0 copy-start.35
  313.3 2.7 copy-start.4
  313.3 3.6 copy-start.26
  313.3 3.6 copy-start.28
  313.3 3.6 copy-start.33
  313.3 77.6 %copy-start.14 = (f32[2048]{0:T(1024)}, f32[2048]{0:T(1024)S(1)}, u32[]{:S(2)}) copy-start(f32[2048]{0:T(1024)S(1)} %broadcast_multiply_fusion.4) | copy-start | bytes 24580
  316.8 74.1 %copy-start.24 = (f32[2048]{0:T(1024)}, f32[2048]{0:T(1024)S(1)}, u32[]{:S(2)}) copy-start(f32[2048]{0:T(1024)S(1)} %add_rsqrt_fusion) | copy-start | bytes 24580
  316.9 74.0 %slice-start.3 = ((s8[6291456]{0:T(1024)(128)(4,1)}), s8[2097152]{0:T(1024)(128)(4,1)S(1)}, s32[]{:S(2)}) async-start(s8[6291456]{0:T(1024)(128)(4,1)} %bitcast.299), calls=%async_computation.22 | async-start | bytes 4194304
  341.0 32.4 %copy-start.38 = (bf16[768,3072]{1,0:T(8,128)(2,1)S(1)}, bf16[768,3072]{1,0:T(8,128)(2,1)}, u32[]{:S(2)}) copy-start(bf16[768,3072]{1,0:T(8,128)(2,1)} %all-gather.13.cloned.1.call-done) | copy-start | bytes 14155780
  341.0 49.9 %slice-start.4 = ((s8[6291456]{0:T(1024)(128)(4,1)}), s8[4194304]{0:T(1024)(128)(4,1)S(1)}, s32[]{:S(2)}) async-start(s8[6291456]{0:T(1024)(128)(4,1)} %bitcast.299), calls=%async_computation.23 | async-start | bytes 8388608
  391.0 9.6 copy-start.13
  397.9 2.7 copy-start.5
  400.6 3.7 copy-start.39
  404.2 494.5 %reduce-scatter.14.cloned.1.call-start = ((), (), s32[]{:S(2)}) async-start(), calls=%async_computation.11 | async-start | bytes 3981312 | tf_op jit(solution)/shard_map/reduce_scatter | solution.py:214
  582.3 16.4 %slice-start = ((s8[12582912]{0:T(1024)(128)(4,1)}), s8[4194304]{0:T(1024)(128)(4,1)S(1)}, s32[]{:S(2)}) async-start(s8[12582912]{0:T(1024)(128)(4,1)} %bitcast.297), calls=%async_computation.19 | async-start | bytes 8388608 | tf_op jit(solution)/shard_map/while
  582.3 16.4 %slice-start.1 = ((s8[12582912]{0:T(1024)(128)(4,1)}), s8[4194304]{0:T(1024)(128)(4,1)S(1)}, s32[]{:S(2)}) async-start(s8[12582912]{0:T(1024)(128)(4,1)} %bitcast.297), calls=%async_computation.20 | async-start | bytes 8388608 | tf_op jit(solution)/shard_map/while
  591.4 7.3 slice-start.2
  591.4 7.3 copy-start.6
  598.8 3.8 copy-start.8
  602.5 1.6 copy-start.7
  604.2 1.6 copy-start.9
  739.6 16.4 %slice-start = ((s8[12582912]{0:T(1024)(128)(4,1)}), s8[4194304]{0:T(1024)(128)(4,1)S(1)}, s32[]{:S(2)}) async-start(s8[12582912]{0:T(1024)(128)(4,1)} %bitcast.297), calls=%async_computation.19 | async-start | bytes 8388608 | tf_op jit(solution)/shard_map/while
  739.6 16.4 %slice-start.1 = ((s8[12582912]{0:T(1024)(128)(4,1)}), s8[4194304]{0:T(1024)(128)(4,1)S(1)}, s32[]{:S(2)}) async-start(s8[12582912]{0:T(1024)(128)(4,1)} %bitcast.297), calls=%async_computation.20 | async-start | bytes 8388608 | tf_op jit(solution)/shard_map/while
  748.8 7.3 slice-start.2
  748.8 7.3 copy-start.6
  756.1 3.8 copy-start.8
  759.9 1.6 copy-start.7
  761.5 1.6 copy-start.9
  783.6 11.5 copy-start.12
  808.0 190.0 %reduce-scatter.20.cloned.1.call-start = ((), (), s32[]{:S(2)}) async-start(), calls=%async_computation.14 | async-start | bytes 5308416 | tf_op jit(solution)/shard_map/reduce_scatter | solution.py:174
  808.0 15.7 %copy-start.15 = (f32[2048]{0:T(1024)S(1)}, f32[2048]{0:T(1024)}, u32[]{:S(2)}) copy-start(f32[2048]{0:T(1024)} %copy-done.14) | copy-start | bytes 24580
  808.0 15.7 %copy-start.25 = (f32[2048]{0:T(1024)S(1)}, f32[2048]{0:T(1024)}, u32[]{:S(2)}) copy-start(f32[2048]{0:T(1024)} %copy-done.24) | copy-start | bytes 24580
  808.0 15.7 %copy-start.27 = (f32[768]{0:T(1024)S(1)}, f32[768]{0:T(1024)}, u32[]{:S(2)}) copy-start(f32[768]{0:T(1024)} %get-tuple-element.163) | copy-start | bytes 9220
  808.0 15.7 %copy-start.34 = (f32[768]{0:T(1024)S(1)}, f32[768]{0:T(1024)}, u32[]{:S(2)}) copy-start(f32[768]{0:T(1024)} %get-tuple-element.165) | copy-start | bytes 9220
  823.7 18.4 %copy-start.21 = (f32[2,1024]{1,0:T(2,128)S(1)}, f32[2,1024]{1,0:T(2,128)}, u32[]{:S(2)}) copy-start(f32[2,1024]{1,0:T(2,128)} %copy-done.20) | copy-start | bytes 24580
  823.7 273.2 %reduce-scatter.18.cloned.1.call-start = ((), (), s32[]{:S(2)}) async-start(), calls=%async_computation.13 | async-start | bytes 5308416 | tf_op jit(solution)/shard_map/reduce_scatter | solution.py:171
  841.9 3.0 copy-start.40
  841.9 4.2 copy-start.37
  841.9 4.2 copy-start.36
  841.9 4.3 copy-start.2
  841.9 4.3 copy-start.17
  841.9 4.3 copy-start.19
  842.0 4.3 copy-start.23
  842.0 317.7 %reduce-scatter.24.cloned.1.call-start = ((), (), s32[]{:S(2)}) async-start(), calls=%async_computation.16 | async-start | bytes 221184
  846.2 15.7 %copy-start.29 = (bf16[768]{0:T(1024)(128)(2,1)S(1)}, bf16[768]{0:T(1024)(128)(2,1)}, u32[]{:S(2)}) copy-start(bf16[768]{0:T(1024)(128)(2,1)} %get-tuple-element.207) | copy-start | bytes 4612
  846.2 17.8 %copy-start.32 = (f32[768]{0:T(1024)S(1)}, f32[768]{0:T(1024)}, u32[]{:S(2)}) copy-start(f32[768]{0:T(1024)} %get-tuple-element.159) | copy-start | bytes 9220
  861.9 361.6 %reduce-scatter.22.cloned.1.call-start = ((), (), s32[]{:S(2)}) async-start(), calls=%async_computation.15 | async-start | bytes 221184
  863.0 424.5 %reduce-scatter.26.cloned.1.call-start = ((), (), s32[]{:S(2)}) async-start(), calls=%async_computation.17 | async-start | bytes 221184
  863.9 473.5 %all-reduce.5.cloned.1.call-start = ((), (), s32[]{:S(2)}) async-start(), calls=%async_computation.18 | async-start | bytes 3538944 | tf_op jit(solution)/shard_map/psum | solution.py:231
  864.0 16.5 %copy-start.31 = (bf16[3072]{0:T(1024)(128)(2,1)S(1)}, bf16[3072]{0:T(1024)(128)(2,1)}, u32[]{:S(2)}) copy-start(bf16[3072]{0:T(1024)(128)(2,1)} %get-tuple-element.238) | copy-start | bytes 18436
  (1 other events, 0.6 us)
Sparse Core Ops, SparseCore 0:
  10.2 66.4 all-gather.8
  78.9 39.3 all-gather.10
  120.5 78.9 all-gather.12
  201.4 78.1 all-gather.14
  404.4 74.3 reduce-scatter.15
  808.1 90.5 reduce-scatter.13
  902.3 95.5 reduce-scatter.19
  1001.6 95.1 reduce-scatter.17
  1100.7 58.9 reduce-scatter.23
  1163.4 60.0 reduce-scatter.21
  1227.3 60.0 reduce-scatter.25
  1290.0 47.4 all-reduce.4
where the time goes:
time: 1360 us; the launch traced here: 1350 us
  matrix products  506 us (37%)
  waiting for transfers between devices  425 us (31%)
  other arithmetic  174 us (13%)
  local copies, waits for them, and re-layouts  114 us (8%)
  blocking collectives  90.4 us (7%)
  loops' own time  26.6 us (2%)
  between operations  15.8 us (1%)
    unnamed x15, waiting for transfers between devices  184 us
    reduce_scatter x1, waiting for transfers between devices, body(): lax.psum_scatter(grad_back.astype(jnp.bfloat16), 'wide', scatter_dimensio...  99.3 us
    reduce_scatter x1, waiting for transfers between devices, body(): lax.psum_scatter(grad_in.astype(jnp.bfloat16), 'wide', scatter_dimension=...  98.9 us
    convert_element_type x2, other arithmetic, attend_back(): grad_scores = (probs * (grad_probs - inner)).astype(jnp.bfloat16)  82.8 us
    dot_general x4, matrix products, attend_back(): jnp.einsum('qhd,khd->hqk', grad_part, value, preferred_element_type=jnp.f...  67.2 us
    dot_general x4, matrix products, attend(): jnp.einsum('qhd,khd->hqk', part, keys, preferred_element_type=jnp.float32)  54.4 us
    dot_general x4, matrix products, attend_back(): jnp.einsum('qhd,khd->hqk', part, keys, preferred_element_type=jnp.float32)  53.9 us
    dot_general x4, matrix products, attend_back(): jnp.einsum('hqk,qhd->khd', rounded, grad_part, preferred_element_type=jnp...  46.1 us
  transfers between devices with their start and end apart: 12, of which 7 were waited for; matrix products, arithmetic and copies ran while one was open for 53% of the time, Pallas kernels for 0%

commit v1 on v0

v1 whole, which is shorter than its diff:
```python
import jax, jax.numpy as jnp, functools
from jax import lax
from jax.experimental import pallas as pl
from jax.experimental.pallas import tpu as pltpu
F32=jnp.float32; BF=jnp.bfloat16
NT=(((1,),(1,)),((),())); NN=(((1,),(0,)),((),())); TN=(((0,),(0,)),((),()))
def dot(a,b,d): return lax.dot_general(a,b,d,preferred_element_type=F32)

def pieces(x):
    hi=x.astype(BF); r=x-hi.astype(F32); mid=r.astype(BF); lo=(r-mid.astype(F32)).astype(BF)
    return hi,mid,lo

def spread(x, lane):
    hi,mid,lo=pieces(x)
    at=lane & 63
    z=jnp.zeros_like(x)
    return jnp.where(at==0,hi.astype(F32),jnp.where(at==1,mid.astype(F32),jnp.where(at==2,lo.astype(F32),z))).astype(BF)

def fwd_kernel(bq, q_ref, k_ref, v_ref, o_ref, l_ref):
    length=q_ref.shape[0]
    lane=lax.broadcasted_iota(jnp.int32,(length,128),1)
    left=lane<64
    lq=lax.broadcasted_iota(jnp.int32,(bq,128),1); leftq=lq<64
    v=v_ref[...].astype(F32)
    ones=jnp.ones_like(v)
    va=jnp.where(left,v,ones).astype(BF); vb=jnp.where(left,ones,v).astype(BF)
    k=k_ref[...]
    for i in range(length//bq):
        q=q_ref[pl.ds(i*bq,bq),:].astype(F32)*0.125
        zero=jnp.zeros_like(q)
        qa=jnp.where(leftq,q,zero).astype(BF); qb=jnp.where(leftq,zero,q).astype(BF)
        outs=[]; peaks=[]
        for qq,vv in ((qa,va),(qb,vb)):
            s=dot(qq,k,NT)
            m=jnp.max(s,axis=1,keepdims=True)
            p=jnp.exp(s-m).astype(BF)
            outs.append(dot(p,vv,NN)); peaks.append(m)
        oa,ob=outs
        num=jnp.where(leftq,oa,ob); den=jnp.where(leftq,ob,oa)
        o_ref[pl.ds(i*bq,bq),:]=(num/pltpu.roll(den,64,1)).astype(BF)
        lse=jnp.where(leftq,peaks[1],peaks[0])+jnp.log(den)
        l_ref[pl.ds(i*bq,bq),:]=spread(lse,lq)

def attn_fwd(qkv, rows, bq=256):
    n=qkv.shape[0]; length=n//rows; width=qkv.shape[1]//3; pairs=width//128
    spec=lambda off: pl.BlockSpec((length,128),lambda s,p,off=off:(s,off+p))
    return pl.pallas_call(functools.partial(fwd_kernel,bq),grid=(rows,pairs),
        in_specs=[spec(0),spec(pairs),spec(2*pairs)],out_specs=[spec(0),spec(0)],
        out_shape=[jax.ShapeDtypeStruct((n,width),BF)]*2,
        compiler_params=pltpu.CompilerParams(vmem_limit_bytes=56<<20),
        cost_estimate=pl.CostEstimate(flops=4*n*length*width,bytes_accessed=n*width*10,transcendentals=n*length*width//64),
        name="attention_forward")(qkv,qkv,qkv)

def bwd_kernel(bq, q_ref,k_ref,v_ref,o_ref,l_ref,g_ref, gq_ref,gk_ref,gv_ref, ak,av):
    length=q_ref.shape[0]
    lane=lax.broadcasted_iota(jnp.int32,(length,128),1)
    left=lane<64; at=lane&63
    lq=lax.broadcasted_iota(jnp.int32,(bq,128),1); leftq=lq<64
    k=k_ref[...].astype(F32); v=v_ref[...].astype(F32)
    tail=jnp.where(at<3,-1.0,0.0).astype(F32)
    zero=jnp.zeros_like(k)
    kx=(jnp.where(left,k,tail).astype(BF),jnp.where(left,tail,k).astype(BF))
    km=(jnp.where(left,k,zero).astype(BF),jnp.where(left,zero,k).astype(BF))
    vx=(jnp.where(left,v,tail).astype(BF),jnp.where(left,tail,v).astype(BF))
    for i in range(length//bq):
        at_q=pl.ds(i*bq,bq)
        q=q_ref[at_q,:].astype(F32)*0.125
        l=l_ref[at_q,:].astype(F32)
        g=g_ref[at_q,:].astype(F32)
        zq=jnp.zeros_like(q)
        prod=g*o_ref[at_q,:].astype(F32)
        da=jnp.sum(jnp.where(leftq,prod,zq),axis=1,keepdims=True)
        db=jnp.sum(jnp.where(leftq,zq,prod),axis=1,keepdims=True)
        d=spread(jnp.where(leftq,db,da),lq).astype(F32)
        qx=(jnp.where(leftq,q,l).astype(BF),jnp.where(leftq,l,q).astype(BF))
        qm=(jnp.where(leftq,q,zq).astype(BF),jnp.where(leftq,zq,q).astype(BF))
        gx=(jnp.where(leftq,g,d).astype(BF),jnp.where(leftq,d,g).astype(BF))
        gm=(jnp.where(leftq,g,zq).astype(BF),jnp.where(leftq,zq,g).astype(BF))
        gq=None; gk=None; gv=None
        for h in range(2):
            p=jnp.exp(dot(kx[h],qx[h],NT))
            ds=(p*dot(vx[h],gx[h],NT)).astype(BF)
            tv=dot(p.astype(BF),gm[h],NN); tk=dot(ds,qm[h],NN); tq=dot(ds,km[h],TN)
            gq=tq if gq is None else gq+tq
            gk=tk if gk is None else gk+tk
            gv=tv if gv is None else gv+tv
        gq_ref[at_q,:]=(gq*0.125).astype(BF)
        if i==0: ak[...]=gk; av[...]=gv
        else: ak[...]+=gk; av[...]+=gv
    gk_ref[...]=ak[...].astype(BF); gv_ref[...]=av[...].astype(BF)

def attn_bwd(qkv,mixed,lse,gmixed,rows,bq=256):
    n=qkv.shape[0]; length=n//rows; width=qkv.shape[1]//3; pairs=width//128
    spec=lambda off: pl.BlockSpec((length,128),lambda s,p,off=off:(s,off+p))
    return pl.pallas_call(functools.partial(bwd_kernel,bq),grid=(rows,pairs),
        in_specs=[spec(0),spec(pairs),spec(2*pairs),spec(0),spec(0),spec(0)],out_specs=[spec(0)]*3,
        out_shape=[jax.ShapeDtypeStruct((n,width),BF)]*3,
        scratch_shapes=[pltpu.VMEM((length,128),F32)]*2,
        compiler_params=pltpu.CompilerParams(vmem_limit_bytes=56<<20),
        cost_estimate=pl.CostEstimate(flops=10*n*length*width,bytes_accessed=n*width*18,transcendentals=n*length*width//64),
        name="attention_backward")(qkv,qkv,qkv,mixed,lse,gmixed)

from jax.sharding import PartitionSpec as P

HEADS = 12


EPSILON = 1e-05
ROOT_TWO_PI = 0.7978845608028654
CUBIC = 0.044715


def normalize(values, gain, shift):
    centre = jnp.mean(values, axis=-1, keepdims=True)
    centred = values - centre
    variance = jnp.mean(centred * centred, axis=-1, keepdims=True)
    inv_std = lax.rsqrt(variance + EPSILON)
    scaled = centred * inv_std
    return (scaled, inv_std, scaled * gain + shift)


def smooth_gate(values):
    return (
        0.5 * values * (1.0 + jnp.tanh(ROOT_TWO_PI * (values + CUBIC * values * values * values)))
    )


def gate_slope(values):
    bent = jnp.tanh(ROOT_TWO_PI * (values + CUBIC * values * values * values))
    return 0.5 * (1.0 + bent) + 0.5 * values * (1.0 - bent * bent) * ROOT_TWO_PI * (
        1.0 + 3.0 * CUBIC * values * values
    )


def norm_back(grad_norm, scaled, inv_std, gain):
    grad_scaled = grad_norm * gain
    first_mean = jnp.mean(grad_scaled, axis=-1, keepdims=True)
    second_mean = jnp.mean(grad_scaled * scaled, axis=-1, keepdims=True)
    return inv_std * (grad_scaled - first_mean - scaled * second_mean)


def body(
    tokens,
    cotangent,
    row_kind,
    grad_mask,
    w_qkv,
    w_out,
    w_in,
    w_back,
    norm_gain,
    norm_shift,
    proj_bias,
    ffn_bias,
):
    rows, length, width = tokens.shape
    count = rows * length
    head_size = width // HEADS
    share = width // lax.axis_size("wide")
    packed = jnp.concatenate([norm_gain, norm_shift, proj_bias, ffn_bias.reshape(-1, share)])
    qkv_full = lax.all_gather(w_qkv, "wide", axis=0, tiled=True)
    small = lax.all_gather(packed, "wide", axis=0)
    out_full = lax.all_gather(w_out, "wide", axis=0, tiled=True)
    in_full = lax.all_gather(w_in, "wide", axis=0, tiled=True)
    back_full = lax.all_gather(w_back, "wide", axis=0, tiled=True)
    by_column = small[:, :8].transpose(1, 0, 2).reshape(8, width)
    gain_full, shift_full, bias_full = by_column[:2], by_column[2:4], by_column[4:8]
    ffn_bias_full = small[:, 8:].reshape(-1)
    gains = gain_full.astype(jnp.float32)
    shifts = shift_full.astype(jnp.float32)
    biases = bias_full.astype(jnp.float32)
    inputs = tokens.reshape(count, width).astype(jnp.float32)
    scaled_one, inv_one, normed = normalize(inputs, gains[0], shifts[0])
    normed_one = normed.astype(jnp.bfloat16)
    zero_bias = jnp.zeros((width,), jnp.float32)
    qkv_bias = jnp.concatenate([biases[0], zero_bias, biases[1]])
    projected = jnp.dot(normed_one, qkv_full, preferred_element_type=jnp.float32) + qkv_bias
    qkv = projected.astype(jnp.bfloat16)
    mixed_low, logsum = attn_fwd(qkv, rows, 512)
    hidden = inputs + jnp.dot(mixed_low, out_full, preferred_element_type=jnp.float32) + biases[2]
    scaled_two, inv_two, normed = normalize(hidden, gains[1], shifts[1])
    normed_two = normed.astype(jnp.bfloat16)
    pre_act = jnp.dot(
        normed_two, in_full, preferred_element_type=jnp.float32
    ) + ffn_bias_full.astype(jnp.float32)
    active = smooth_gate(pre_act).astype(jnp.bfloat16)
    result = hidden + jnp.dot(active, back_full, preferred_element_type=jnp.float32) + biases[3]
    layer_out = result.astype(jnp.bfloat16).reshape(rows, length, width)
    keep = jnp.where(
        row_kind[:, None] == 1,
        jnp.ones(grad_mask.shape, jnp.float32),
        grad_mask.astype(jnp.float32),
    )
    grad_result = (cotangent.astype(jnp.float32) * keep[:, :, None]).reshape(count, width)
    grad_ffn = grad_result.astype(jnp.bfloat16)
    grad_back = jnp.einsum("nf,nd->fd", active, grad_ffn, preferred_element_type=jnp.float32)
    bias_four = jnp.sum(grad_ffn.astype(jnp.float32), axis=0)
    grad_active = jnp.einsum("nd,fd->nf", grad_ffn, back_full, preferred_element_type=jnp.float32)
    grad_pre = (grad_active * gate_slope(pre_act)).astype(jnp.bfloat16)
    grad_in = jnp.einsum("nd,nf->df", normed_two, grad_pre, preferred_element_type=jnp.float32)
    grad_ffn_bias = jnp.sum(grad_pre.astype(jnp.float32), axis=0)
    grad_two = jnp.einsum("nf,df->nd", grad_pre, in_full, preferred_element_type=jnp.float32)
    gain_two = jnp.sum(grad_two * scaled_two, axis=0)
    shift_two = jnp.sum(grad_two, axis=0)
    grad_hidden = grad_result + norm_back(grad_two, scaled_two, inv_two, gains[1])
    in_share = lax.psum_scatter(
        grad_in.astype(jnp.bfloat16), "wide", scatter_dimension=0, tiled=True
    )
    back_share = lax.psum_scatter(
        grad_back.astype(jnp.bfloat16), "wide", scatter_dimension=0, tiled=True
    )
    grad_attn = grad_hidden.astype(jnp.bfloat16)
    grad_out = jnp.einsum("nc,nd->cd", mixed_low, grad_attn, preferred_element_type=jnp.float32)
    bias_three = jnp.sum(grad_attn.astype(jnp.float32), axis=0)
    grad_mixed = jnp.einsum("nd,cd->nc", grad_attn, out_full, preferred_element_type=jnp.float32)
    grad_proj = jnp.concatenate(
        attn_bwd(qkv, mixed_low, logsum, grad_mixed.astype(jnp.bfloat16), rows), axis=1
    )
    grad_qkv = jnp.einsum("nd,ne->de", normed_one, grad_proj, preferred_element_type=jnp.float32)
    column_sums = jnp.sum(grad_proj.astype(jnp.float32), axis=0)
    grad_one = jnp.einsum("ne,de->nd", grad_proj, qkv_full, preferred_element_type=jnp.float32)
    gain_one = jnp.sum(grad_one * scaled_one, axis=0)
    shift_one = jnp.sum(grad_one, axis=0)
    input_grad = grad_hidden + norm_back(grad_one, scaled_one, inv_one, gains[0])
    qkv_share = lax.psum_scatter(
        grad_qkv.astype(jnp.bfloat16), "wide", scatter_dimension=0, tiled=True
    )
    out_share = lax.psum_scatter(
        grad_out.astype(jnp.bfloat16), "wide", scatter_dimension=0, tiled=True
    )
    by_column = jnp.stack(
        [
            gain_one,
            gain_two,
            shift_one,
            shift_two,
            column_sums[:width],
            column_sums[2 * width :],
            bias_three,
            bias_four,
        ]
    )
    by_column = by_column.reshape(8, -1, share).transpose(1, 0, 2)
    small = jnp.concatenate([by_column, grad_ffn_bias.reshape(by_column.shape[0], -1, share)], axis=1)
    small = lax.psum(small.astype(jnp.bfloat16), ("wide", "narrow"))
    small = lax.dynamic_index_in_dim(small, lax.axis_index("wide"), 0, keepdims=False)
    small = small.astype(jnp.float32)
    summed = lax.psum((qkv_share, out_share, in_share, back_share), "narrow")
    summed = [part.astype(jnp.float32) for part in summed]
    return (
        layer_out,
        input_grad.reshape(rows, length, width),
        summed[0],
        summed[1],
        summed[2],
        summed[3],
        small[:2],
        small[2:4],
        small[4:8],
        small[8:].reshape(-1),
    )


def solution(mesh):
    in_specs = (
        P(("wide", "narrow"), None, None),
        P(("wide", "narrow"), None, None),
        P(("wide", "narrow")),
        P(("wide", "narrow"), None),
        P("wide", None),
        P("wide", None),
        P("wide", None),
        P("wide", None),
        P(None, "wide"),
        P(None, "wide"),
        P(None, "wide"),
        P("wide"),
    )
    out_specs = (
        P(("wide", "narrow"), None, None),
        P(("wide", "narrow"), None, None),
        P("wide", None),
        P("wide", None),
        P("wide", None),
        P("wide", None),
        P(None, "wide"),
        P(None, "wide"),
        P(None, "wide"),
        P("wide"),
    )
    return jax.shard_map(body, mesh=mesh, in_specs=in_specs, out_specs=out_specs, check_vma=False)
```

time: 1360 us -> 782 us (0.57)
  matrix products: 506 us -> 175 us
  other arithmetic: 174 us -> 48.4 us
  Pallas kernels: 0 us -> 113 us
  local copies, waits for them, and re-layouts: 114 us -> 17.8 us
  waiting for transfers between devices: 425 us -> 343 us
  loops' own time: 26.6 us -> 0 us
  blocking collectives: 90.4 us -> 66.2 us
    dot_general x32 -> x4, matrix products: 397 us -> 69.8 us  [the longest x1 31.9 us: body(): jnp.einsum('nd,fd->nf', grad_ffn, back_full, preferred_element_type=jnp.f...]
    unnamed x15 -> x9, waiting for transfers between devices: 184 us -> 2.66 us
    all_gather x4, waiting for transfers between devices: 0.04 us -> 138 us  [the longest x1 61 us: body(): in_full = lax.all_gather(w_in, 'wide', axis=0, tiled=True)]
    pallas_call x0 -> x2, Pallas kernels: none -> 113 us  [the longest x1 72.7 us: attn_bwd(): pl.pallas_call(functools.partial(bwd_kernel, bq), grid=(rows, pairs), in_...]
    convert_element_type x11 -> x5, other arithmetic: 93 us -> 7.97 us  [the longest x4 7.95 us: body(): summed = [part.astype(jnp.float32) for part in summed]]
    reduce_sum x4 -> x0, other arithmetic: 44.1 us -> none  [attend(): totals = jnp.sum(expo, axis=-1, keepdims=True)]
    all_gather x4 -> x1, blocking collectives: 68 us -> 25.4 us  [body(): small = lax.all_gather(packed, 'wide', axis=0)]
    reduce_scatter x1, waiting for transfers between devices: 99.3 us -> 62.1 us  [body(): lax.psum_scatter(grad_back.astype(jnp.bfloat16), 'wide', scatter_dimensio...]
  transfers between devices with their start and end apart: 12 -> 9, of which waited for: 7 -> 6; matrix products, arithmetic and copies ran while one was open for 53% -> 21% of each run, Pallas kernels for 0% -> 15%
where the time goes in v1:
time: 782 us; the launch traced here: 778 us
  waiting for transfers between devices  343 us (44%)
  matrix products  175 us (22%)
  Pallas kernels  113 us (14%)
  blocking collectives  66.2 us (8%)
  other arithmetic  48.4 us (6%)
  local copies, waits for them, and re-layouts  17.8 us (2%)
  between operations  14.4 us (2%)
    reduce_scatter x1, waiting for transfers between devices, body(): lax.psum_scatter(grad_in.astype(jnp.bfloat16), 'wide', scatter_dimension=...  98.7 us
    pallas_call x1, Pallas kernels, attn_bwd(): pl.pallas_call(functools.partial(bwd_kernel, bq), grid=(rows, pairs), in_...  72.7 us
    reduce_scatter x1, waiting for transfers between devices, body(): lax.psum_scatter(grad_back.astype(jnp.bfloat16), 'wide', scatter_dimensio...  62.1 us
    all_gather x1, waiting for transfers between devices, body(): in_full = lax.all_gather(w_in, 'wide', axis=0, tiled=True)  61 us
    all_gather x1, waiting for transfers between devices, body(): back_full = lax.all_gather(w_back, 'wide', axis=0, tiled=True)  55.9 us
    psum x1, waiting for transfers between devices, body(): summed = lax.psum((qkv_share, out_share, in_share, back_share), 'narrow')  41.6 us
    psum x1, blocking collectives, body(): small = lax.psum(small.astype(jnp.bfloat16), ('wide', 'narrow'))  40.8 us
    pallas_call x1, Pallas kernels, attn_fwd(): pl.pallas_call(functools.partial(fwd_kernel, bq), grid=(rows, pairs), in_...  40.2 us
  transfers between devices with their start and end apart: 9, of which 6 were waited for; matrix products, arithmetic and copies ran while one was open for 21% of the time, Pallas kernels for 15%

profile of v1, /device:TPU:1, one launch (start us, length us, event | category | flops | bytes accessed | tf_op | source)
XLA Modules:
  0.0 778.0 jit_solution(10563872166267028622)
XLA Ops:
  7.2 0.7 all-gather.7.cloned.1.call-update
  8.0 0.7 all-gather.9.cloned.1.call-update
  8.7 0.7 all-gather.11.cloned.1.call-update
  9.5 0.5 all-gather.13.cloned.1.call-update
  10.0 0.8 reshape.180
  10.8 0.7 maximum_bitcast_fusion
  11.5 25.4 %all-gather.1 = bf16[8,12,96]{2,1,0:T(8,128)(2,1)S(1)} all-gather(bf16[1,12,96]{2,1,0:T(8,128)(2,1)S(1)} %maximum_bitcast_fusion), channel_id=2, replica_groups=mesh['wide'=8,'narrow'=4] {'wide'}, dimensions={0}, use_global_device_ids=true | all-gather | bytes 20736 | tf_op jit(solution)/shard_map/all_gather | solution.py:162
  36.9 0.7 broadcast_compare_fusion
  37.6 2.4 convert_reduce_fusion
  40.0 1.1 fusion.8
  41.2 0.6 slice_reduce_fusion
  42.0 5.2 convert_multiply_fusion
  47.2 2.9 fusion.15
  50.6 4.9 bitcast_convert_fusion
  55.5 21.2 %all-gather.7.cloned.1.call-done = bf16[768,2304]{1,0:T(8,128)(2,1)} async-done(((bf16[96,2304]{1,0:T(8,128)(2,1)}), bf16[768,2304]{1,0:T(8,128)(2,1)}) %all-gather.7.cloned.1.call-update) | async-done | bytes 3538960 | tf_op jit(solution)/shard_map/all_gather | solution.py:161
  76.7 12.3 %add_convert_fusion.q_ref.k_ref.v_ref = bf16[2048,2304]{1,0:T(8,128)(2,1)} fusion(bf16[2048,768]{1,0:T(8,128)(2,1)} %fusion.15, bf16[768,2304]{1,0:T(8,128)(2,1)} %all-gather.7.cloned.1.call-done, f32[2304]{0:T(1024)S(1)} %pad_maximum_fusion.1), kind=kOutput, calls=%fused_computation.10 | convolution fusion | flops 7257194496 | bytes 16131072 | tf_op jit(solution)/shard_map/dot_general | solution.py:177
  89.0 40.2 %attention_forward.1 = (bf16[2048,768]{1,0:T(8,128)(2,1)}, bf16[2048,768]{1,0:T(8,128)(2,1)}) custom-call(bf16[2048,2304]{1,0:T(8,128)(2,1)} %add_convert_fusion.q_ref.k_ref.v_ref, bf16[2048,2304]{1,0:T(8,128)(2,1)} %add_convert_fusion.q_ref.k_ref.v_ref, bf16[2048,2304]{1,0:T(8,128)(2,1)} %add_convert_fusion.q_ref.k_ref.v_ref), custom_call_target="tpu_custom_call" | custom-call | flops 6442450944 | bytes 15728640 | tf_op jit(solution)/shard_map/attention_forward/pallas_call | solution.py:47
  129.3 5.5 fusion.28
  134.8 2.7 copy-done.2
  137.5 0.8 multiply_reduce_fusion.2
  138.3 61.0 %all-gather.11.cloned.1.call-done = bf16[768,3072]{1,0:T(8,128)(2,1)} async-done(((bf16[96,3072]{1,0:T(8,128)(2,1)}), bf16[768,3072]{1,0:T(8,128)(2,1)}) %all-gather.11.cloned.1.call-update) | async-done | bytes 4718608 | tf_op jit(solution)/shard_map/all_gather | solution.py:164
  199.3 24.2 %multiply_convert_fusion = (bf16[2048,3072]{1,0:T(8,128)(2,1)}, f32[2048,3072]{1,0:T(8,128)}) fusion(f32[3072]{0:T(1024)S(1)} %reshape.187, bf16[768,3072]{1,0:T(8,128)(2,1)} %all-gather.11.cloned.1.call-done, f32[2048,768]{1,0:T(8,128)} %copy-done.2, f32[768]{0:T(1024)S(1)} %add.132, f32[768]{0:T(1024)S(1)} %mul.162, f32[2048]{0:T(1024)S(1)} %add_rsqrt_fusion, ...), kind=kOutput, calls=%fused_computation.9 | convolution fusion | flops 9734455296 | bytes 48793600 | tf_op jit(solution)/shard_map/dot_general | solution.py:183
  223.5 55.9 %all-gather.13.cloned.1.call-done = bf16[3072,768]{1,0:T(8,128)(2,1)} async-done(((bf16[384,768]{1,0:T(8,128)(2,1)}), bf16[3072,768]{1,0:T(8,128)(2,1)}) %all-gather.13.cloned.1.call-update) | async-done | bytes 4718608 | tf_op jit(solution)/shard_map/all_gather | solution.py:165
  279.4 31.9 %fusion.29 = (bf16[3072]{0:T(1024)(128)(2,1)S(1)}, bf16[2048,3072]{1,0:T(8,128)(2,1)}) fusion(f32[2048,3072]{1,0:T(8,128)} %get-tuple-element.55, f32[3072]{0:T(1024)S(1)} %reshape.187, bf16[2048,768]{1,0:T(8,128)(2,1)} %bitcast_convert_fusion, bf16[3072,768]{1,0:T(8,128)(2,1)} %all-gather.13.cloned.1.call-done), kind=kOutput, calls=%fused_computation.96 | convolution fusion | flops 9795793920 | bytes 45631488 | tf_op jit(solution)/shard_map/nd,fd->nf/dot_general | solution.py:198
  311.3 16.9 %multiply_reduce_fusion = (bf16[768]{0:T(1024)(128)(2,1)S(1)}, f32[2048]{0:T(1024)S(1)}, f32[2048]{0:T(1024)S(1)}, bf16[768]{0:T(1024)(128)(2,1)S(1)}, f32[2048,768]{1,0:T(8,128)}) fusion(f32[2048,768]{1,0:T(8,128)} %copy-done.2, f32[2048]{0:T(1024)S(1)} %add_rsqrt_fusion, f32[2048]{0:T(1024)S(1)} %broadcast_multiply_fusion.4, f32[768]{0:T(1024)S(1)} %mul.162, ...), kind=kOutput, calls=%fused_computation.32 | convolution fusion | flops 9677826048 | bytes 29923328 | tf_op jit(solution)/shard_map/nf,df->nd/dot_general | solution.py:202
  328.2 6.4 convert_reduce_fusion.2
  334.6 2.7 copy-done.3
  337.3 3.8 convolution_convert_fusion.4
  341.1 7.1 convolution_convert_fusion.3.g_ref
  348.2 72.7 %attention_backward.1 = (bf16[2048,768]{1,0:T(8,128)(2,1)}, bf16[2048,768]{1,0:T(8,128)(2,1)}, bf16[2048,768]{1,0:T(8,128)(2,1)}) custom-call(bf16[2048,2304]{1,0:T(8,128)(2,1)} %add_convert_fusion.q_ref.k_ref.v_ref, bf16[2048,2304]{1,0:T(8,128)(2,1)} %add_convert_fusion.q_ref.k_ref.v_ref, bf16[2048,2304]{1,0:T(8,128)(2,1)} %add_convert_fusion.q_ref.k_ref.v_ref, ...), custom_call_target="tpu_custom_call" | custom-call | flops 16106127360 | bytes 28311552 | tf_op jit(solution)/shard_map/attention_backward/pallas_call | solution.py:95
  421.0 2.2 constant_dynamic-update-slice_fusion.2
  423.2 0.6 copy-done.7
  423.8 0.2 constant_dynamic-update-slice_fusion.1
  424.0 0.7 copy-done.6
  424.7 0.2 constant_dynamic-update-slice_fusion
  425.0 3.6 copy-done.4
  428.6 9.7 %convolution_convert_fusion.2 = bf16[768,2304]{1,0:T(8,128)(2,1)} fusion(bf16[2048,768]{1,0:T(8,128)(2,1)S(1)} %copy-done.5, bf16[2048,2304]{1,0:T(8,128)(2,1)S(1)} %constant_dynamic-update-slice_fusion), kind=kOutput, calls=%fused_computation.43 | convolution fusion | flops 7249526784 | bytes 16121856 | tf_op jit(solution)/shard_map/nd,ne->de/dot_general | solution.py:219
  438.4 14.7 %convolution_convert_fusion = bf16[3072,768]{1,0:T(8,128)(2,1)} fusion(bf16[2048,3072]{1,0:T(8,128)(2,1)} %get-tuple-element.54, bf16[2048,768]{1,0:T(8,128)(2,1)S(1)} %copy-done.8), kind=kOutput, calls=%fused_computation.41 | convolution fusion | flops 9666035712 | bytes 20447232 | tf_op jit(solution)/shard_map/nf,nd->fd/dot_general | solution.py:196
  453.2 18.1 %convolution_convert_fusion.1 = bf16[768,3072]{1,0:T(8,128)(2,1)} fusion(bf16[2048,3072]{1,0:T(8,128)(2,1)} %get-tuple-element.59, f32[2048,768]{1,0:T(8,128)} %copy-done.2, f32[768]{0:T(1024)S(1)} %add.132, f32[768]{0:T(1024)S(1)} %mul.162, f32[2048]{0:T(1024)S(1)} %add_rsqrt_fusion, f32[2048]{0:T(1024)S(1)} %broadcast_multiply_fusion.4), kind=kOutput, calls=%fused_computation.42 | convolution fusion | flops 9673900032 | bytes 23615488 | tf_op jit(solution)/shard_map/nd,nf->df/dot_general | solution.py:200
  471.3 0.3 all-reduce.3.cloned.1.call-start
  471.6 2.8 convert_reduce_fusion.1
  474.4 0.1 stack.34
  474.5 0.1 reshape.184
  474.6 0.1 stack.28
  474.7 0.1 stack.30
  474.8 0.1 stack.33
  474.9 5.2 reduce.3
  480.1 0.1 stack.32
  480.2 0.1 stack.31
  480.3 14.0 %fusion.20 = (bf16[768]{0:T(1024)(128)(2,1)S(1)}, f32[2048]{0:T(1024)S(1)}, f32[2048]{0:T(1024)S(1)}, bf16[768]{0:T(1024)(128)(2,1)S(1)}, f32[2048,768]{1,0:T(8,128)}) fusion(bf16[2,1024,768]{2,1,0:T(8,128)(2,1)S(1)} %copy-done.1, f32[2048]{0:T(1024)S(1)} %copy-done.10, f32[2048]{0:T(1024)S(1)} %copy-done.12, f32[768]{0:T(1024)S(1)} %copy-done.16, ...), kind=kOutput, calls=%fused_computation.30 | convolution fusion | flops 7263479808 | bytes 22452224 | tf_op jit(solution)/shard_map/ne,de->nd/dot_general | solution.py:221
  494.3 0.1 stack.27
  494.5 40.8 %psum.39 = bf16[8,12,96]{2,0,1:T(8,128)(2,1)S(1)} all-reduce(bf16[8,12,96]{2,0,1:T(8,128)(2,1)S(1)} %pad_maximum_fusion), channel_id=1, replica_groups=mesh['wide'=8,'narrow'=4] {'wide','narrow'}, use_global_device_ids=true, to_apply=%region_24.25 | all-reduce | flops 9216 | bytes 36864 | tf_op jit(solution)/shard_map/psum | solution.py:245
  535.3 0.6 slice_reduce_fusion.8
  535.9 0.7 reshape.185
  536.6 0.6 fusion.26
  537.2 16.4 %add_convert_fusion.1 = bf16[2048,768]{1,0:T(8,128)(2,1)} fusion(f32[2048,768]{1,0:T(8,128)} %copy-done.2, bf16[2048,3072]{1,0:T(8,128)(2,1)} %get-tuple-element.54, bf16[3072,768]{1,0:T(8,128)(2,1)} %all-gather.13.cloned.1.call-done, f32[768]{0:T(1024)S(1)} %add.140), kind=kOutput, calls=%fused_computation.35 | convolution fusion | flops 9668395008 | bytes 26741760 | tf_op jit(solution)/shard_map/dot_general | solution.py:187
  553.6 62.1 %reduce-scatter.11.cloned.1.call-done = bf16[384,768]{1,0:T(8,128)(2,1)} async-done(((bf16[3072,768]{1,0:T(8,128)(2,1)}), bf16[384,768]{1,0:T(8,128)(2,1)}) %reduce-scatter.11.cloned.1.call-update) | async-done | bytes 589840 | tf_op jit(solution)/shard_map/reduce_scatter | solution.py:209
  615.7 98.7 %reduce-scatter.9.cloned.1.call-done = bf16[96,3072]{1,0:T(8,128)(2,1)} async-done(((bf16[768,3072]{1,0:T(8,128)(2,1)}), bf16[96,3072]{1,0:T(8,128)(2,1)}) %reduce-scatter.9.cloned.1.call-update) | async-done | bytes 589840 | tf_op jit(solution)/shard_map/reduce_scatter | solution.py:206
  714.4 7.3 fusion.19
  721.7 41.6 %all-reduce.3.cloned.1.call-done = (bf16[96,2304]{1,0:T(8,128)(2,1)}, bf16[96,768]{1,0:T(8,128)(2,1)}, bf16[96,3072]{1,0:T(8,128)(2,1)}, bf16[384,768]{1,0:T(8,128)(2,1)}) async-done(((bf16[96,2304]{1,0:T(8,128)(2,1)}, bf16[96,768]{1,0:T(8,128)(2,1)}, bf16[96,3072]{1,0:T(8,128)(2,1)}, bf16[384,768]{1,0:T(8,128)(2,1)}), (bf16[96,2304]{1,0:T(8,128)(2,1)}, bf16[96,768]{1,0:T(8,128)(2,1)}, ...) | async-done | bytes 1769488 | tf_op jit(solution)/shard_map/psum | solution.py:248
  763.3 1.6 convert_element_type.132
  764.9 2.0 convert_element_type.130
  766.9 2.2 convert_element_type.134
  769.1 2.2 convert_element_type.136
  (99 shorter events, 1.5 us)
Async XLA Ops:
  7.2 32.8 %copy-start = (bf16[2,1024,768]{2,1,0:T(8,128)(2,1)S(1)}, bf16[2,1024,768]{2,1,0:T(8,128)(2,1)}, u32[]{:S(2)}) copy-start(bf16[2,1024,768]{2,1,0:T(8,128)(2,1)} %param.12) | copy-start | bytes 9437188
  7.2 34.7 %copy-start.18 = (s32[2,1024]{1,0:T(2,128)S(1)}, s32[2,1024]{1,0:T(2,128)}, u32[]{:S(2)}) copy-start(s32[2,1024]{1,0:T(2,128)} %param.15) | copy-start | bytes 24580
  7.2 69.5 %all-gather.7.cloned.1.call-start = ((), (), s32[]{:S(2)}) async-start(), calls=%async_computation.4 | async-start | bytes 3981312 | tf_op jit(solution)/shard_map/all_gather | solution.py:161
  7.9 121.3 %all-gather.9.cloned.1.call-start = ((), (), s32[]{:S(2)}) async-start(), calls=%async_computation.5 | async-start | bytes 1327104 | tf_op jit(solution)/shard_map/all_gather | solution.py:163
  8.7 190.6 %all-gather.11.cloned.1.call-start = ((), (), s32[]{:S(2)}) async-start(), calls=%async_computation.6 | async-start | bytes 5308416 | tf_op jit(solution)/shard_map/all_gather | solution.py:164
  9.4 270.0 %all-gather.13.cloned.1.call-start = ((), (), s32[]{:S(2)}) async-start(), calls=%async_computation.7 | async-start | bytes 5308416 | tf_op jit(solution)/shard_map/all_gather | solution.py:165
  10.0 543.6 %reduce-scatter.7.cloned.1.call-start = ((), (), s32[]{:S(2)}) async-start(), calls=%async_computation.9 | async-start | bytes 1327104 | tf_op jit(solution)/shard_map/reduce_scatter | solution.py:228
  41.2 8.9 %copy-start.15 = (f32[768]{0:T(1024)}, f32[768]{0:T(1024)S(1)}, u32[]{:S(2)}) copy-start(f32[768]{0:T(1024)S(1)} %mul.156) | copy-start | bytes 9220
  42.0 8.1 %copy-start.13 = (f32[2,1024]{1,0:T(2,128)}, f32[2,1024]{1,0:T(2,128)S(1)}, u32[]{:S(2)}) copy-start(f32[2,1024]{1,0:T(2,128)S(1)} %convert_select_fusion) | copy-start | bytes 24580
  42.0 8.1 %copy-start.9 = (f32[2048]{0:T(1024)}, f32[2048]{0:T(1024)S(1)}, u32[]{:S(2)}) copy-start(f32[2048]{0:T(1024)S(1)} %get-tuple-element.62) | copy-start | bytes 24580
  42.0 8.1 %copy-start.11 = (f32[2048]{0:T(1024)}, f32[2048]{0:T(1024)S(1)}, u32[]{:S(2)}) copy-start(f32[2048]{0:T(1024)S(1)} %get-tuple-element.63) | copy-start | bytes 24580
  134.7 2.7 copy-start.2
  199.3 128.9 %slice-start = ((s8[6291456]{0:T(1024)(128)(4,1)}), s8[2097152]{0:T(1024)(128)(4,1)S(1)}, s32[]{:S(2)}) async-start(s8[6291456]{0:T(1024)(128)(4,1)} %bitcast.71), calls=%async_computation.13 | async-start | bytes 4194304
  279.4 31.9 %copy-start.19 = (bf16[768,3072]{1,0:T(8,128)(2,1)S(1)}, bf16[768,3072]{1,0:T(8,128)(2,1)}, u32[]{:S(2)}) copy-start(bf16[768,3072]{1,0:T(8,128)(2,1)} %all-gather.11.cloned.1.call-done) | copy-start | bytes 14155780
  279.4 48.8 %slice-start.1 = ((s8[6291456]{0:T(1024)(128)(4,1)}), s8[4194304]{0:T(1024)(128)(4,1)S(1)}, s32[]{:S(2)}) async-start(s8[6291456]{0:T(1024)(128)(4,1)} %bitcast.71), calls=%async_computation.14 | async-start | bytes 8388608
  328.2 9.1 %copy-start.21 = (bf16[2048,768]{1,0:T(8,128)(2,1)S(1)}, bf16[2048,768]{1,0:T(8,128)(2,1)}, u32[]{:S(2)}) copy-start(bf16[2048,768]{1,0:T(8,128)(2,1)} %get-tuple-element.15.o_ref) | copy-start | bytes 9437188
  334.6 2.7 copy-start.3
  337.3 3.8 copy-start.20
  341.1 212.5 %reduce-scatter.5.cloned.1.call-start = ((), (), s32[]{:S(2)}) async-start(), calls=%async_computation.8 | async-start | bytes 3981312 | tf_op jit(solution)/shard_map/reduce_scatter | solution.py:225
  421.0 2.8 copy-start.7
  421.0 3.8 copy-start.6
  423.8 4.8 copy-start.5
  425.0 3.6 copy-start.4
  428.6 9.8 %copy-start.8 = (bf16[2048,768]{1,0:T(8,128)(2,1)S(1)}, bf16[2048,768]{1,0:T(8,128)(2,1)}, u32[]{:S(2)}) copy-start(bf16[2048,768]{1,0:T(8,128)(2,1)} %bitcast_convert_fusion) | copy-start | bytes 9437188
  438.3 177.4 %reduce-scatter.11.cloned.1.call-start = ((), (), s32[]{:S(2)}) async-start(), calls=%async_computation.11 | async-start | bytes 5308416 | tf_op jit(solution)/shard_map/reduce_scatter | solution.py:209
  453.1 18.4 %copy-start.14 = (f32[2,1024]{1,0:T(2,128)S(1)}, f32[2,1024]{1,0:T(2,128)}, u32[]{:S(2)}) copy-start(f32[2,1024]{1,0:T(2,128)} %copy-done.13) | copy-start | bytes 24580
  453.1 261.2 %reduce-scatter.9.cloned.1.call-start = ((), (), s32[]{:S(2)}) async-start(), calls=%async_computation.10 | async-start | bytes 5308416 | tf_op jit(solution)/shard_map/reduce_scatter | solution.py:206
  471.3 3.2 copy-start.17
  471.3 292.0 %all-reduce.3.cloned.1.call-start = ((), (), s32[]{:S(2)}) async-start(), calls=%async_computation.12 | async-start | bytes 3538944 | tf_op jit(solution)/shard_map/psum | solution.py:248
  471.6 8.7 %copy-start.1 = (bf16[2,1024,768]{2,1,0:T(8,128)(2,1)S(1)}, bf16[2,1024,768]{2,1,0:T(8,128)(2,1)}, u32[]{:S(2)}) copy-start(bf16[2,1024,768]{2,1,0:T(8,128)(2,1)} %param.12) | copy-start | bytes 9437188
  471.6 8.7 %copy-start.10 = (f32[2048]{0:T(1024)S(1)}, f32[2048]{0:T(1024)}, u32[]{:S(2)}) copy-start(f32[2048]{0:T(1024)} %copy-done.9) | copy-start | bytes 24580
  471.6 8.7 %copy-start.12 = (f32[2048]{0:T(1024)S(1)}, f32[2048]{0:T(1024)}, u32[]{:S(2)}) copy-start(f32[2048]{0:T(1024)} %copy-done.11) | copy-start | bytes 24580
  471.6 8.7 %copy-start.16 = (f32[768]{0:T(1024)S(1)}, f32[768]{0:T(1024)}, u32[]{:S(2)}) copy-start(f32[768]{0:T(1024)} %copy-done.15) | copy-start | bytes 9220
Sparse Core Ops, SparseCore 0:
  10.2 66.4 all-gather.6
  78.9 39.2 all-gather.8
  120.4 78.8 all-gather.10
  201.4 78.0 all-gather.12
  341.2 61.6 reduce-scatter.6
  438.5 78.6 reduce-scatter.4
  520.8 94.8 reduce-scatter.10
  619.4 94.9 reduce-scatter.8
  717.0 46.2 all-reduce.2

commit v2 on v1

v2 whole, which is shorter than its diff:
```python
import functools

import jax
import jax.numpy as jnp
from jax import lax
from jax.experimental import pallas as pl
from jax.experimental.pallas import tpu as pltpu
from jax.sharding import PartitionSpec as P

HEADS = 12
F32 = jnp.float32
BF = jnp.bfloat16
EPS = 1e-05
ROOT = 0.7978845608028654
CUBIC = 0.044715
NN = (((1,), (0,)), ((), ()))
NT = (((1,), (1,)), ((), ()))
TN = (((0,), (0,)), ((), ()))


def dot(a, b, dims):
    return lax.dot_general(a, b, dims, preferred_element_type=F32)


def spread(x, lane):
    hi = x.astype(BF).astype(F32)
    rest = x - hi
    mid = rest.astype(BF).astype(F32)
    at = lane & 63
    zero = jnp.zeros_like(x)
    picked = jnp.where(at == 0, hi, jnp.where(at == 1, mid, jnp.where(at == 2, rest - mid, zero)))
    return picked.astype(BF)

def fwd_kernel(bq, q_ref, k_ref, v_ref, o_ref, l_ref):
    length=q_ref.shape[0]
    lane=lax.broadcasted_iota(jnp.int32,(length,128),1)
    left=lane<64
    lq=lax.broadcasted_iota(jnp.int32,(bq,128),1); leftq=lq<64
    v=v_ref[...].astype(F32)
    ones=jnp.ones_like(v)
    va=jnp.where(left,v,ones).astype(BF); vb=jnp.where(left,ones,v).astype(BF)
    k=k_ref[...]
    for i in range(length//bq):
        q=q_ref[pl.ds(i*bq,bq),:].astype(F32)*0.125
        zero=jnp.zeros_like(q)
        qa=jnp.where(leftq,q,zero).astype(BF); qb=jnp.where(leftq,zero,q).astype(BF)
        outs=[]; peaks=[]
        for qq,vv in ((qa,va),(qb,vb)):
            s=dot(qq,k,NT)
            m=jnp.max(s,axis=1,keepdims=True)
            p=jnp.exp(s-m).astype(BF)
            outs.append(dot(p,vv,NN)); peaks.append(m)
        oa,ob=outs
        num=jnp.where(leftq,oa,ob); den=jnp.where(leftq,ob,oa)
        o_ref[pl.ds(i*bq,bq),:]=(num/pltpu.roll(den,64,1)).astype(BF)
        lse=jnp.where(leftq,peaks[1],peaks[0])+jnp.log(den)
        l_ref[pl.ds(i*bq,bq),:]=spread(lse,lq)


def attn_fwd(qkv, rows, bq=512):
    n = qkv.shape[0]
    length = n // rows
    width = qkv.shape[1] // 3
    pairs = width // 128

    def spec(off):
        return pl.BlockSpec((length, 128), lambda s, p: (s, off + p))

    return pl.pallas_call(
        functools.partial(fwd_kernel, bq),
        grid=(rows, pairs),
        in_specs=[spec(0), spec(pairs), spec(2 * pairs)],
        out_specs=[spec(0), spec(0)],
        out_shape=[jax.ShapeDtypeStruct((n, width), BF)] * 2,
        compiler_params=pltpu.CompilerParams(vmem_limit_bytes=56 << 20),
        cost_estimate=pl.CostEstimate(
            flops=30 * n * length * width,
            bytes_accessed=n * width * 10,
            transcendentals=n * length * width // 64,
        ),
        name="attention_forward",
    )(qkv, qkv, qkv)


def bwd_kernel(bq, q_ref,k_ref,v_ref,o_ref,l_ref,g_ref,out_ref,ak,av):
    length=q_ref.shape[0]
    part=out_ref.shape[1]//3
    start=pl.program_id(1)*128
    cols=[pl.ds(pl.multiple_of(start+j*part,128),128) for j in range(3)]
    lane=lax.broadcasted_iota(jnp.int32,(length,128),1)
    left=lane<64; at=lane&63
    lq=lax.broadcasted_iota(jnp.int32,(bq,128),1); leftq=lq<64
    k=k_ref[...].astype(F32); v=v_ref[...].astype(F32)
    tail=jnp.where(at<3,-1.0,0.0).astype(F32)
    zero=jnp.zeros_like(k)
    kx=(jnp.where(left,k,tail).astype(BF),jnp.where(left,tail,k).astype(BF))
    km=(jnp.where(left,k,zero).astype(BF),jnp.where(left,zero,k).astype(BF))
    vx=(jnp.where(left,v,tail).astype(BF),jnp.where(left,tail,v).astype(BF))
    for i in range(length//bq):
        at_q=pl.ds(i*bq,bq)
        q=q_ref[at_q,:].astype(F32)*0.125
        l=l_ref[at_q,:].astype(F32)
        g=g_ref[at_q,:].astype(F32)
        zq=jnp.zeros_like(q)
        prod=g*o_ref[at_q,:].astype(F32)
        da=jnp.sum(jnp.where(leftq,prod,zq),axis=1,keepdims=True)
        db=jnp.sum(jnp.where(leftq,zq,prod),axis=1,keepdims=True)
        d=spread(jnp.where(leftq,db,da),lq).astype(F32)
        qx=(jnp.where(leftq,q,l).astype(BF),jnp.where(leftq,l,q).astype(BF))
        qm=(jnp.where(leftq,q,zq).astype(BF),jnp.where(leftq,zq,q).astype(BF))
        gx=(jnp.where(leftq,g,d).astype(BF),jnp.where(leftq,d,g).astype(BF))
        gm=(jnp.where(leftq,g,zq).astype(BF),jnp.where(leftq,zq,g).astype(BF))
        gq=None; gk=None; gv=None
        for h in range(2):
            p=jnp.exp(dot(kx[h],qx[h],NT))
            ds=(p*dot(vx[h],gx[h],NT)).astype(BF)
            tv=dot(p.astype(BF),gm[h],NN); tk=dot(ds,qm[h],NN); tq=dot(ds,km[h],TN)
            gq=tq if gq is None else gq+tq
            gk=tk if gk is None else gk+tk
            gv=tv if gv is None else gv+tv
        out_ref[at_q,cols[0]]=(gq*0.125).astype(BF)
        if i==0: ak[...]=gk; av[...]=gv
        else: ak[...]+=gk; av[...]+=gv
    out_ref[:,cols[1]]=ak[...].astype(BF)
    out_ref[:,cols[2]]=av[...].astype(BF)


def attn_bwd(qkv, mixed, lse, gmixed, first, rows, bq=256):
    n = qkv.shape[0]
    length = n // rows
    width = qkv.shape[1] // 3
    pairs = width // 128

    def spec(off):
        return pl.BlockSpec((length, 128), lambda s, p: (s, off + p))

    return pl.pallas_call(
        functools.partial(bwd_kernel, bq),
        grid=(rows, pairs),
        in_specs=[
            spec(0),
            spec(pairs),
            spec(2 * pairs),
            spec(0),
            spec(0),
            spec(first),
        ],
        out_specs=pl.BlockSpec((length, 3 * width), lambda s, p: (s, 0)),
        out_shape=jax.ShapeDtypeStruct((n, 3 * width), BF),
        scratch_shapes=[pltpu.VMEM((length, 128), F32)] * 2,
        compiler_params=pltpu.CompilerParams(vmem_limit_bytes=56 << 20),
        cost_estimate=pl.CostEstimate(
            flops=52 * n * length * width,
            bytes_accessed=n * width * 18,
            transcendentals=n * length * width // 64,
        ),
        name="attention_backward",
    )(qkv, qkv, qkv, mixed, lse, gmixed)


def mid_kernel(T, at, x_any, m0_any, m1_any, g, mine, other, back_mine, back_other, vec_ref, fb_ref,
               out_ref, gh_ref, gm_ref, keep, send, sum_ref, fs_ref,
               wo, wi_s, wb_s, gi_s, gb_s, n2, n2t, gt, xh, acc, ai, ab, sem, wsem, gsem):
    f, nf = pl.program_id(0), pl.num_programs(0)
    core = at[0]
    n, D = n2.shape
    F = wi_s.shape[2]
    blocks, half, r = n // T, D // 2, D // 8
    x_ref, m_ref, gtw = out_ref, gm_ref, gh_ref

    def weights(step, slot):
        part, local = step // (nf // 2), lax.rem(step, nf // 2)
        cols = pl.ds(pl.multiple_of(half + local * F, 128), F)
        rows = pl.ds(pl.multiple_of(step * F, 128), F)
        left = pl.ds(pl.multiple_of(core * half, 128), half)
        right = pl.ds(pl.multiple_of((1 - core) * half, 128), half)
        return part, (
            pltpu.make_async_copy(mine.at[:, cols], wi_s.at[slot], wsem.at[slot, 0]),
            pltpu.make_async_copy(other.at[:, cols], wi_s.at[slot], wsem.at[slot, 0]),
            pltpu.make_async_copy(back_mine.at[rows, :], wb_s.at[slot, :, left], wsem.at[slot, 1]),
            pltpu.make_async_copy(back_other.at[rows, :], wb_s.at[slot, :, right], wsem.at[slot, 2]),
        )

    def fetch(step, slot):
        part, (a, b, c, d) = weights(step, slot)

        @pl.when(part == core)
        def _():
            a.start()

        @pl.when(part != core)
        def _():
            b.start()

        c.start()
        d.start()

    def grads(step):
        part, local = step // (nf // 2), lax.rem(step, nf // 2)
        out = []
        per = F // half
        for w in range(8):
            for k in range(per):
                row = pl.multiple_of(r + (local * per + k) * r, r)
                out.append((part, w, pl.ds(row, r), gi_s.at[w * r : (w + 1) * r, k * half : (k + 1) * half]))
        for k in range(per):
            for h in range(2):
                out.append((h, step * per + k, pl.ds(5 * r, half), gb_s.at[h * half : (h + 1) * half, k * half : (k + 1) * half]))
        return out

    def store(copies, first):
        for i, (part, w, rows, src) in enumerate(copies):
            @pl.when(part == core)
            def _():
                pltpu.make_async_copy(src, keep.at[w, rows, :], gsem.at[first + i]).start()

            @pl.when(part != core)
            def _():
                pltpu.make_async_copy(src, send.at[w, rows, :], gsem.at[first + i]).start()

    def settle(copies, first):
        for i, (part, w, rows, src) in enumerate(copies):
            pltpu.make_async_copy(src, keep.at[w, rows, :], gsem.at[first + i]).wait()

    slot = lax.rem(f, 2)

    @pl.when(f == 0)
    def _():
        cx = pltpu.make_async_copy(x_any, x_ref, sem.at[0])
        cx.start()
        start = 0
        cm = []
        for j, a in enumerate((m0_any, m1_any)):
            w = a.shape[1]
            cm.append(pltpu.make_async_copy(a, m_ref.at[:, pl.ds(start, w)], sem.at[1 + j]))
            start += w
        left = pl.ds(pl.multiple_of(core * half, 128), half)
        right = pl.ds(pl.multiple_of((1 - core) * half, 128), half)
        cm.append(pltpu.make_async_copy(mine.at[:, pl.ds(0, half)], wo.at[:, left], sem.at[3]))
        cm.append(pltpu.make_async_copy(other.at[:, pl.ds(0, half)], wo.at[:, right], sem.at[4]))
        for copy in cm:
            copy.start()
        fetch(0, 0)
        for copy in [cx] + cm:
            copy.wait()

        @pl.loop(0, blocks)
        def _(i):
            at_t = pl.ds(pl.multiple_of(i * T, T), T)
            hidden = x_ref[at_t, :].astype(F32) + dot(m_ref[at_t, :], wo[...], NN) + vec_ref[2:3, :]
            c = hidden - jnp.mean(hidden, axis=1, keepdims=True)
            inv = lax.rsqrt(jnp.mean(c * c, axis=1, keepdims=True) + EPS)
            nn = (c * inv * vec_ref[0:1, :] + vec_ref[1:2, :]).astype(BF)
            acc[at_t, :] = hidden + vec_ref[3:4, :]
            xh[at_t, :] = c
            n2[at_t, :] = nn
            n2t[:, at_t] = nn.T
            gt[:, at_t] = g[at_t, :].T

    @pl.when(f < nf - 1)
    def _():
        fetch(f + 1, 1 - slot)

    _, (a, b, c, d) = weights(f, slot)
    a.wait()
    c.wait()
    d.wait()
    wi_ref, wb_ref = wi_s.at[slot], wb_s.at[slot]
    fs = None
    for i in range(blocks):
        at_t = pl.ds(i * T, T)
        pre = dot(n2[at_t, :], wi_ref[...], NN) + fb_ref[...]
        ga = dot(g[at_t, :], wb_ref[...], NT)
        sq = pre * pre
        t = jnp.tanh(pre * (ROOT + (ROOT * CUBIC) * sq))
        part = 0.5 * pre
        act = (part + part * t).astype(BF)
        slope = (0.5 + 0.5 * t) + part * (1.0 - t * t) * (ROOT + (3 * ROOT * CUBIC) * sq)
        gp = (ga * slope).astype(BF)
        s = jnp.sum(gp.astype(F32), axis=0, keepdims=True)
        fs = s if fs is None else fs + s
        a = dot(n2t[:, i * T : (i + 1) * T], gp, NN)
        b = dot(gt[:, i * T : (i + 1) * T], act, NN)
        if i == 0:
            ai[...] = a
            ab[...] = b
        elif i < blocks - 1:
            ai[...] += a
            ab[...] += b
        else:
            @pl.when(f > 0)
            def _():
                settle(grads(f - 1), 0)

            gi_s[...] = (ai[...] + a).astype(BF)
            gb_s[...] = (ab[...] + b).astype(BF)
            store(grads(f), 0)
        acc[at_t, :] += dot(act, wb_ref[...], NN)
        gtwo = dot(gp, wi_ref[...], NT)

        @pl.when(f == 0)
        def _():
            gtw[at_t, :] = gtwo

        @pl.when(f > 0)
        def _():
            gtw[at_t, :] += gtwo

    fs_ref[...] = fs

    @pl.when(f == nf - 1)
    def _():
        sum_ref[...] = jnp.zeros_like(sum_ref)
        ai[...] = jnp.zeros_like(ai)

        @pl.loop(0, blocks)
        def _(i):
            at_t = pl.ds(pl.multiple_of(i * T, T), T)
            out_ref[at_t, :] = acc[at_t, :].astype(BF)
            gtwo, c = gtw[at_t, :], xh[at_t, :]
            inv = lax.rsqrt(jnp.mean(c * c, axis=1, keepdims=True) + EPS)
            xhat = c * inv
            e = gtwo * vec_ref[0:1, :]
            m1 = jnp.mean(e, axis=1, keepdims=True)
            m2 = jnp.mean(e * xhat, axis=1, keepdims=True)
            gg = g[at_t, :].astype(F32)
            gh = gg + inv * (e - m1 - xhat * m2)
            gh_ref[at_t, :] = gh
            ga = gh.astype(BF)
            ai[...] += dot(m_ref[at_t, :], ga, TN)
            gm_ref[at_t, :] = dot(ga, wo[...], NT).astype(BF)
            rows = (gtwo * xhat, gtwo, ga.astype(F32), gg)
            sum_ref[...] += jnp.concatenate([jnp.sum(v, axis=0, keepdims=True) for v in rows], axis=0)

        settle(grads(f), 0)
        gi_s[...] = ai[...].astype(BF)
        last_ones = [
            (h, w, pl.ds(0, r), gi_s.at[w * r : (w + 1) * r, h * half : (h + 1) * half])
            for w in range(8)
            for h in range(2)
        ]
        store(last_ones, 0)
        settle(last_ones, 0)


def middle(core, x, mixed, g, mine, other, back_mine, back_other, vec, fb, F=768, T=256):
    n, D = x.shape
    FF = fb.shape[1]
    one = pl.Buffered(1)

    def full(shape):
        return pl.BlockSpec(shape, lambda f: (0, 0), pipeline_mode=one)

    anywhere = pl.BlockSpec(memory_space=pl.ANY)
    packed = (8, D // 8 + 2 * FF // 16 + D // 2, D // 2)
    return pl.pallas_call(
        functools.partial(mid_kernel, T),
        grid=(FF // F,),
        in_specs=[pl.BlockSpec(memory_space=pltpu.SMEM)]
        + [anywhere] * 3
        + [full((n, D))]
        + [anywhere] * 4
        + [full((4, D)), pl.BlockSpec((1, F), lambda f: (0, f))],
        out_specs=[full((n, D)), full((n, D)), full((n, D)), anywhere, anywhere]
        + [full((4, D)), pl.BlockSpec((1, F), lambda f: (0, f))],
        out_shape=[
            jax.ShapeDtypeStruct((n, D), BF),
            jax.ShapeDtypeStruct((n, D), F32),
            jax.ShapeDtypeStruct((n, D), BF),
            jax.ShapeDtypeStruct(packed, BF),
            jax.ShapeDtypeStruct(packed, BF),
            jax.ShapeDtypeStruct((4, D), F32),
            jax.ShapeDtypeStruct((1, FF), F32),
        ],
        scratch_shapes=[
            pltpu.VMEM((D, D), BF),
            pltpu.VMEM((2, D, F), BF),
            pltpu.VMEM((2, F, D), BF),
            pltpu.VMEM((D, F), BF),
            pltpu.VMEM((D, F), BF),
            pltpu.VMEM((n, D), BF),
            pltpu.VMEM((D, n), BF),
            pltpu.VMEM((D, n), BF),
            pltpu.VMEM((n, D), F32),
            pltpu.VMEM((n, D), F32),
            pltpu.VMEM((D, F), F32),
            pltpu.VMEM((D, F), F32),
            pltpu.SemaphoreType.DMA((5,)),
            pltpu.SemaphoreType.DMA((2, 3)),
            pltpu.SemaphoreType.DMA((20,)),
        ],
        compiler_params=pltpu.CompilerParams(vmem_limit_bytes=63 << 20),
        cost_estimate=pl.CostEstimate(
            flops=24 * n * D * FF,
            bytes_accessed=n * D * 16 + 12 * D * FF,
            transcendentals=n * FF,
        ),
        name="feed_forward",
    )(core, x, *mixed, g, mine, other, back_mine, back_other, vec, fb)


def last_kernel(x_ref, gh_ref, gain_ref, *refs):
    groups = (len(refs) - 2) // 2
    grads, weights = refs[:groups], refs[groups : 2 * groups]
    out_ref, sum_ref = refs[2 * groups :]
    x = x_ref[...].astype(F32)
    c = x - jnp.mean(x, axis=1, keepdims=True)
    inv = lax.rsqrt(jnp.mean(c * c, axis=1, keepdims=True) + EPS)
    xhat = c * inv
    one = None
    for grad, weight in zip(grads, weights):
        part = dot(grad[...], weight[...], NT)
        one = part if one is None else one + part
    e = one * gain_ref[...]
    m1 = jnp.mean(e, axis=1, keepdims=True)
    m2 = jnp.mean(e * xhat, axis=1, keepdims=True)
    out_ref[...] = gh_ref[...] + inv * (e - m1 - xhat * m2)
    sums = [one * xhat, one] + [grad[...].astype(F32) for grad in grads]
    sums = jnp.concatenate([jnp.sum(v, axis=0, keepdims=True) for v in sums], axis=1)

    @pl.when(pl.program_id(0) == 0)
    def _():
        sum_ref[...] = sums

    @pl.when(pl.program_id(0) > 0)
    def _():
        sum_ref[...] += sums


def last(x, gh, gain, grads, weights, T=256):
    n, D = x.shape
    total = 2 * D + sum(grad.shape[1] for grad in grads)
    block = pl.BlockSpec((T, D), lambda i: (i, 0))
    return pl.pallas_call(
        last_kernel,
        grid=(n // T,),
        in_specs=[block, block, pl.BlockSpec((1, D), lambda i: (0, 0))]
        + [pl.BlockSpec((T, grad.shape[1]), lambda i: (i, 0)) for grad in grads]
        + [pl.BlockSpec(weight.shape, lambda i: (0, 0)) for weight in weights],
        out_specs=[block, pl.BlockSpec((1, total), lambda i: (0, 0))],
        out_shape=[jax.ShapeDtypeStruct((n, D), F32), jax.ShapeDtypeStruct((1, total), F32)],
        compiler_params=pltpu.CompilerParams(vmem_limit_bytes=56 << 20),
        cost_estimate=pl.CostEstimate(
            flops=12 * n * D * D, bytes_accessed=n * D * 16, transcendentals=0
        ),
        name="input_gradient",
    )(x, gh, gain, *grads, *weights)


def project_kernel(order, rows, half, at, n1, mine, other, bias, qkv, w, sem):
    me, core = at[0], at[1]

    @pl.when(pl.program_id(0) == 0)
    def _():
        copies = []
        for i, o in enumerate(order):
            row = pl.ds(pl.multiple_of((me ^ o) * rows, rows), rows)
            for src, part in ((mine, core), (other, 1 - core)):
                col = pl.ds(pl.multiple_of(part * half, 128), half)
                copies.append(
                    pltpu.make_async_copy(src.at[i, pl.ds(0, rows), :], w.at[row, col], sem.at[len(copies)])
                )
        for copy in copies:
            copy.start()
        for copy in copies:
            copy.wait()

    qkv[...] = (dot(n1[...], w[...], NN) + bias[...]).astype(BF)


def project(n1, mine, other, order, rows, bias, T=512):
    n, D = n1.shape
    half = mine.shape[2]
    me, core = lax.axis_index("wide"), lax.axis_index("narrow") & 1
    if rows % 16:
        mine, other = [natural(p[:, :rows], order).reshape(-1, half) for p in (mine, other)]
        w = jnp.where(core == 0, jnp.concatenate([mine, other], 1), jnp.concatenate([other, mine], 1))
        return (dot(n1, w, NN) + bias).astype(BF), w
    anywhere = pl.BlockSpec(memory_space=pl.ANY)
    return pl.pallas_call(
        functools.partial(project_kernel, order, rows, half),
        grid=(n // T,),
        in_specs=[
            pl.BlockSpec(memory_space=pltpu.SMEM),
            pl.BlockSpec((T, D), lambda i: (i, 0)),
            anywhere,
            anywhere,
            pl.BlockSpec((1, 2 * half), lambda i: (0, 0)),
        ],
        out_specs=[
            pl.BlockSpec((T, 2 * half), lambda i: (i, 0)),
            pl.BlockSpec((D, 2 * half), lambda i: (0, 0)),
        ],
        out_shape=[
            jax.ShapeDtypeStruct((n, 2 * half), BF),
            jax.ShapeDtypeStruct((D, 2 * half), BF),
        ],
        scratch_shapes=[pltpu.SemaphoreType.DMA((2 * len(order),))],
        compiler_params=pltpu.CompilerParams(vmem_limit_bytes=56 << 20),
        cost_estimate=pl.CostEstimate(
            flops=8 * n * D * half, bytes_accessed=n * D * 4 + n * half * 4, transcendentals=0
        ),
        name="project",
    )(jnp.stack([me, core]).astype(jnp.int32), n1, mine, other, bias)


def swap(x, axis, mask):
    size = lax.axis_size(axis)
    return lax.ppermute(x, axis, [(i, i ^ mask) for i in range(size)])


def bit_groups(size):
    top = size.bit_length() - 1
    cuts = [(0, 1)]
    low = 1
    while low < top:
        high = min(low + 2, top)
        cuts.append((low, high))
        low = high
    return cuts


def gather_wide(piece):
    size = lax.axis_size("wide")
    me = lax.axis_index("wide")
    stack, order = piece[None], [0]
    for low, high in reversed(bit_groups(size)):
        masks = [m << low for m in range(1 << (high - low))]
        stack = jnp.concatenate([stack] + [swap(stack, "wide", m) for m in masks[1:]])
        order = [o ^ m for m in masks for o in order]
    return stack, order


def natural(stack, order):
    size = len(order)
    me = lax.axis_index("wide")
    place = jnp.argsort(jnp.array(order))
    return jnp.take(stack, place[me ^ jnp.arange(size)], axis=0)


def gather(piece):
    mine, order = gather_wide(piece)
    return mine, swap(mine, "narrow", 1), order


def half_of(x, index, size, axis):
    return lax.dynamic_slice_in_dim(x, index * size, size, axis)


def add(*terms):
    total = terms[0].astype(F32)
    for term in terms[1:]:
        total = total + term.astype(F32)
    return total.astype(BF)


def scatter_wide(x):
    me = lax.axis_index("wide")
    size = x.shape[0]
    for low, high in bit_groups(size):
        ways = 1 << (high - low)
        mine = (me >> low) & (ways - 1)
        split = x.reshape((x.shape[0] // ways, ways) + x.shape[1:])
        got = [lax.dynamic_index_in_dim(split, mine, 1, keepdims=False)]
        for m in range(1, ways):
            sent = lax.dynamic_index_in_dim(split, mine ^ m, 1, keepdims=False)
            got.append(swap(sent, "wide", m << low))
        x = add(*got)
    return x[0]


def exchange(mine):
    core = lax.axis_index("narrow") & 1
    mine = add(mine, swap(mine, "narrow", 2))
    other = swap(mine, "narrow", 1)
    return [jnp.where(core == 0, mine, other), jnp.where(core == 0, other, mine)]


def reduce(grad):
    half = grad.shape[2] // 2
    core = lax.axis_index("narrow") & 1
    kept = add(half_of(grad, core, half, 2), swap(half_of(grad, 1 - core, half, 2), "narrow", 1))
    return jnp.concatenate(exchange(scatter_wide(kept)), axis=1).astype(F32)


def reduce_small(x):
    me = lax.axis_index("wide")
    for low, high in bit_groups(x.shape[0]):
        ways = 1 << (high - low)
        mine = (me >> low) & (ways - 1)
        split = x.reshape((x.shape[0] // ways, ways) + x.shape[1:])
        got = [lax.dynamic_index_in_dim(split, mine, 1, keepdims=False)]
        for m in range(1, ways):
            got.append(swap(lax.dynamic_index_in_dim(split, mine ^ m, 1, keepdims=False), "wide", m << low))
        x = sum(got[1:], got[0])
    x = x[0]
    a, b, c = [swap(x, "narrow", m) for m in (1, 2, 3)]
    return (x + a) + (b + c)


def regroup(summed, size):
    eight, depth, step = summed.shape
    r = 2 * step // eight
    rows = summed[:, : 5 * r].reshape(eight, 5, r, step).transpose(0, 2, 1, 3).reshape(size, -1, 5, step)
    rows = rows.transpose(0, 2, 1, 3).reshape(size, -1, step)
    back = summed[:, 5 * r :].transpose(1, 0, 2).reshape(step, size, -1).transpose(1, 0, 2)
    return jnp.concatenate([rows, back.reshape(size, -1, step)], axis=1).reshape(-1, step)


def body(tokens, cotangent, row_kind, grad_mask, w_qkv, w_out, w_in, w_back, norm_gain, norm_shift, proj_bias, ffn_bias):
    rows, length, width = tokens.shape
    n = rows * length
    size = lax.axis_size("wide")
    share = width // size
    core = lax.axis_index("narrow") & 1
    packed = jnp.concatenate([norm_gain, norm_shift, proj_bias, ffn_bias.reshape(-1, share)])
    cuts = [0, width // 3, width]
    split = w_qkv.reshape(share, 3, width)
    pieces = []
    for low, high in zip(cuts, cuts[1:]):
        columns = split[:, :, low:high].reshape(share, 3 * (high - low))
        pieces.append(half_of(columns, core, 3 * (high - low) // 2, 1))
    half = pieces[0].shape[1]
    extra = jnp.pad(packed.reshape(-1), (0, 16 * half - packed.size)).reshape(16, half)
    pieces[0] = jnp.concatenate([pieces[0], extra])
    gathered = [gather(piece) for piece in pieces]
    small = natural(gathered[0][0][:, share:], gathered[0][2])
    small = small.reshape(size, -1)[:, : packed.size].reshape((size,) + packed.shape).astype(F32)
    hid = w_in.shape[1] // 2
    piece = jnp.concatenate(
        [half_of(w_out, core, width // 2, 1), half_of(w_in, core, hid, 1)]
        + [half_of(w_back[i * share : (i + 1) * share], core, width // 2, 1) for i in range(w_back.shape[0] // share)],
        axis=1,
    )
    mine = lax.all_gather(piece, "wide", axis=0, tiled=True)
    other = swap(mine, "narrow", 1)

    def back_half(gathered):
        chunks = gathered[:, width // 2 + hid :].reshape(size, share, -1, width // 2)
        return chunks.transpose(0, 2, 1, 3).reshape(-1, width // 2)

    by_column = small[:, :8].transpose(1, 0, 2).reshape(8, width)
    gains, shifts, biases = by_column[:2], by_column[2:4], by_column[4:8]
    ffn_bias_full = small[:, 8:].reshape(1, -1)
    x = tokens.reshape(n, width)
    inputs = x.astype(F32)
    centred = inputs - jnp.mean(inputs, axis=-1, keepdims=True)
    inv = lax.rsqrt(jnp.mean(centred * centred, axis=-1, keepdims=True) + EPS)
    normed_one = (centred * inv * gains[0] + shifts[0]).astype(BF)
    keep = jnp.where(row_kind[:, None] == 1, jnp.ones(grad_mask.shape, F32), grad_mask.astype(F32))
    g_ffn = (cotangent.astype(F32) * keep[:, :, None]).reshape(n, width).astype(BF)
    qkv, mixed, lse, w_groups = [], [], [], []
    for g, (low, high) in enumerate(zip(cuts, cuts[1:])):
        bias = jnp.concatenate([biases[0, low:high], jnp.zeros((high - low,), F32), biases[1, low:high]])
        got, w = project(normed_one, *gathered[g], share, bias[None])
        qkv.append(got)
        w_groups.append(w)
        m, l = attn_fwd(got, rows)
        mixed.append(m)
        lse.append(l)
    vec = jnp.stack([gains[1], shifts[1], biases[2], biases[3]])
    layer_out, g_hidden, g_mixed, kept, sent, sums, ffn_sum = middle(
        core[None], x, mixed, g_ffn, mine, other, back_half(mine), back_half(other), vec, ffn_bias_full
    )
    summed = add(kept, swap(sent, "narrow", 1))
    if size != summed.shape[0]:
        summed = regroup(summed, size)
    else:
        summed = summed.reshape(-1, summed.shape[2])
    summed = lax.psum_scatter(summed, "wide", scatter_dimension=0, tiled=True)
    left, right = exchange(summed)
    step = width // 2
    both = [t.astype(F32) for t in (left, right)]
    share_out = jnp.concatenate([t[:share] for t in both], axis=1)
    share_in = jnp.concatenate(
        [t[i * share : (i + 1) * share] for t in both for i in range(1, 5)], axis=1
    )
    share_back = jnp.concatenate([t[5 * share :].reshape(step, -1) for t in both], axis=0).T
    g_groups, share_groups = [None, None], [None, None]
    for g in (1, 0):
        low, high = cuts[g], cuts[g + 1]
        g_groups[g] = attn_bwd(qkv[g], mixed[g], lse[g], g_mixed, low // 128, rows)
        grad = dot(normed_one, g_groups[g], TN).astype(BF)
        share_groups[g] = reduce(grad.reshape(size, share, -1)).reshape(share, 3, high - low)
    input_grad, last_sums = last(x, g_hidden, gains[:1], g_groups, w_groups)
    last_sums = last_sums[0]
    columns, at = [], 2 * width
    for low, high in zip(cuts, cuts[1:]):
        columns.append(last_sums[at : at + 3 * (high - low)].reshape(3, high - low))
        at += 3 * (high - low)
    column_sums = jnp.concatenate(columns, axis=1)
    by_column = jnp.stack(
        [last_sums[:width], sums[0], last_sums[width : 2 * width], sums[1], column_sums[0], column_sums[2], sums[2], sums[3]]
    )
    by_column = by_column.reshape(8, size, share).transpose(1, 0, 2)
    small = reduce_small(jnp.concatenate([by_column, ffn_sum.reshape(size, -1, share)], axis=1))
    return (
        layer_out.reshape(rows, length, width),
        input_grad.reshape(rows, length, width),
        jnp.concatenate(share_groups, axis=2).reshape(share, 3 * width),
        share_out,
        share_in,
        share_back,
        small[:2],
        small[2:4],
        small[4:8],
        small[8:].reshape(-1),
    )


def solution(mesh):
    in_specs = (
        P(("wide", "narrow"), None, None),
        P(("wide", "narrow"), None, None),
        P(("wide", "narrow")),
        P(("wide", "narrow"), None),
        P("wide", None),
        P("wide", None),
        P("wide", None),
        P("wide", None),
        P(None, "wide"),
        P(None, "wide"),
        P(None, "wide"),
        P("wide"),
    )
    out_specs = (
        P(("wide", "narrow"), None, None),
        P(("wide", "narrow"), None, None),
        P("wide", None),
        P("wide", None),
        P("wide", None),
        P("wide", None),
        P(None, "wide"),
        P(None, "wide"),
        P(None, "wide"),
        P("wide"),
    )
    return jax.shard_map(body, mesh=mesh, in_specs=in_specs, out_specs=out_specs, check_vma=False)
```

time: 782 us -> 510 us (0.65)
  waiting for transfers between devices: 343 us -> 87.2 us
  matrix products: 175 us -> 13.4 us
  Pallas kernels: 113 us -> 260 us
  blocking collectives: 66.2 us -> 0 us
  starting transfers between devices: 0.57 us -> 47.8 us
  local copies, waits for them, and re-layouts: 17.8 us -> 54.5 us
  other arithmetic: 48.4 us -> 25.3 us
    dot_general x12 -> x2, matrix products: 175 us -> 13.4 us  [dot(): return lax.dot_general(a, b, dims, preferred_element_type=F32)]
    reduce_scatter x4 -> x1, waiting for transfers between devices: 161 us -> 0.01 us  [body(): summed = lax.psum_scatter(summed, 'wide', scatter_dimension=0, tiled=True)]
    pallas_call x0 -> x4, Pallas kernels: none -> 141 us  [the longest x1 105 us: middle(): pl.pallas_call(functools.partial(mid_kernel, T), grid=(FF // F,), in_spec...]
    all_gather x4 -> x1, waiting for transfers between devices: 138 us -> 41.8 us  [body(): mine = lax.all_gather(piece, 'wide', axis=0, tiled=True)]
    ppermute x0 -> x35, starting transfers between devices: none -> 47.8 us  [swap(): return lax.ppermute(x, axis, [(i, i ^ mask) for i in range(size)])]
    ppermute x0 -> x35, waiting for transfers between devices: none -> 45.4 us  [swap(): return lax.ppermute(x, axis, [(i, i ^ mask) for i in range(size)])]
    psum x1 -> x0, waiting for transfers between devices: 41.6 us -> none  [body(): summed = lax.psum((qkv_share, out_share, in_share, back_share), 'narrow')]
    psum x1 -> x0, blocking collectives: 40.8 us -> none  [body(): small = lax.psum(small.astype(jnp.bfloat16), ('wide', 'narrow'))]
  transfers between devices with their start and end apart: 9 -> 37, of which waited for: 6 -> 14; matrix products, arithmetic and copies ran while one was open for 21% -> 13% of each run, Pallas kernels for 15% -> 31%
where the time goes in v2:
time: 510 us; the launch traced here: 504 us
  Pallas kernels  260 us (51%)
  waiting for transfers between devices  87.2 us (17%)
  local copies, waits for them, and re-layouts  54.5 us (11%)
  starting transfers between devices  47.8 us (9%)
  other arithmetic  25.3 us (5%)
  between operations  15.2 us (3%)
  matrix products  13.4 us (3%)
    pallas_call x1, Pallas kernels, middle(): pl.pallas_call(functools.partial(mid_kernel, T), grid=(FF // F,), in_spec...  105 us
    pallas_call x2, Pallas kernels, attn_bwd(): pl.pallas_call(functools.partial(bwd_kernel, bq), grid=(rows, pairs), in_...  76.6 us
    ppermute x35, starting transfers between devices, swap(): return lax.ppermute(x, axis, [(i, i ^ mask) for i in range(size)])  47.8 us
    ppermute x35, waiting for transfers between devices, swap(): return lax.ppermute(x, axis, [(i, i ^ mask) for i in range(size)])  45.4 us
    pallas_call x2, Pallas kernels, attn_fwd(): pl.pallas_call(functools.partial(fwd_kernel, bq), grid=(rows, pairs), in_...  42.1 us
    all_gather x1, waiting for transfers between devices, body(): mine = lax.all_gather(piece, 'wide', axis=0, tiled=True)  41.8 us
    pallas_call x2, Pallas kernels, project(): pl.pallas_call(functools.partial(project_kernel, order, rows, half), grid...  18.5 us
    pallas_call x1, Pallas kernels, last(): pl.pallas_call(last_kernel, grid=(n // T,), in_specs=[block, block, pl.Bl...  17.5 us
  transfers between devices with their start and end apart: 37, of which 14 were waited for; matrix products, arithmetic and copies ran while one was open for 13% of the time, Pallas kernels for 31%

profile of v2, /device:TPU:1, one launch (start us, length us, event | category | flops | bytes accessed | tf_op | source)
XLA Modules:
  0.0 503.6 jit_solution(16747860856503244184)
XLA Ops:
  7.2 1.2 fusion.10
  8.5 0.9 dynamic-slice_dynamic-update-slice_fusion.5
  9.4 1.0 dynamic-slice_dynamic-update-slice_fusion
  13.4 2.1 collective-permute-start
  15.5 2.3 collective-permute-start.1
  17.8 1.1 slice.247
  20.1 3.2 collective-permute-start.6
  25.2 1.1 fusion.1
  27.1 2.2 multiply_convert_fusion
  30.2 1.1 pad_maximum_fusion.2
  31.2 1.3 collective-permute-start.3
  32.5 1.5 constant_dynamic-update-slice_fusion.3
  34.1 1.5 constant_dynamic-update-slice_fusion.2
  35.6 1.5 constant_dynamic-update-slice_fusion.1
  37.1 3.0 collective-permute-done.6
  40.9 1.8 pad_maximum_fusion
  42.7 1.2 collective-permute-start.8
  46.7 0.9 slice.239
  47.6 9.6 %collective-permute-start.4 = (bf16[8,112,384]{2,1,0:T(8,128)(2,1)}, bf16[8,112,384]{2,1,0:T(8,128)(2,1)}, u32[]{:S(2)}, u32[]{:S(2)}) collective-permute-start(bf16[8,112,384]{2,1,0:T(8,128)(2,1)} %constant_dynamic-update-slice_fusion.mine), channel_id=1, source_target_pairs={{0,1},{1,0},{2,3},{3,2},{4,5},{5,4},{6,7},{7,6},{8,9},{9,8},{10,11... | collective-permute-start | bytes 2064392 | tf_op jit(solution)/shard_map/ppermute | solution.py:509
  61.8 2.8 add_convert_fusion.1.n1
  64.6 1.9 constant_dynamic-update-slice_fusion.5.mine
  66.5 7.8 %project.2 = (bf16[2048,768]{1,0:T(8,128)(2,1)}, bf16[768,768]{1,0:T(8,128)(2,1)}) custom-call(s32[2]{0:T(128)} %pad_add_fusion.at, bf16[2048,768]{1,0:T(8,128)(2,1)} %add_convert_fusion.1.n1, bf16[8,112,384]{2,1,0:T(8,128)(2,1)} %constant_dynamic-update-slice_fusion.mine, bf16[8,112,384]{2,1,0:T(8,128)(2,1)} %collective-permute-done.4.other, ...), custom_call_target="tpu_custom_call" | custom-call | flops 4831838208 | bytes 9437184 | tf_op jit(solution)/shard_map/project/pallas_call | solution.py:480
  74.4 41.8 %all-gather.2.cloned.1.call-done.mine = bf16[768,3456]{1,0:T(8,128)(2,1)} async-done(((bf16[96,3456]{1,0:T(8,128)(2,1)}), bf16[768,3456]{1,0:T(8,128)(2,1)}) %all-gather.2.cloned.1.call-update) | async-done | bytes 5308432 | tf_op jit(solution)/shard_map/all_gather | solution.py:635
  116.6 14.6 %attention_forward.2 = (bf16[2048,256]{1,0:T(8,128)(2,1)}, bf16[2048,256]{1,0:T(8,128)(2,1)}) custom-call(bf16[2048,768]{1,0:T(8,128)(2,1)} %get-tuple-element.29.q_ref.k_ref.v_ref, bf16[2048,768]{1,0:T(8,128)(2,1)} %get-tuple-element.29.q_ref.k_ref.v_ref, bf16[2048,768]{1,0:T(8,128)(2,1)} %get-tuple-element.29.q_ref.k_ref.v_ref), custom_call_target="tpu_custom_call" | custom-call | flops 16106127360 | bytes 5242880 | tf_op jit(solution)/shard_map/attention_forward/pallas_call | solution.py:69
  131.3 1.0 copy-done.19
  132.3 10.7 %project.3 = (bf16[2048,1536]{1,0:T(8,128)(2,1)}, bf16[768,1536]{1,0:T(8,128)(2,1)}) custom-call(s32[2]{0:T(128)} %pad_add_fusion.at, bf16[2048,768]{1,0:T(8,128)(2,1)} %add_convert_fusion.1.n1, bf16[8,96,768]{2,1,0:T(8,128)(2,1)} %constant_dynamic-update-slice_fusion.5.mine, bf16[8,96,768]{2,1,0:T(8,128)(2,1)} %copy-done.19, f32[1,1536]{1,0:T(1,128)} %broadcast_in_dim.55.bias), custom_call_target="tpu_custom_call" | custom-call | flops 9663676416 | bytes 12582912 | tf_op jit(solution)/shard_map/project/pallas_call | solution.py:480
  143.0 27.5 %attention_forward.3 = (bf16[2048,512]{1,0:T(8,128)(2,1)}, bf16[2048,512]{1,0:T(8,128)(2,1)}) custom-call(bf16[2048,1536]{1,0:T(8,128)(2,1)} %get-tuple-element.31.q_ref.k_ref.v_ref, bf16[2048,1536]{1,0:T(8,128)(2,1)} %get-tuple-element.31.q_ref.k_ref.v_ref, bf16[2048,1536]{1,0:T(8,128)(2,1)} %get-tuple-element.31.q_ref.k_ref.v_ref), custom_call_target="tpu_custom_call" | custom-call | flops 32212254720 | bytes 10485760 | tf_op jit(solution)/shard_map/attention_forward/pallas_call | solution.py:69
  170.5 3.2 slice.250
  173.7 4.1 reshape.251
  177.8 1.8 copy.47
  179.6 3.2 slice.251
  182.9 4.1 reshape.253
  187.0 1.9 copy.48
  188.9 105.3 %feed_forward.1 = (bf16[2048,768]{1,0:T(8,128)(2,1)}, f32[2048,768]{1,0:T(8,128)}, bf16[2048,768]{1,0:T(8,128)(2,1)}, bf16[8,864,384]{2,1,0:T(8,128)(2,1)}, bf16...) custom-call(s32[1]{0:T(128)} %bitcast.at, bf16[2048,768]{1,0:T(8,128)(2,1)} %bitcast.84, ...), custom_call_target="tpu_custom_call" | custom-call | flops 115964116992 | bytes 53477376 | tf_op jit(solution)/shard_map/feed_forward/pallas_call | solution.py:356
  295.1 50.3 %attention_backward.3.refs_1_ = bf16[2048,1536]{1,0:T(8,128)(2,1)} custom-call(bf16[2048,1536]{1,0:T(8,128)(2,1)} %get-tuple-element.31.q_ref.k_ref.v_ref, bf16[2048,1536]{1,0:T(8,128)(2,1)} %get-tuple-element.31.q_ref.k_ref.v_ref, bf16[2048,1536]{1,0:T(8,128)(2,1)} %get-tuple-element.31.q_ref.k_ref.v_ref, bf16[2048,512]{1,0:T(8,128)(2,1)} %get-tuple-element.32.m1_any.o_ref, ...), custom_call_target="tpu_custom_call" | custom-call | flops 55834574848 | bytes 18874368 | tf_op jit(solution)/shard_map/attention_backward/pallas_call | solution.py:137
  345.4 6.2 %add_convert_fusion = bf16[8,864,384]{2,1,0:T(8,128)(2,1)} fusion(bf16[8,864,384]{2,1,0:T(8,128)(2,1)} %collective-permute-done.25, bf16[8,864,384]{2,1,0:T(8,128)(2,1)S(1)} %bitcast.88), kind=kLoop, calls=%fused_computation.2 | loop fusion | flops 10616832 | bytes 15925248 | tf_op jit(solution)/shard_map/convert_element_type | solution.py:554
  351.6 26.3 %attention_backward.2.refs_0_ = bf16[2048,768]{1,0:T(8,128)(2,1)} custom-call(bf16[2048,768]{1,0:T(8,128)(2,1)} %get-tuple-element.29.q_ref.k_ref.v_ref, bf16[2048,768]{1,0:T(8,128)(2,1)} %get-tuple-element.29.q_ref.k_ref.v_ref, bf16[2048,768]{1,0:T(8,128)(2,1)} %get-tuple-element.29.q_ref.k_ref.v_ref, bf16[2048,256]{1,0:T(8,128)(2,1)} %get-tuple-element.30.m0_any.o_ref, ...), custom_call_target="tpu_custom_call" | custom-call | flops 27917287424 | bytes 9437184 | tf_op jit(solution)/shard_map/attention_backward/pallas_call | solution.py:137
  377.8 17.5 %input_gradient.1 = (f32[2048,768]{1,0:T(8,128)}, f32[1,3840]{1,0:T(1,128)}) custom-call(bf16[2048,768]{1,0:T(8,128)(2,1)} %bitcast.85, f32[2048,768]{1,0:T(8,128)} %get-tuple-element.34.gh_ref, f32[1,768]{1,0:T(1,128)} %slice.208.gain_ref, bf16[2048,768]{1,0:T(8,128)(2,1)} %attention_backward.2.refs_0_, bf16[2048,1536]{1,0:T(8,128)(2,1)} %attention_backward.3.refs_1_, ...), custom_call_target="tpu_custom_call" | custom-call | flops 14495514624 | bytes 25165824 | tf_op jit(solution)/shard_map/input_gradient/pallas_call | solution.py:434
  399.5 4.6 convolution_convert_fusion.1
  404.2 8.8 %convolution_convert_fusion = bf16[768,1536]{1,0:T(8,128)(2,1)S(1)} fusion(bf16[2048,768]{1,0:T(8,128)(2,1)S(1)} %copy-done.3, bf16[2048,1536]{1,0:T(8,128)(2,1)} %attention_backward.3.refs_1_), kind=kOutput, calls=%fused_computation.9 | convolution fusion | flops 4833017856 | bytes 11796480 | tf_op jit(solution)/shard_map/dot_general | solution.py:22
  413.8 2.1 collective-permute-start.30
  415.9 1.5 collective-permute-start.31
  419.1 1.1 collective-permute-done.31
  420.2 1.7 collective-permute-start.32
  422.0 1.4 collective-permute-start.33
  423.7 0.9 collective-permute-done.33
  424.6 2.0 collective-permute-done.34
  427.9 1.4 add_convert_fusion.4
  430.0 1.9 add_convert_fusion.2
  432.6 10.8 %collective-permute-done.12 = bf16[4,96,384]{2,1,0:T(8,128)(2,1)S(1)} collective-permute-done((bf16[4,96,384]{2,1,0:T(8,128)(2,1)S(1)}, bf16[4,96,384]{2,1,0:T(8,128)(2,1)S(1)}, u32[]{:S(2)}, u32[]{:S(2)}) %collective-permute-start.12) | collective-permute-done | bytes 294944 | tf_op jit(solution)/shard_map/ppermute | solution.py:509
  443.6 3.5 collective-permute-start.15
  449.1 4.6 collective-permute-done.14
  453.8 3.9 collective-permute-done.19
  458.0 3.0 collective-permute-start.20
  460.9 2.2 collective-permute-start.22
  463.1 3.5 collective-permute-start.17
  466.7 1.8 collective-permute-start.26
  468.4 1.0 collective-permute-done.20
  469.4 3.5 collective-permute-done.21
  473.0 1.4 collective-permute-start.23
  474.5 12.5 %collective-permute-done.23 = bf16[96,768]{1,0:T(8,128)(2,1)S(1)} collective-permute-done((bf16[96,768]{1,0:T(8,128)(2,1)S(1)}, bf16[96,768]{1,0:T(8,128)(2,1)S(1)}, u32[]{:S(2)}, u32[]{:S(2)}) %collective-permute-start.23) | collective-permute-done | bytes 147488 | tf_op jit(solution)/shard_map/ppermute | solution.py:509
  489.7 1.1 copy.66
  493.0 1.5 copy.58
  495.4 1.1 maximum_bitcast_fusion
  (229 shorter events, 34.8 us)
Async XLA Ops:
  7.2 109.0 %all-gather.2.cloned.1.call-start = ((), (), s32[]{:S(2)}) async-start(), calls=%async_computation.1 | async-start | bytes 5971968 | tf_op jit(solution)/shard_map/all_gather | solution.py:635
  7.2 4.2 copy-start.10
  10.3 2.1 copy-start.16
  10.4 2.2 copy-start.15
  10.4 2.2 copy-start.17
  10.4 2.2 copy-start.18
  10.5 0.8 copy-start.8
  11.4 455.3 %reduce-scatter.4.cloned.1.call-start = ((), (), s32[]{:S(2)}) async-start(), calls=%async_computation.2 | async-start | bytes 5971968 | tf_op jit(solution)/shard_map/reduce_scatter | solution.py:670
  11.6 0.8 copy-start.6
  11.6 11.7 %copy-start = (s32[8]{0:T(128)S(1)}, s32[8]{0:T(128)}, u32[]{:S(2)}) copy-start(s32[8]{0:T(128)} %constant.116) | copy-start | bytes 100
  12.4 12.3 %copy-start.1 = (bf16[2,1024,768]{2,1,0:T(8,128)(2,1)S(1)}, bf16[2,1024,768]{2,1,0:T(8,128)(2,1)}, u32[]{:S(2)}) copy-start(bf16[2,1024,768]{2,1,0:T(8,128)(2,1)} %param.13) | copy-start | bytes 9437188
  12.5 12.2 %copy-start.20 = (s32[2]{0:T(128)S(1)}, s32[2]{0:T(128)}, u32[]{:S(2)}) copy-start(s32[2]{0:T(128)} %param.15) | copy-start | bytes 28
  13.4 16.5 %collective-permute-start = (bf16[1,112,384]{2,1,0:T(8,128)(2,1)}, bf16[1,112,384]{2,1,0:T(8,128)(2,1)}, u32[]{:S(2)}, u32[]{:S(2)}) collective-permute-start(bf16[1,112,384]{2,1,0:T(8,128)(2,1)} %maximum_bitcast_fusion.1), channel_id=1, source_target_pairs={{0,8},{4,12},{8,0},{12,4},{16,24},{20,28},{24,16},{28,20},{1,9},{5... | collective-permute-start | bytes 258056 | tf_op jit(solution)/shard_map/ppermute | solution.py:509
  15.5 14.6 %collective-permute-start.1 = (bf16[1,112,384]{2,1,0:T(8,128)(2,1)}, bf16[1,112,384]{2,1,0:T(8,128)(2,1)}, u32[]{:S(2)}, u32[]{:S(2)}) collective-permute-start(bf16[1,112,384]{2,1,0:T(8,128)(2,1)} %maximum_bitcast_fusion.1), channel_id=1, source_target_pairs={{0,16},{4,20},{8,24},{12,28},{16,0},{20,4},{24,8},{28,12},{1,17},{... | collective-permute-start | bytes 258056 | tf_op jit(solution)/shard_map/ppermute | solution.py:509
  17.8 12.3 %collective-permute-start.2 = (bf16[1,112,384]{2,1,0:T(8,128)(2,1)}, bf16[1,112,384]{2,1,0:T(8,128)(2,1)}, u32[]{:S(2)}, u32[]{:S(2)}) collective-permute-start(bf16[1,112,384]{2,1,0:T(8,128)(2,1)} %maximum_bitcast_fusion.1), channel_id=1, source_target_pairs={{0,24},{4,28},{8,16},{12,20},{16,8},{20,12},{24,0},{28,4},{1,25},{... | collective-permute-start | bytes 258056 | tf_op jit(solution)/shard_map/ppermute | solution.py:509
  19.8 17.3 %collective-permute-start.5 = (bf16[1,96,768]{2,1,0:T(8,128)(2,1)}, bf16[1,96,768]{2,1,0:T(8,128)(2,1)S(1)}, u32[]{:S(2)}, u32[]{:S(2)}) collective-permute-start(bf16[1,96,768]{2,1,0:T(8,128)(2,1)} %get-tuple-element.100), channel_id=1, source_target_pairs={{0,8},{4,12},{8,0},{12,4},{16,24},{20,28},{24,16},{28,20},{1,9},{5... | collective-permute-start | bytes 442376 | tf_op jit(solution)/shard_map/ppermute | solution.py:509
  20.1 20.0 %collective-permute-start.6 = (bf16[1,96,768]{2,1,0:T(8,128)(2,1)}, bf16[1,96,768]{2,1,0:T(8,128)(2,1)S(1)}, u32[]{:S(2)}, u32[]{:S(2)}) collective-permute-start(bf16[1,96,768]{2,1,0:T(8,128)(2,1)} %get-tuple-element.100), channel_id=1, source_target_pairs={{0,16},{4,20},{8,24},{12,28},{16,0},{20,4},{24,8},{28,12},{1,17},{... | collective-permute-start | bytes 442376 | tf_op jit(solution)/shard_map/ppermute | solution.py:509
  25.2 1.1 copy-start.14
  25.2 1.9 copy-start.2
  29.9 11.0 %collective-permute-start.7 = (bf16[1,96,768]{2,1,0:T(8,128)(2,1)}, bf16[1,96,768]{2,1,0:T(8,128)(2,1)S(1)}, u32[]{:S(2)}, u32[]{:S(2)}) collective-permute-start(bf16[1,96,768]{2,1,0:T(8,128)(2,1)} %get-tuple-element.100), channel_id=1, source_target_pairs={{0,24},{4,28},{8,16},{12,20},{16,8},{20,12},{24,0},{28,4},{1,25},{... | collective-permute-start | bytes 442376 | tf_op jit(solution)/shard_map/ppermute | solution.py:509
  31.2 14.7 %collective-permute-start.3 = (bf16[4,112,384]{2,1,0:T(8,128)(2,1)S(1)}, bf16[4,112,384]{2,1,0:T(8,128)(2,1)S(1)}, u32[]{:S(2)}, u32[]{:S(2)}) collective-permute-start(bf16[4,112,384]{2,1,0:T(8,128)(2,1)S(1)} %pad_maximum_fusion.2), channel_id=1, source_target_pairs={{0,4},{4,0},{8,12},{12,8},{16,20},{20,16},{24,28},{28,24},{1,5},{5... | collective-permute-start | bytes 1032200 | tf_op jit(solution)/shard_map/ppermute | solution.py:509
  42.7 21.9 %collective-permute-start.8 = (bf16[4,96,768]{2,1,0:T(8,128)(2,1)}, bf16[4,96,768]{2,1,0:T(8,128)(2,1)}, u32[]{:S(2)}, u32[]{:S(2)}) collective-permute-start(bf16[4,96,768]{2,1,0:T(8,128)(2,1)} %pad_maximum_fusion), channel_id=1, source_target_pairs={{0,4},{4,0},{8,12},{12,8},{16,20},{20,16},{24,28},{28,24},{1,5},{5... | collective-permute-start | bytes 1769480 | tf_op jit(solution)/shard_map/ppermute | solution.py:509
  47.6 18.9 %collective-permute-start.4 = (bf16[8,112,384]{2,1,0:T(8,128)(2,1)}, bf16[8,112,384]{2,1,0:T(8,128)(2,1)}, u32[]{:S(2)}, u32[]{:S(2)}) collective-permute-start(bf16[8,112,384]{2,1,0:T(8,128)(2,1)} %constant_dynamic-update-slice_fusion.mine), channel_id=1, source_target_pairs={{0,1},{1,0},{2,3},{3,2},{4,5},{5,4},{6,7},{7,6},{8,9},{9,8},{10,11... | collective-permute-start | bytes 2064392 | tf_op jit(solution)/shard_map/ppermute | solution.py:509
  66.5 64.8 %collective-permute-start.9 = (bf16[8,96,768]{2,1,0:T(8,128)(2,1)}, bf16[8,96,768]{2,1,0:T(8,128)(2,1)S(1)}, u32[]{:S(2)}, u32[]{:S(2)}) collective-permute-start(bf16[8,96,768]{2,1,0:T(8,128)(2,1)} %constant_dynamic-update-slice_fusion.5.mine), channel_id=1, source_target_pairs={{0,1},{1,0},{2,3},{3,2},{4,5},{5,4},{6,7},{7,6},{8,9},{9,8},{10,11... | collective-permute-start | bytes 3538952 | tf_op jit(solution)/shard_map/ppermute | solution.py:509
  116.2 63.4 %collective-permute-start.10 = (bf16[768,3456]{1,0:T(8,128)(2,1)}, bf16[768,3456]{1,0:T(8,128)(2,1)}, u32[]{:S(2)}, u32[]{:S(2)}) collective-permute-start(bf16[768,3456]{1,0:T(8,128)(2,1)} %all-gather.2.cloned.1.call-done.mine), channel_id=1, source_target_pairs={{0,1},{1,0},{2,3},{3,2},{4,5},{5,4},{6,7},{7,6},{8,9},{9,8},{10,11... | collective-permute-start | bytes 15925256 | tf_op jit(solution)/shard_map/ppermute | solution.py:509
  131.3 1.0 copy-start.19
  188.9 105.5 %copy-start.11 = (f32[1,8,96]{2,0,1:T(1,128)S(1)}, f32[1,8,96]{2,0,1:T(1,128)}, u32[]{:S(2)}) copy-start(f32[1,8,96]{2,0,1:T(1,128)} %get-tuple-element.124) | copy-start | bytes 9220
  294.2 51.2 %collective-permute-start.25 = (bf16[8,864,384]{2,1,0:T(8,128)(2,1)}, bf16[8,864,384]{2,1,0:T(8,128)(2,1)}, u32[]{:S(2)}, u32[]{:S(2)}) collective-permute-start(bf16[8,864,384]{2,1,0:T(8,128)(2,1)} %get-tuple-element.42), channel_id=1, source_target_pairs={{0,1},{1,0},{2,3},{3,2},{4,5},{5,4},{6,7},{7,6},{8,9},{9,8},{10,11... | collective-permute-start | bytes 15925256 | tf_op jit(solution)/shard_map/ppermute | solution.py:509
  295.1 50.3 %slice-start = ((s8[5308416]{0:T(1024)(128)(4,1)}), s8[4194304]{0:T(1024)(128)(4,1)S(1)}, s32[]{:S(2)}) async-start(s8[5308416]{0:T(1024)(128)(4,1)} %bitcast.87), calls=%async_computation.3 | async-start | bytes 8388608
  295.1 50.3 %slice-start.1 = ((s8[5308416]{0:T(1024)(128)(4,1)}), s8[1114112]{0:T(1024)(128)(4,1)S(1)}, s32[]{:S(2)}) async-start(s8[5308416]{0:T(1024)(128)(4,1)} %bitcast.87), calls=%async_computation.4 | async-start | bytes 2228224
  377.8 19.2 %copy-start.12 = (f32[4,768]{1,0:T(4,128)S(1)}, f32[4,768]{1,0:T(4,128)}, u32[]{:S(2)}) copy-start(f32[4,768]{1,0:T(4,128)} %get-tuple-element.44) | copy-start | bytes 36868
  377.8 20.2 %copy-start.13 = (f32[1,3072]{1,0:T(1,128)S(1)}, f32[1,3072]{1,0:T(1,128)}, u32[]{:S(2)}) copy-start(f32[1,3072]{1,0:T(1,128)} %get-tuple-element.45) | copy-start | bytes 36868
  377.8 21.7 %copy-start.3 = (bf16[2048,768]{1,0:T(8,128)(2,1)S(1)}, bf16[2048,768]{1,0:T(8,128)(2,1)}, u32[]{:S(2)}) copy-start(bf16[2048,768]{1,0:T(8,128)(2,1)} %add_convert_fusion.1.n1) | copy-start | bytes 9437188
  398.9 14.8 %collective-permute-start.28 = (f32[4,12,96]{2,1,0:T(8,128)S(1)}, f32[4,12,96]{2,1,0:T(8,128)S(1)}, u32[]{:S(2)}, u32[]{:S(2)}) collective-permute-start(f32[4,12,96]{2,1,0:T(8,128)S(1)} %dynamic-slice_bitcast_fusion.3), channel_id=1, source_target_pairs={{0,4},{4,0},{8,12},{12,8},{16,20},{20,16},{24,28},{28,24},{1,5},{5... | collective-permute-start | bytes 55304 | tf_op jit(solution)/shard_map/ppermute | solution.py:509
  404.2 13.2 %copy-start.7 = (bf16[768,768]{1,0:T(8,128)(2,1)}, bf16[768,768]{1,0:T(8,128)(2,1)S(1)}, u32[]{:S(2)}) copy-start(bf16[768,768]{1,0:T(8,128)(2,1)S(1)} %convolution_convert_fusion.1) | copy-start | bytes 3538948
  413.0 5.3 %copy-start.4 = (bf16[768,1536]{1,0:T(8,128)(2,1)}, bf16[768,1536]{1,0:T(8,128)(2,1)S(1)}, u32[]{:S(2)}) copy-start(bf16[768,1536]{1,0:T(8,128)(2,1)S(1)} %convolution_convert_fusion) | copy-start | bytes 7077892
  413.1 16.9 %collective-permute-start.18 = (bf16[8,96,768]{2,1,0:T(8,128)(2,1)S(1)}, bf16[8,96,768]{2,1,0:T(8,128)(2,1)}, u32[]{:S(2)}, u32[]{:S(2)}) collective-permute-start(bf16[8,96,768]{2,1,0:T(8,128)(2,1)S(1)} %constant_dynamic-slice_fusion.6), channel_id=1, source_target_pairs={{0,1},{1,0},{2,3},{3,2},{4,5},{5,4},{6,7},{7,6},{8,9},{9,8},{10,11... | collective-permute-start | bytes 3538952 | tf_op jit(solution)/shard_map/ppermute | solution.py:509
  413.8 5.4 %collective-permute-start.29 = (f32[1,12,96]{2,1,0:T(8,128)S(1)}, f32[1,12,96]{2,1,0:T(8,128)S(1)}, u32[]{:S(2)}, u32[]{:S(2)}) collective-permute-start(f32[1,12,96]{2,1,0:T(8,128)S(1)} %get-tuple-element.121), channel_id=1, source_target_pairs={{0,8},{4,12},{8,0},{12,4},{16,24},{20,28},{24,16},{28,20},{1,9},{5... | collective-permute-start | bytes 13832 | tf_op jit(solution)/shard_map/ppermute | solution.py:509
  413.8 5.3 %collective-permute-start.30 = (f32[1,12,96]{2,1,0:T(8,128)S(1)}, f32[1,12,96]{2,1,0:T(8,128)S(1)}, u32[]{:S(2)}, u32[]{:S(2)}) collective-permute-start(f32[1,12,96]{2,1,0:T(8,128)S(1)} %get-tuple-element.123), channel_id=1, source_target_pairs={{0,16},{4,20},{8,24},{12,28},{16,0},{20,4},{24,8},{28,12},{1,17},{... | collective-permute-start | bytes 13832 | tf_op jit(solution)/shard_map/ppermute | solution.py:509
  415.9 4.3 collective-permute-start.31
  418.3 9.6 %collective-permute-start.11 = (bf16[8,96,384]{2,1,0:T(8,128)(2,1)}, bf16[8,96,384]{2,1,0:T(8,128)(2,1)}, u32[]{:S(2)}, u32[]{:S(2)}) collective-permute-start(bf16[8,96,384]{2,1,0:T(8,128)(2,1)} %constant_dynamic-slice_fusion.10), channel_id=1, source_target_pairs={{0,1},{1,0},{2,3},{3,2},{4,5},{5,4},{6,7},{7,6},{8,9},{9,8},{10,11... | collective-permute-start | bytes 1769480 | tf_op jit(solution)/shard_map/ppermute | solution.py:509
  419.1 10.9 %copy-start.5 = (bf16[768,1536]{1,0:T(8,128)(2,1)S(1)}, bf16[768,1536]{1,0:T(8,128)(2,1)}, u32[]{:S(2)}) copy-start(bf16[768,1536]{1,0:T(8,128)(2,1)} %copy-done.4) | copy-start | bytes 7077892
  420.2 3.4 collective-permute-start.32
  422.0 2.6 collective-permute-start.33
  423.4 3.2 collective-permute-start.34
  429.3 14.0 %collective-permute-start.12 = (bf16[4,96,384]{2,1,0:T(8,128)(2,1)S(1)}, bf16[4,96,384]{2,1,0:T(8,128)(2,1)S(1)}, u32[]{:S(2)}, u32[]{:S(2)}) collective-permute-start(bf16[4,96,384]{2,1,0:T(8,128)(2,1)S(1)} %dynamic-slice_bitcast_fusion.1), channel_id=1, source_target_pairs={{0,4},{4,0},{8,12},{12,8},{16,20},{20,16},{24,28},{28,24},{1,5},{5... | collective-permute-start | bytes 884744 | tf_op jit(solution)/shard_map/ppermute | solution.py:509
  432.0 25.8 %collective-permute-start.19 = (bf16[4,96,768]{2,1,0:T(8,128)(2,1)S(1)}, bf16[4,96,768]{2,1,0:T(8,128)(2,1)S(1)}, u32[]{:S(2)}, u32[]{:S(2)}) collective-permute-start(bf16[4,96,768]{2,1,0:T(8,128)(2,1)S(1)} %dynamic-slice_bitcast_fusion), channel_id=1, source_target_pairs={{0,4},{4,0},{8,12},{12,8},{16,20},{20,16},{24,28},{28,24},{1,5},{5... | collective-permute-start | bytes 1769480 | tf_op jit(solution)/shard_map/ppermute | solution.py:509
  443.5 5.6 %collective-permute-start.13 = (bf16[1,96,384]{2,1,0:T(8,128)(2,1)S(1)}, bf16[1,96,384]{2,1,0:T(8,128)(2,1)S(1)}, u32[]{:S(2)}, u32[]{:S(2)}) collective-permute-start(bf16[1,96,384]{2,1,0:T(8,128)(2,1)S(1)} %get-tuple-element.114), channel_id=1, source_target_pairs={{0,8},{4,12},{8,0},{12,4},{16,24},{20,28},{24,16},{28,20},{1,9},{5... | collective-permute-start | bytes 221192 | tf_op jit(solution)/shard_map/ppermute | solution.py:509
  443.6 10.1 %collective-permute-start.14 = (bf16[1,96,384]{2,1,0:T(8,128)(2,1)S(1)}, bf16[1,96,384]{2,1,0:T(8,128)(2,1)S(1)}, u32[]{:S(2)}, u32[]{:S(2)}) collective-permute-start(bf16[1,96,384]{2,1,0:T(8,128)(2,1)S(1)} %get-tuple-element.116), channel_id=1, source_target_pairs={{0,16},{4,20},{8,24},{12,28},{16,0},{20,4},{24,8},{28,12},{1,17},{... | collective-permute-start | bytes 221192 | tf_op jit(solution)/shard_map/ppermute | solution.py:509
  443.6 10.1 %collective-permute-start.15 = (bf16[1,96,384]{2,1,0:T(8,128)(2,1)S(1)}, bf16[1,96,384]{2,1,0:T(8,128)(2,1)S(1)}, u32[]{:S(2)}, u32[]{:S(2)}) collective-permute-start(bf16[1,96,384]{2,1,0:T(8,128)(2,1)S(1)} %get-tuple-element.115), channel_id=1, source_target_pairs={{0,24},{4,28},{8,16},{12,20},{16,8},{20,12},{24,0},{28,4},{1,25},{... | collective-permute-start | bytes 221192 | tf_op jit(solution)/shard_map/ppermute | solution.py:509
  453.7 9.3 %collective-permute-start.16 = (bf16[96,384]{1,0:T(8,128)(2,1)S(1)}, bf16[96,384]{1,0:T(8,128)(2,1)S(1)}, u32[]{:S(2)}, u32[]{:S(2)}) collective-permute-start(bf16[96,384]{1,0:T(8,128)(2,1)S(1)} %fusion.5), channel_id=1, source_target_pairs={{0,2},{1,3},{2,0},{3,1},{4,6},{5,7},{6,4},{7,5},{8,10},{9,11},{10,... | collective-permute-start | bytes 221192 | tf_op jit(solution)/shard_map/ppermute | solution.py:509
  458.0 11.5 %collective-permute-start.20 = (bf16[1,96,768]{2,1,0:T(8,128)(2,1)S(1)}, bf16[1,96,768]{2,1,0:T(8,128)(2,1)S(1)}, u32[]{:S(2)}, u32[]{:S(2)}) collective-permute-start(bf16[1,96,768]{2,1,0:T(8,128)(2,1)S(1)} %get-tuple-element.107), channel_id=1, source_target_pairs={{0,8},{4,12},{8,0},{12,4},{16,24},{20,28},{24,16},{28,20},{1,9},{5... | collective-permute-start | bytes 442376 | tf_op jit(solution)/shard_map/ppermute | solution.py:509
  460.9 12.0 %collective-permute-start.21 = (bf16[1,96,768]{2,1,0:T(8,128)(2,1)S(1)}, bf16[1,96,768]{2,1,0:T(8,128)(2,1)S(1)}, u32[]{:S(2)}, u32[]{:S(2)}) collective-permute-start(bf16[1,96,768]{2,1,0:T(8,128)(2,1)S(1)} %get-tuple-element.109), channel_id=1, source_target_pairs={{0,16},{4,20},{8,24},{12,28},{16,0},{20,4},{24,8},{28,12},{1,17},{... | collective-permute-start | bytes 442376 | tf_op jit(solution)/shard_map/ppermute | solution.py:509
  460.9 12.0 %collective-permute-start.22 = (bf16[1,96,768]{2,1,0:T(8,128)(2,1)S(1)}, bf16[1,96,768]{2,1,0:T(8,128)(2,1)S(1)}, u32[]{:S(2)}, u32[]{:S(2)}) collective-permute-start(bf16[1,96,768]{2,1,0:T(8,128)(2,1)S(1)} %get-tuple-element.108), channel_id=1, source_target_pairs={{0,24},{4,28},{8,16},{12,20},{16,8},{20,12},{24,0},{28,4},{1,25},{... | collective-permute-start | bytes 442376 | tf_op jit(solution)/shard_map/ppermute | solution.py:509
  463.1 11.3 %collective-permute-start.17 = (bf16[96,384]{1,0:T(8,128)(2,1)S(1)}, bf16[96,384]{1,0:T(8,128)(2,1)S(1)}, u32[]{:S(2)}, u32[]{:S(2)}) collective-permute-start(bf16[96,384]{1,0:T(8,128)(2,1)S(1)} %add_convert_fusion.7), channel_id=1, source_target_pairs={{0,1},{1,0},{2,3},{3,2},{4,5},{5,4},{6,7},{7,6},{8,9},{9,8},{10,11... | collective-permute-start | bytes 221192 | tf_op jit(solution)/shard_map/ppermute | solution.py:509
  466.7 21.1 %copy-start.9 = (bf16[864,384]{1,0:T(8,128)(2,1)S(1)}, bf16[864,384]{1,0:T(8,128)(2,1)}, u32[]{:S(2)}) copy-start(bf16[864,384]{1,0:T(8,128)(2,1)} %reduce-scatter.4.cloned.1.call-done) | copy-start | bytes 1990660
  466.7 21.5 %collective-permute-start.26 = (bf16[864,384]{1,0:T(8,128)(2,1)}, bf16[864,384]{1,0:T(8,128)(2,1)S(1)}, u32[]{:S(2)}, u32[]{:S(2)}) collective-permute-start(bf16[864,384]{1,0:T(8,128)(2,1)} %reduce-scatter.4.cloned.1.call-done), channel_id=1, source_target_pairs={{0,2},{1,3},{2,0},{3,1},{4,6},{5,7},{6,4},{7,5},{8,10},{9,11},{10,... | collective-permute-start | bytes 1990664 | tf_op jit(solution)/shard_map/ppermute | solution.py:509
  473.0 14.0 %collective-permute-start.23 = (bf16[96,768]{1,0:T(8,128)(2,1)S(1)}, bf16[96,768]{1,0:T(8,128)(2,1)S(1)}, u32[]{:S(2)}, u32[]{:S(2)}) collective-permute-start(bf16[96,768]{1,0:T(8,128)(2,1)S(1)} %fusion.4), channel_id=1, source_target_pairs={{0,2},{1,3},{2,0},{3,1},{4,6},{5,7},{6,4},{7,5},{8,10},{9,11},{10,... | collective-permute-start | bytes 442376 | tf_op jit(solution)/shard_map/ppermute | solution.py:509
  487.1 2.1 collective-permute-start.24
  489.0 2.2 collective-permute-start.27
Sparse Core Ops, SparseCore 0:
  11.5 104.6 all-gather.1
  351.7 113.7 reduce-scatter.3

commit v3 on v2

v3 whole, which is shorter than its diff:
```python
import functools

import jax
import jax.numpy as jnp
from jax import lax
from jax.experimental import pallas as pl
from jax.experimental.pallas import tpu as pltpu
from jax.sharding import PartitionSpec as P

HEADS = 12
F32 = jnp.float32
BF = jnp.bfloat16
EPS = 1e-05
ROOT = 0.7978845608028654
CUBIC = 0.044715
NN = (((1,), (0,)), ((), ()))
NT = (((1,), (1,)), ((), ()))
TN = (((0,), (0,)), ((), ()))


def dot(a, b, dims):
    return lax.dot_general(a, b, dims, preferred_element_type=F32)


def spread(x, lane):
    hi = x.astype(BF).astype(F32)
    rest = x - hi
    mid = rest.astype(BF).astype(F32)
    at = lane & 63
    zero = jnp.zeros_like(x)
    picked = jnp.where(at == 0, hi, jnp.where(at == 1, mid, jnp.where(at == 2, rest - mid, zero)))
    return picked.astype(BF)

def fwd_kernel(bq, x_ref, o_ref, l_ref, *_):
    length = x_ref.shape[0]
    lane = lax.broadcasted_iota(jnp.int32, (length, 128), 1)
    left = lane < 64
    lq = lax.broadcasted_iota(jnp.int32, (bq, 128), 1)
    leftq = lq < 64
    k = x_ref[:, 128:256]
    v = x_ref[:, 256:384].astype(F32)
    ones = jnp.ones_like(v)
    va = jnp.where(left, v, ones).astype(BF)
    vb = jnp.where(left, ones, v).astype(BF)
    for i in range(length // bq):
        q = x_ref[i * bq : (i + 1) * bq, :128].astype(F32) * 0.125
        zero = jnp.zeros_like(q)
        qa = jnp.where(leftq, q, zero).astype(BF)
        qb = jnp.where(leftq, zero, q).astype(BF)
        outs, peaks = [], []
        for qq, vv in ((qa, va), (qb, vb)):
            s = dot(qq, k, NT)
            m = jnp.max(s, axis=1, keepdims=True)
            p = jnp.exp(s - m).astype(BF)
            outs.append(dot(p, vv, NN))
            peaks.append(m)
        oa, ob = outs
        num = jnp.where(leftq, oa, ob)
        den = jnp.where(leftq, ob, oa)
        o_ref[i * bq : (i + 1) * bq, :] = (num / pltpu.roll(den, 64, 1)).astype(BF)
        lse = jnp.where(leftq, peaks[1], peaks[0]) + jnp.log(den)
        l_ref[i * bq : (i + 1) * bq, :] = spread(lse, lq)


def attn_fwd(qkv, first, pairs, rows, deps=(), bq=512):
    n = qkv.shape[0]
    length = n // rows
    width = pairs * 128
    out = pl.BlockSpec((length, 128), lambda s, p: (s, p))

    def kernel(x_ref, *refs):
        fwd_kernel(bq, x_ref, *refs[len(deps) :])

    return pl.pallas_call(
        kernel,
        grid=(rows, pairs),
        in_specs=[pl.BlockSpec((length, 384), lambda s, p: (s, first + p))]
        + [pl.BlockSpec(memory_space=pl.ANY)] * len(deps),
        out_specs=[out, out],
        out_shape=[jax.ShapeDtypeStruct((n, width), BF)] * 2,
        compiler_params=pltpu.CompilerParams(vmem_limit_bytes=56 << 20),
        cost_estimate=pl.CostEstimate(
            flops=30 * n * length * width,
            bytes_accessed=n * width * 10,
            transcendentals=n * length * width // 64,
        ),
        name="attention_forward",
    )(qkv, *deps)


def bwd_kernel(bq, at, x_ref, o_ref, l_ref, g_ref, n1t_ref, out_ref, keep_ref, send_ref, sum_ref, ak, av, dw):
    length = x_ref.shape[0]
    p, s, last = pl.program_id(0), pl.program_id(1), pl.num_programs(1) - 1
    lane = lax.broadcasted_iota(jnp.int32, (length, 128), 1)
    left = lane < 64
    lq = lax.broadcasted_iota(jnp.int32, (bq, 128), 1)
    leftq = lq < 64
    k = x_ref[:, 128:256].astype(F32)
    v = x_ref[:, 256:384].astype(F32)
    tail = jnp.where((lane & 63) < 3, -1.0, 0.0).astype(F32)
    zero = jnp.zeros_like(k)
    kx = (jnp.where(left, k, tail).astype(BF), jnp.where(left, tail, k).astype(BF))
    km = (jnp.where(left, k, zero).astype(BF), jnp.where(left, zero, k).astype(BF))
    vx = (jnp.where(left, v, tail).astype(BF), jnp.where(left, tail, v).astype(BF))
    for i in range(length // bq):
        here = slice(i * bq, (i + 1) * bq)
        q = x_ref[here, :128].astype(F32) * 0.125
        l = l_ref[here, :].astype(F32)
        g = g_ref[here, :].astype(F32)
        zq = jnp.zeros_like(q)
        prod = g * o_ref[here, :].astype(F32)
        da = jnp.sum(jnp.where(leftq, prod, zq), axis=1, keepdims=True)
        db = jnp.sum(jnp.where(leftq, zq, prod), axis=1, keepdims=True)
        d = spread(jnp.where(leftq, db, da), lq).astype(F32)
        qx = (jnp.where(leftq, q, l).astype(BF), jnp.where(leftq, l, q).astype(BF))
        qm = (jnp.where(leftq, q, zq).astype(BF), jnp.where(leftq, zq, q).astype(BF))
        gx = (jnp.where(leftq, g, d).astype(BF), jnp.where(leftq, d, g).astype(BF))
        gm = (jnp.where(leftq, g, zq).astype(BF), jnp.where(leftq, zq, g).astype(BF))
        gq = gk = gv = None
        for h in range(2):
            pr = jnp.exp(dot(kx[h], qx[h], NT))
            ds = (pr * dot(vx[h], gx[h], NT)).astype(BF)
            tv = dot(pr.astype(BF), gm[h], NN)
            tk = dot(ds, qm[h], NN)
            tq = dot(ds, km[h], TN)
            gq = tq if gq is None else gq + tq
            gk = tk if gk is None else gk + tk
            gv = tv if gv is None else gv + tv
        out_ref[here, :128] = (gq * 0.125).astype(BF)
        if i == 0:
            ak[...] = gk
            av[...] = gv
        else:
            ak[...] += gk
            av[...] += gv
    out_ref[:, 128:256] = ak[...].astype(BF)
    out_ref[:, 256:384] = av[...].astype(BF)
    got = out_ref[...]
    grad = dot(n1t_ref[...], got, NN)
    sums = jnp.sum(got.astype(F32), axis=0, keepdims=True)

    @pl.when(s == 0)
    def _():
        dw[...] = grad
        sum_ref[...] = jnp.broadcast_to(sums, (8, 384))

    @pl.when((s > 0) & (s < last))
    def _():
        dw[...] += grad

    @pl.when(s > 0)
    def _():
        sum_ref[...] += jnp.broadcast_to(sums, (8, 384))

    @pl.when((s == last) & (p == at[0]))
    def _():
        keep_ref[...] = (dw[...] + grad).astype(BF)

    @pl.when((s == last) & (p != at[0]))
    def _():
        send_ref[...] = (dw[...] + grad).astype(BF)


def attn_bwd(core, qkv, first, mixed, lse, gmixed, at_g, n1t, rows, deps=(), bq=256):
    n = qkv.shape[0]
    length = n // rows
    D = n1t.shape[0]
    pairs = 2
    block = pl.BlockSpec((length, 128), lambda p, s: (s, p))
    whole = pl.BlockSpec((D, 384), lambda p, s: (0, 0))

    def kernel(at, x, o, l, g, t, *refs):
        bwd_kernel(bq, at, x, o, l, g, t, *refs[len(deps) :])

    assert rows > 1
    return pl.pallas_call(
        kernel,
        grid=(pairs, rows),
        in_specs=[
            pl.BlockSpec(memory_space=pltpu.SMEM),
            pl.BlockSpec((length, 384), lambda p, s: (s, first + p)),
            block,
            block,
            pl.BlockSpec((length, 128), lambda p, s: (s, at_g + p)),
            pl.BlockSpec((D, length), lambda p, s: (0, s)),
        ]
        + [pl.BlockSpec(memory_space=pl.ANY)] * len(deps),
        out_specs=[
            pl.BlockSpec((length, 384), lambda p, s: (s, p)),
            whole,
            whole,
            pl.BlockSpec((8, 384), lambda p, s: (0, p)),
        ],
        out_shape=[
            jax.ShapeDtypeStruct((n, pairs * 384), BF),
            jax.ShapeDtypeStruct((D, 384), BF),
            jax.ShapeDtypeStruct((D, 384), BF),
            jax.ShapeDtypeStruct((8, pairs * 384), F32),
        ],
        scratch_shapes=[pltpu.VMEM((length, 128), F32)] * 2 + [pltpu.VMEM((D, 384), F32)],
        compiler_params=pltpu.CompilerParams(vmem_limit_bytes=56 << 20),
        cost_estimate=pl.CostEstimate(
            flops=56 * n * length * pairs * 128,
            bytes_accessed=n * pairs * 128 * 18,
            transcendentals=n * length * pairs * 2,
        ),
        name="attention_backward",
    )(core, qkv, mixed, lse, gmixed, n1t, *deps)


def tie_kernel(a, b, out):
    pass


def tie(x, after):
    anywhere = pl.BlockSpec(memory_space=pl.ANY)
    return pl.pallas_call(
        tie_kernel,
        in_specs=[anywhere] * 2,
        out_specs=anywhere,
        out_shape=jax.ShapeDtypeStruct(x.shape, x.dtype),
        input_output_aliases={0: 0},
        name="tie",
    )(x, after)


def mid_kernel(T, direct, at, x_any, m0_any, m1_any, m2_any, g, mine, other, back_mine, back_other, vec_ref, fb_ref,
               out_ref, gh_ref, gm_ref, keep, send, keep_b, send_b, sum_ref, fs_ref,
               wo, wi_s, wb_s, gi_s, gb_s, n2, n2t, gt, xh, acc, ai, ab, sem, wsem, gsem):
    f, nf = pl.program_id(0), pl.num_programs(0)
    core = at[0]
    n, D = n2.shape
    F = wi_s.shape[2]
    blocks, half, r = n // T, D // 2, D // 8
    at_back = mine.shape[1] - (half // r) * half
    x_ref, m_ref, gtw = out_ref, gm_ref, gh_ref

    left = pl.ds(pl.multiple_of(core * half, 128), half)
    right = pl.ds(pl.multiple_of((1 - core) * half, 128), half)

    def back(step, slot):
        if not direct:
            rows = pl.ds(pl.multiple_of(step * F, 128), F)
            return [(back_mine.at[rows, :], wb_s.at[slot, :, left]), (back_other.at[rows, :], wb_s.at[slot, :, right])]
        out = []
        for k in range(F // half):
            rows = pl.ds(pl.multiple_of((step * (F // half) + k) * r, r), r)
            for t in range(half // r):
                cols = pl.ds(at_back + t * half, half)
                to = slice(k * half + t * r, k * half + (t + 1) * r)
                out.append((mine.at[rows, cols], wb_s.at[slot, to, left]))
                out.append((other.at[rows, cols], wb_s.at[slot, to, right]))
        return out

    def inner(step):
        return pl.ds(pl.multiple_of(half + lax.rem(step, nf // 2) * F, 128), F)

    def fetch(step, slot):
        @pl.when(step // (nf // 2) == core)
        def _():
            pltpu.make_async_copy(mine.at[:, inner(step)], wi_s.at[slot], wsem.at[slot, 0]).start()

        @pl.when(step // (nf // 2) != core)
        def _():
            pltpu.make_async_copy(other.at[:, inner(step)], wi_s.at[slot], wsem.at[slot, 0]).start()

        for i, (src, to) in enumerate(back(step, slot)):
            pltpu.make_async_copy(src, to, wsem.at[slot, 1 + i]).start()

    def grads(step):
        part, local = step // (nf // 2), lax.rem(step, nf // 2)
        out = []
        per = F // half
        for w in range(8):
            for k in range(per):
                row = pl.multiple_of(r + (local * per + k) * r, r)
                src = gi_s.at[w * r : (w + 1) * r, k * half : (k + 1) * half]
                out.append((part, (keep, send), w, pl.ds(row, r), src))
        for k in range(per):
            for h in range(2):
                src = gb_s.at[h * half : (h + 1) * half, k * half : (k + 1) * half]
                out.append((h, (keep_b, send_b), step * per + k, pl.ds(0, half), src))
        return out

    def store(copies):
        for i, (part, to, w, rows, src) in enumerate(copies):
            @pl.when(part == core)
            def _():
                pltpu.make_async_copy(src, to[0].at[w, rows, :], gsem.at[i]).start()

            @pl.when(part != core)
            def _():
                pltpu.make_async_copy(src, to[1].at[w, rows, :], gsem.at[i]).start()

    def settle(copies):
        for i, (part, to, w, rows, src) in enumerate(copies):
            pltpu.make_async_copy(src, to[0].at[w, rows, :], gsem.at[i]).wait()

    slot = lax.rem(f, 2)

    @pl.when(f == 0)
    def _():
        cx = pltpu.make_async_copy(x_any, x_ref, sem.at[0])
        cx.start()
        start = 0
        cm = []
        for j, a in enumerate((m0_any, m1_any, m2_any)):
            w = a.shape[1]
            cm.append(pltpu.make_async_copy(a, m_ref.at[:, pl.ds(start, w)], sem.at[1 + j]))
            start += w
        cm.append(pltpu.make_async_copy(mine.at[:, pl.ds(0, half)], wo.at[:, left], sem.at[4]))
        cm.append(pltpu.make_async_copy(other.at[:, pl.ds(0, half)], wo.at[:, right], sem.at[5]))
        for copy in cm:
            copy.start()
        fetch(0, 0)
        for copy in [cx] + cm:
            copy.wait()

        @pl.loop(0, blocks)
        def _(i):
            at_t = pl.ds(pl.multiple_of(i * T, T), T)
            hidden = x_ref[at_t, :].astype(F32) + dot(m_ref[at_t, :], wo[...], NN) + vec_ref[2:3, :]
            c = hidden - jnp.mean(hidden, axis=1, keepdims=True)
            inv = lax.rsqrt(jnp.mean(c * c, axis=1, keepdims=True) + EPS)
            nn = (c * inv * vec_ref[0:1, :] + vec_ref[1:2, :]).astype(BF)
            acc[at_t, :] = hidden + vec_ref[3:4, :]
            xh[at_t, :] = c
            n2[at_t, :] = nn
            n2t[:, at_t] = nn.T
            gt[:, at_t] = g[at_t, :].T

    @pl.when(f < nf - 1)
    def _():
        fetch(f + 1, 1 - slot)

    pltpu.make_async_copy(mine.at[:, inner(f)], wi_s.at[slot], wsem.at[slot, 0]).wait()
    for i, (src, to) in enumerate(back(f, slot)):
        pltpu.make_async_copy(src, to, wsem.at[slot, 1 + i]).wait()
    wi_ref, wb_ref = wi_s.at[slot], wb_s.at[slot]
    fs = None
    for i in range(blocks):
        at_t = pl.ds(i * T, T)
        pre = dot(n2[at_t, :], wi_ref[...], NN) + fb_ref[...]
        ga = dot(g[at_t, :], wb_ref[...], NT)
        sq = pre * pre
        t = jnp.tanh(pre * (ROOT + (ROOT * CUBIC) * sq))
        part = 0.5 * pre
        act = (part + part * t).astype(BF)
        slope = (0.5 + 0.5 * t) + part * (1.0 - t * t) * (ROOT + (3 * ROOT * CUBIC) * sq)
        gp = (ga * slope).astype(BF)
        s = jnp.sum(gp.astype(F32), axis=0, keepdims=True)
        fs = s if fs is None else fs + s
        a = dot(n2t[:, i * T : (i + 1) * T], gp, NN)
        b = dot(gt[:, i * T : (i + 1) * T], act, NN)
        if i == 0:
            ai[...] = a
            ab[...] = b
        elif i < blocks - 1:
            ai[...] += a
            ab[...] += b
        else:
            @pl.when(f > 0)
            def _():
                settle(grads(f - 1))

            gi_s[...] = (ai[...] + a).astype(BF)
            gb_s[...] = (ab[...] + b).astype(BF)
            store(grads(f))
        acc[at_t, :] += dot(act, wb_ref[...], NN)
        gtwo = dot(gp, wi_ref[...], NT)

        @pl.when(f == 0)
        def _():
            gtw[at_t, :] = gtwo

        @pl.when(f > 0)
        def _():
            gtw[at_t, :] += gtwo

    fs_ref[...] = fs

    @pl.when(f == nf - 1)
    def _():
        sum_ref[...] = jnp.zeros_like(sum_ref)
        ai[...] = jnp.zeros_like(ai)

        @pl.loop(0, blocks)
        def _(i):
            at_t = pl.ds(pl.multiple_of(i * T, T), T)
            out_ref[at_t, :] = acc[at_t, :].astype(BF)
            gtwo, c = gtw[at_t, :], xh[at_t, :]
            inv = lax.rsqrt(jnp.mean(c * c, axis=1, keepdims=True) + EPS)
            xhat = c * inv
            e = gtwo * vec_ref[0:1, :]
            m1 = jnp.mean(e, axis=1, keepdims=True)
            m2 = jnp.mean(e * xhat, axis=1, keepdims=True)
            gg = g[at_t, :].astype(F32)
            gh = gg + inv * (e - m1 - xhat * m2)
            gh_ref[at_t, :] = gh
            ga = gh.astype(BF)
            ai[...] += dot(m_ref[at_t, :], ga, TN)
            gm_ref[at_t, :] = dot(ga, wo[...], NT).astype(BF)
            rows = (gtwo * xhat, gtwo, ga.astype(F32), gg)
            sum_ref[...] += jnp.concatenate([jnp.sum(v, axis=0, keepdims=True) for v in rows], axis=0)

        settle(grads(f))
        gi_s[...] = ai[...].astype(BF)
        last_ones = [
            (h, (keep, send), w, pl.ds(0, r), gi_s.at[w * r : (w + 1) * r, h * half : (h + 1) * half])
            for w in range(8)
            for h in range(2)
        ]
        store(last_ones)
        settle(last_ones)


def middle(core, x, mixed, g, mine, other, back_mine, back_other, direct, vec, fb, F=768, T=256):
    n, D = x.shape
    FF = fb.shape[1]
    one = pl.Buffered(1)

    def full(shape):
        return pl.BlockSpec(shape, lambda f: (0, 0), pipeline_mode=one)

    anywhere = pl.BlockSpec(memory_space=pl.ANY)
    packed = (8, D // 8 + FF // 8, D // 2)
    packed_b = (8, D // 2, FF // 8)
    return pl.pallas_call(
        functools.partial(mid_kernel, T, direct),
        grid=(FF // F,),
        in_specs=[pl.BlockSpec(memory_space=pltpu.SMEM)]
        + [anywhere] * 4
        + [full((n, D))]
        + [anywhere] * 4
        + [full((4, D)), pl.BlockSpec((1, F), lambda f: (0, f))],
        out_specs=[full((n, D)), full((n, D)), full((n, D))] + [anywhere] * 4
        + [full((4, D)), pl.BlockSpec((1, F), lambda f: (0, f))],
        out_shape=[
            jax.ShapeDtypeStruct((n, D), BF),
            jax.ShapeDtypeStruct((n, D), F32),
            jax.ShapeDtypeStruct((n, D), BF),
            jax.ShapeDtypeStruct(packed, BF),
            jax.ShapeDtypeStruct(packed, BF),
            jax.ShapeDtypeStruct(packed_b, BF),
            jax.ShapeDtypeStruct(packed_b, BF),
            jax.ShapeDtypeStruct((4, D), F32),
            jax.ShapeDtypeStruct((1, FF), F32),
        ],
        scratch_shapes=[
            pltpu.VMEM((D, D), BF),
            pltpu.VMEM((2, D, F), BF),
            pltpu.VMEM((2, F, D), BF),
            pltpu.VMEM((D, F), BF),
            pltpu.VMEM((D, F), BF),
            pltpu.VMEM((n, D), BF),
            pltpu.VMEM((D, n), BF),
            pltpu.VMEM((D, n), BF),
            pltpu.VMEM((n, D), F32),
            pltpu.VMEM((n, D), F32),
            pltpu.VMEM((D, F), F32),
            pltpu.VMEM((D, F), F32),
            pltpu.SemaphoreType.DMA((6,)),
            pltpu.SemaphoreType.DMA((2, 17)),
            pltpu.SemaphoreType.DMA((20,)),
        ],
        compiler_params=pltpu.CompilerParams(vmem_limit_bytes=63 << 20),
        cost_estimate=pl.CostEstimate(
            flops=24 * n * D * FF,
            bytes_accessed=n * D * 16 + 12 * D * FF,
            transcendentals=n * FF,
        ),
        name="feed_forward",
    )(core, x, *mixed, g, mine, other, back_mine, back_other, vec, fb)


def last_kernel(x_ref, gh_ref, gain_ref, *refs):
    grads, w0, w1 = refs[:3], refs[3], refs[4]
    out_ref, sum_ref = refs[-2:]
    x = x_ref[...].astype(F32)
    c = x - jnp.mean(x, axis=1, keepdims=True)
    inv = lax.rsqrt(jnp.mean(c * c, axis=1, keepdims=True) + EPS)
    xhat = c * inv
    half = w1.shape[1] // 2
    one = dot(grads[0][...], w0[...], NT)
    one += dot(grads[1][...], w1[:, :half], NT)
    one += dot(grads[2][...], w1[:, half:], NT)
    e = one * gain_ref[...]
    m1 = jnp.mean(e, axis=1, keepdims=True)
    m2 = jnp.mean(e * xhat, axis=1, keepdims=True)
    out_ref[...] = gh_ref[...] + inv * (e - m1 - xhat * m2)
    sums = jnp.concatenate([jnp.sum(v, axis=0, keepdims=True) for v in (one * xhat, one)], axis=0)

    @pl.when(pl.program_id(0) == 0)
    def _():
        sum_ref[...] = sums

    @pl.when(pl.program_id(0) > 0)
    def _():
        sum_ref[...] += sums


def last(x, gh, gain, grads, weights, deps=(), T=512):
    n, D = x.shape
    block = pl.BlockSpec((T, D), lambda i: (i, 0))
    return pl.pallas_call(
        last_kernel,
        grid=(n // T,),
        in_specs=[block, block, pl.BlockSpec((1, D), lambda i: (0, 0))]
        + [block] * 3
        + [pl.BlockSpec(weight.shape, lambda i: (0, 0)) for weight in weights]
        + [pl.BlockSpec(memory_space=pl.ANY)] * len(deps),
        out_specs=[block, pl.BlockSpec((2, D), lambda i: (0, 0))],
        out_shape=[jax.ShapeDtypeStruct((n, D), F32), jax.ShapeDtypeStruct((2, D), F32)],
        compiler_params=pltpu.CompilerParams(vmem_limit_bytes=56 << 20),
        cost_estimate=pl.CostEstimate(
            flops=12 * n * D * D, bytes_accessed=n * D * 16, transcendentals=0
        ),
        name="input_gradient",
    )(x, gh, gain, *grads, *weights, *deps)


def project_kernel(order, rows, half, at, n1, mine, other, bias, *refs):
    qkv, w, sem = refs[-3:]
    me, core = at[0], at[1]

    @pl.when(pl.program_id(0) == 0)
    def _():
        copies = []
        for i, o in enumerate(order):
            row = pl.ds(pl.multiple_of((me ^ o) * rows, rows), rows)
            for src, part in ((mine, core), (other, 1 - core)):
                col = pl.ds(pl.multiple_of(part * half, 128), half)
                copies.append(
                    pltpu.make_async_copy(src.at[i, pl.ds(0, rows), :], w.at[row, col], sem.at[len(copies)])
                )
        for copy in copies:
            copy.start()
        for copy in copies:
            copy.wait()

    qkv[...] = (dot(n1[...], w[...], NN) + bias[...]).astype(BF)


def project(n1, mine, other, order, rows, bias, deps=(), T=512):
    n, D = n1.shape
    half = mine.shape[2]
    me, core = lax.axis_index("wide"), lax.axis_index("narrow") & 1
    if rows % 16:
        mine, other = [natural(p[:, :rows], order).reshape(-1, half) for p in (mine, other)]
        w = jnp.where(core == 0, jnp.concatenate([mine, other], 1), jnp.concatenate([other, mine], 1))
        return (dot(n1, w, NN) + bias).astype(BF), w
    anywhere = pl.BlockSpec(memory_space=pl.ANY)
    return pl.pallas_call(
        functools.partial(project_kernel, order, rows, half),
        grid=(n // T,),
        in_specs=[
            pl.BlockSpec(memory_space=pltpu.SMEM),
            pl.BlockSpec((T, D), lambda i: (i, 0)),
            anywhere,
            anywhere,
            pl.BlockSpec((1, 2 * half), lambda i: (0, 0)),
        ]
        + [anywhere] * len(deps),
        out_specs=[
            pl.BlockSpec((T, 2 * half), lambda i: (i, 0)),
            pl.BlockSpec((D, 2 * half), lambda i: (0, 0)),
        ],
        out_shape=[
            jax.ShapeDtypeStruct((n, 2 * half), BF),
            jax.ShapeDtypeStruct((D, 2 * half), BF),
        ],
        scratch_shapes=[pltpu.SemaphoreType.DMA((2 * len(order),))],
        compiler_params=pltpu.CompilerParams(vmem_limit_bytes=56 << 20),
        cost_estimate=pl.CostEstimate(
            flops=8 * n * D * half, bytes_accessed=n * D * 4 + n * half * 4, transcendentals=0
        ),
        name="project",
    )(jnp.stack([me, core]).astype(jnp.int32), n1, mine, other, bias, *deps)


def swap(x, axis, mask):
    size = lax.axis_size(axis)
    return lax.ppermute(x, axis, [(i, i ^ mask) for i in range(size)])


def bit_groups(size):
    top = size.bit_length() - 1
    cuts = [(0, 1)]
    low = 1
    while low < top:
        high = min(low + 2, top)
        cuts.append((low, high))
        low = high
    return cuts


def gather_wide(piece):
    size = lax.axis_size("wide")
    me = lax.axis_index("wide")
    stack, order = piece[None], [0]
    for low, high in reversed(bit_groups(size)):
        masks = [m << low for m in range(1 << (high - low))]
        stack = jnp.concatenate([stack] + [swap(stack, "wide", m) for m in masks[1:]])
        order = [o ^ m for m in masks for o in order]
    return stack, order


def natural(stack, order):
    size = len(order)
    me = lax.axis_index("wide")
    place = jnp.argsort(jnp.array(order))
    return jnp.take(stack, place[me ^ jnp.arange(size)], axis=0)


def gather(piece):
    mine, order = gather_wide(piece)
    return mine, swap(mine, "narrow", 1), order


def half_of(x, index, size, axis):
    return lax.dynamic_slice_in_dim(x, index * size, size, axis)


def add(*terms):
    total = terms[0].astype(F32)
    for term in terms[1:]:
        total = total + term.astype(F32)
    return total.astype(BF)


def scatter_wide(x):
    me = lax.axis_index("wide")
    size = x.shape[0]
    for low, high in bit_groups(size):
        ways = 1 << (high - low)
        mine = (me >> low) & (ways - 1)
        split = x.reshape((x.shape[0] // ways, ways) + x.shape[1:])
        got = [lax.dynamic_index_in_dim(split, mine, 1, keepdims=False)]
        for m in range(1, ways):
            sent = lax.dynamic_index_in_dim(split, mine ^ m, 1, keepdims=False)
            got.append(swap(sent, "wide", m << low))
        x = add(*got)
    return x[0]


def pick(x, low, high):
    me = lax.axis_index("wide")
    ways = 1 << (high - low)
    mine = (me >> low) & (ways - 1)
    split = [t.reshape((t.shape[0] // ways, ways) + t.shape[1:]) for t in x]
    return [add(*[lax.dynamic_index_in_dim(t, mine ^ m, 1, keepdims=False) for t in split]) for m in range(ways)]


def send(picked, low):
    return [picked[0]] + [swap(t, "wide", m << low) for m, t in enumerate(picked) if m]


def regroup(blocks, size):
    eight, depth, step = blocks.shape
    r = depth // 5
    blocks = blocks.reshape(eight, 5, r, step).transpose(0, 2, 1, 3).reshape(size, -1, 5, step)
    return blocks.transpose(0, 2, 1, 3).reshape(size, -1, step)


def regroup_back(blocks, size):
    eight, depth, step = blocks.shape
    blocks = blocks.transpose(1, 0, 2).reshape(depth, size, -1)
    return blocks.transpose(1, 0, 2)


def body(tokens, cotangent, row_kind, grad_mask, w_qkv, w_out, w_in, w_back, norm_gain, norm_shift, proj_bias, ffn_bias):
    rows, length, width = tokens.shape
    n = rows * length
    size = lax.axis_size("wide")
    share = width // size
    core = lax.axis_index("narrow") & 1
    packed = jnp.concatenate([norm_gain, norm_shift, proj_bias, ffn_bias.reshape(-1, share)])
    pairs = width // 128
    by_pair = w_qkv.reshape(share, 3, pairs, 128).transpose(0, 2, 1, 3).reshape(share, 3 * width)
    pieces = [half_of(by_pair[:, :768], core, 384, 1), half_of(by_pair[:, 768:], core, 768, 1)]
    extra = jnp.pad(packed.reshape(-1), (0, 16 * 384 - packed.size)).reshape(16, 384)
    pieces[0] = jnp.concatenate([pieces[0], extra])
    gathered = [gather(piece) for piece in pieces]
    small = natural(gathered[0][0][:, share:], gathered[0][2])
    small = small.reshape(size, -1)[:, : packed.size].reshape((size,) + packed.shape).astype(F32)
    hid = w_in.shape[1] // 2
    piece = jnp.concatenate(
        [half_of(w_out, core, width // 2, 1), half_of(w_in, core, hid, 1)]
        + [half_of(w_back[i * share : (i + 1) * share], core, width // 2, 1) for i in range(w_back.shape[0] // share)],
        axis=1,
    )
    mine = lax.all_gather(piece, "wide", axis=0, tiled=True)

    def back_half(gathered):
        chunks = gathered[:, width // 2 + hid :].reshape(size, share, -1, width // 2)
        return chunks.transpose(0, 2, 1, 3).reshape(-1, width // 2)

    by_column = small[:, :8].transpose(1, 0, 2).reshape(8, width)
    gains, shifts, biases = by_column[:2], by_column[2:4], by_column[4:8]
    ffn_bias_full = small[:, 8:].reshape(1, -1)
    x = tokens.reshape(n, width)
    inputs = x.astype(F32)
    centred = inputs - jnp.mean(inputs, axis=-1, keepdims=True)
    inv = lax.rsqrt(jnp.mean(centred * centred, axis=-1, keepdims=True) + EPS)
    normed_one = (centred * inv * gains[0] + shifts[0]).astype(BF)
    keep = jnp.where(row_kind[:, None] == 1, jnp.ones(grad_mask.shape, F32), grad_mask.astype(F32))
    g_ffn = (cotangent.astype(F32) * keep[:, :, None]).reshape(n, width).astype(BF)
    n1t = normed_one.T
    bias = jnp.stack([biases[0], jnp.zeros((width,), F32), biases[1]])
    bias = bias.reshape(3, pairs, 128).transpose(1, 0, 2).reshape(1, -1)
    qkv_a, w_a = project(normed_one, *gathered[0], share, bias[:, :768])
    mixed_a, lse_a = attn_fwd(qkv_a, 0, 2, rows)
    qkv_b, w_b = project(normed_one, *gathered[1], share, bias[:, 768:], deps=(mixed_a,))
    mixed_b, lse_b = attn_fwd(qkv_b, 0, 2, rows)
    mine = tie(mine, mixed_b)
    other = swap(mine, "narrow", 1)
    mixed_c, lse_c = attn_fwd(qkv_b, 2, 2, rows, deps=(mine,))
    vec = jnp.stack([gains[1], shifts[1], biases[2], biases[3]])
    direct = size == 8 and share % 16 == 0
    backs = (mine, other) if direct else (back_half(mine), back_half(other))
    at = core[None]
    layer_out, g_hidden, g_mixed, kept, sent, kept_b, sent_b, sums, ffn_sum = middle(
        at, x, (mixed_a, mixed_b, mixed_c), g_ffn, mine, other, *backs, direct, vec, ffn_bias_full
    )
    if size != 8:
        kept, sent, kept_b, sent_b = (
            regroup(kept, size), regroup(sent, size), regroup_back(kept_b, size), regroup_back(sent_b, size)
        )
    groups = [(bit, bit + 1) for bit in range(size.bit_length() - 1)]

    def finish(x, stage):
        for low, high in groups[stage:]:
            x = send(pick(x, low, high), low)
        return add(*x)[0]

    def step_on(x, stage):
        picked = pick(x, *groups[stage])
        return picked, send(picked, groups[stage][0])

    from_core = swap(sent, "narrow", 1)
    from_core_b = swap(sent_b, "narrow", 1)
    g_c, keep_c, send_c, sum_c = attn_bwd(at, qkv_b, 2, mixed_c, lse_c, g_mixed, 4, n1t, rows)
    both = add(kept, from_core)
    picked_b, x_b = step_on([kept_b, from_core_b], 0)
    summed = lax.psum_scatter(both.reshape(-1, both.shape[2]), "wide", scatter_dimension=0, tiled=True)
    from_core_c = swap(send_c, "narrow", 1)
    g_b, keep_d, send_d, sum_b = attn_bwd(
        at, qkv_b, 0, mixed_b, lse_b, g_mixed, 2, n1t, rows, deps=[both, keep_c] + picked_b
    )
    from_core_d = swap(send_d, "narrow", 1)
    picked_b, x_b = step_on(x_b, 1)
    tied = tie(from_core_c, keep_d)
    picked_c, x_c = step_on([t.reshape(size, share, -1) for t in (keep_c, tied)], 0)
    g_a, keep_e, send_e, sum_a = attn_bwd(
        at, qkv_a, 0, mixed_a, lse_a, g_mixed, 0, n1t, rows, deps=picked_b + picked_c + [keep_d]
    )
    from_core_e = swap(send_e, "narrow", 1)
    picked_b, x_b = step_on([x_b[0], tie(x_b[1], keep_e)], 2)
    picked_c, x_c = step_on([x_c[0], tie(x_c[1], keep_e)], 1)
    input_grad, last_sums = last(
        x, g_hidden, gains[:1], (g_a, g_b, g_c), (w_a, w_b), deps=picked_b + picked_c + [from_core_d]
    )
    column_sums = jnp.concatenate([t[0] for t in (sum_a, sum_b, sum_c)])
    column_sums = column_sums.reshape(pairs, 3, 128).transpose(1, 0, 2).reshape(3, width)
    by_column = jnp.stack(
        [last_sums[0], sums[0], last_sums[1], sums[1], column_sums[0], column_sums[2], sums[2], sums[3]]
    )
    by_column = by_column.reshape(8, size, share).transpose(1, 0, 2)
    small = jnp.concatenate([by_column, ffn_sum.reshape(size, -1, share)], axis=1).astype(BF).reshape(size, -1)
    count = small.shape[1]
    extra = -(-count // 768)
    small = jnp.pad(small, ((0, 0), (0, extra * 768 - count))).reshape(size, extra, 768)
    halves = [pick([t.reshape(size, share, -1) for t in ts], *groups[0]) for ts in ((keep_d, from_core_d), (keep_e, from_core_e))]
    picked = [
        jnp.concatenate([jnp.concatenate([d, e], axis=2), s], axis=1)
        for d, e, s in zip(*halves, pick([small], *groups[0]))
    ]
    x_b = [x_b[0], tie(x_b[1], last_sums)]
    x_c = [x_c[0], tie(x_c[1], last_sums)]
    block_b = finish(x_b, 3)
    early = jnp.concatenate([summed, block_b.reshape(-1, width // 2)], axis=0)
    early_y = swap(early, "narrow", 2)
    x_de = send(picked, 0)
    picked_c, x_c = step_on(x_c, 2)
    early = add(early, early_y)
    early_core = swap(early, "narrow", 1)
    x_de = [x_de[0], tie(x_de[1], early)]
    _, x_de = step_on(x_de, 1)
    x_de = [x_de[0], tie(x_de[1], early_core)]
    late = finish(x_de, 2)
    more = finish(x_c, 3)
    late = jnp.concatenate([late, jnp.pad(more, ((0, extra), (0, 0)))], axis=1)
    late = add(late, swap(late, "narrow", 2))
    late_core = swap(late, "narrow", 1)

    def ordered(mine, other):
        return [jnp.where(core == 0, mine, other), jnp.where(core == 0, other, mine)]

    left, right = ordered(early, early_core)
    five, step = 5 * share, width // 2
    share_out = jnp.concatenate([t[:share] for t in (left, right)], axis=1).astype(F32)
    share_in = jnp.concatenate(
        [t[i * share : (i + 1) * share] for t in (left, right) for i in range(1, 5)], axis=1
    ).astype(F32)
    share_back = jnp.concatenate([t[five:].reshape(step, -1).T for t in (left, right)], axis=1).astype(F32)
    small = late[share:, :768].astype(F32) + late_core[share:, :768].astype(F32)
    small = small.reshape(-1)[:count].reshape(-1, share)
    left, right = ordered(late[:share], late_core[:share])
    share_qkv = jnp.stack([left[:, 384:768], right[:, 384:768], left[:, :384], right[:, :384], left[:, 768:], right[:, 768:]], axis=1)
    share_qkv = share_qkv.reshape(share, pairs, 3, 128).transpose(0, 2, 1, 3).reshape(share, -1).astype(F32)
    return (
        layer_out.reshape(rows, length, width),
        input_grad.reshape(rows, length, width),
        share_qkv,
        share_out,
        share_in,
        share_back,
        small[:2],
        small[2:4],
        small[4:8],
        small[8:].reshape(-1),
    )


def solution(mesh):
    in_specs = (
        P(("wide", "narrow"), None, None),
        P(("wide", "narrow"), None, None),
        P(("wide", "narrow")),
        P(("wide", "narrow"), None),
        P("wide", None),
        P("wide", None),
        P("wide", None),
        P("wide", None),
        P(None, "wide"),
        P(None, "wide"),
        P(None, "wide"),
        P("wide"),
    )
    out_specs = (
        P(("wide", "narrow"), None, None),
        P(("wide", "narrow"), None, None),
        P("wide", None),
        P("wide", None),
        P("wide", None),
        P("wide", None),
        P(None, "wide"),
        P(None, "wide"),
        P(None, "wide"),
        P("wide"),
    )
    return jax.shard_map(body, mesh=mesh, in_specs=in_specs, out_specs=out_specs, check_vma=False)
```

time: 510 us -> 484 us (0.949); the launches traced: 504 us -> 485 us
  waiting for transfers between devices: 87.2 us -> 45 us
  Pallas kernels: 260 us -> 291 us
  other arithmetic: 25.3 us -> 45.6 us
  matrix products: 13.4 us -> 0 us
  starting transfers between devices: 47.8 us -> 36.3 us
    all_gather x1, waiting for transfers between devices: 41.8 us -> 4.36 us  [body(): mine = lax.all_gather(piece, 'wide', axis=0, tiled=True)]
    pallas_call x5 -> x15, Pallas kernels: 224 us -> 256 us  [the longest x1 119 us: middle(): pl.pallas_call(functools.partial(mid_kernel, T, direct), grid=(FF // F,),...]
    convert_element_type x8 -> x15, other arithmetic: 9.93 us -> 23.5 us  [add(): return total.astype(BF)]
    dot_general x2 -> x0, matrix products: 13.4 us -> none  [dot(): return lax.dot_general(a, b, dims, preferred_element_type=F32)]
    ppermute x35 -> x29, starting transfers between devices: 47.8 us -> 36.2 us  [swap(): return lax.ppermute(x, axis, [(i, i ^ mask) for i in range(size)])]
    reshape x9 -> x6, local copies, waits for them, and re-layouts: 12.8 us -> 2.04 us  [the longest x2 1.9 us: body(): w_qkv.reshape(share, 3, pairs, 128).transpose(0, 2, 1, 3)]
    unnamed x80 -> x112, local copies, waits for them, and re-layouts: 17.3 us -> 23.4 us
    slice x13 -> x12, local copies, waits for them, and re-layouts: 9.65 us -> 4.22 us  [the longest x3 2.27 us: body(): column_sums = jnp.concatenate([t[0] for t in (sum_a, sum_b, sum_c)])]
  transfers between devices with their start and end apart: 37 -> 31, of which waited for: 14 -> 7; matrix products, arithmetic and copies ran while one was open for 13% -> 17% of each run, Pallas kernels for 31% -> 35%
where the time goes in v3:
time: 484 us; the launch traced here: 485 us
  Pallas kernels  291 us (60%)
  local copies, waits for them, and re-layouts  52.1 us (11%)
  other arithmetic  45.6 us (9%)
  waiting for transfers between devices  45 us (9%)
  starting transfers between devices  36.3 us (7%)
  between operations  15.1 us (3%)
    pallas_call x1, Pallas kernels, middle(): pl.pallas_call(functools.partial(mid_kernel, T, direct), grid=(FF // F,),...  119 us
    pallas_call x3, Pallas kernels, attn_bwd(): pl.pallas_call(kernel, grid=(pairs, rows), in_specs=[pl.BlockSpec(memory_...  92.8 us
    pallas_call x3, Pallas kernels, attn_fwd(): pl.pallas_call(kernel, grid=(rows, pairs), in_specs=[pl.BlockSpec((length...  43.8 us
    ppermute x29, waiting for transfers between devices, swap(): return lax.ppermute(x, axis, [(i, i ^ mask) for i in range(size)])  40.6 us
    ppermute x29, starting transfers between devices, swap(): return lax.ppermute(x, axis, [(i, i ^ mask) for i in range(size)])  36.2 us
    convert_element_type x15, other arithmetic, add(): return total.astype(BF)  23.5 us
    unnamed x112, local copies, waits for them, and re-layouts  23.4 us
    pallas_call x2, Pallas kernels, project(): pl.pallas_call(functools.partial(project_kernel, order, rows, half), grid...  18.3 us
  transfers between devices with their start and end apart: 31, of which 7 were waited for; matrix products, arithmetic and copies ran while one was open for 17% of the time, Pallas kernels for 35%

profile of v3, /device:TPU:1, one launch (start us, length us, event | category | flops | bytes accessed | tf_op | source)
XLA Modules:
  0.0 484.9 jit_solution(3594497599660213883)
XLA Ops:
  7.2 1.5 reshape.401
  10.4 2.1 collective-permute-start
  12.5 2.3 collective-permute-start.1
  15.9 3.2 collective-permute-start.6
  19.8 2.1 fusion.26
  21.9 1.7 dynamic-slice_dynamic-update-slice_fusion
  23.6 1.6 dynamic-slice_dynamic-update-slice_fusion.4
  25.1 1.5 dynamic-slice_dynamic-update-slice_fusion.3
  26.7 1.5 dynamic-slice_dynamic-update-slice_fusion.2
  28.2 1.5 dynamic-slice_dynamic-update-slice_fusion.1
  33.5 1.1 pad_maximum_fusion.4
  34.5 1.3 collective-permute-start.3
  35.8 1.5 constant_dynamic-update-slice_fusion.3
  37.3 1.5 constant_dynamic-update-slice_fusion.2
  38.9 1.6 constant_dynamic-update-slice_fusion.1
  40.5 1.8 pad_maximum_fusion.3
  46.3 9.3 %collective-permute-start.4 = (bf16[8,112,384]{2,1,0:T(8,128)(2,1)}, bf16[8,112,384]{2,1,0:T(8,128)(2,1)}, u32[]{:S(2)}, u32[]{:S(2)}) collective-permute-start(bf16[8,112,384]{2,1,0:T(8,128)(2,1)} %constant_dynamic-update-slice_fusion.mine), channel_id=1, source_target_pairs={{0,1},{1,0},{2,3},{3,2},{4,5},{5,4},{6,7},{7,6},{8,9},{9,8},{10,11... | collective-permute-start | bytes 2064392 | tf_op jit(solution)/shard_map/ppermute | solution.py:583
  58.1 2.9 add_convert_fusion.n1
  61.0 1.5 collective-permute-done.8
  62.5 1.1 constant_dynamic-update-slice_fusion.5.mine
  63.6 2.5 collective-permute-start.9
  66.1 7.6 %project.2 = (bf16[2048,768]{1,0:T(8,128)(2,1)}, bf16[768,768]{1,0:T(8,128)(2,1)}) custom-call(s32[2]{0:T(128)} %pad_add_fusion.at, bf16[2048,768]{1,0:T(8,128)(2,1)} %add_convert_fusion.n1, bf16[8,112,384]{2,1,0:T(8,128)(2,1)} %constant_dynamic-update-slice_fusion.mine, bf16[8,112,384]{2,1,0:T(8,128)(2,1)} %collective-permute-done.4.other, ...), custom_call_target="tpu_custom_call" | custom-call | flops 4831838208 | bytes 9437184 | tf_op jit(solution)/shard_map/project/pallas_call | solution.py:553
  73.7 14.6 %attention_forward.3 = (bf16[2048,256]{1,0:T(8,128)(2,1)}, bf16[2048,256]{1,0:T(8,128)(2,1)}) custom-call(bf16[2048,768]{1,0:T(8,128)(2,1)} %get-tuple-element.45.x_ref.x), custom_call_target="tpu_custom_call" | custom-call | flops 16106127360 | bytes 5242880 | tf_op jit(solution)/shard_map/attention_forward/pallas_call | solution.py:74
  88.3 1.1 copy-done.41
  89.4 10.7 %project.3 = (bf16[2048,1536]{1,0:T(8,128)(2,1)}, bf16[768,1536]{1,0:T(8,128)(2,1)}) custom-call(s32[2]{0:T(128)} %pad_add_fusion.at, bf16[2048,768]{1,0:T(8,128)(2,1)} %add_convert_fusion.n1, bf16[8,96,768]{2,1,0:T(8,128)(2,1)} %copy-done.31, bf16[8,96,768]{2,1,0:T(8,128)(2,1)} %copy-done.41, f32[1,1536]{1,0:T(1,128)} %slice.305.bias, ...), custom_call_target="tpu_custom_call" | custom-call | flops 9663676416 | bytes 12582912 | tf_op jit(solution)/shard_map/project/pallas_call | solution.py:553
  100.1 14.6 %attention_forward.4 = (bf16[2048,256]{1,0:T(8,128)(2,1)}, bf16[2048,256]{1,0:T(8,128)(2,1)}) custom-call(bf16[2048,1536]{1,0:T(8,128)(2,1)} %get-tuple-element.47.x_ref.x), custom_call_target="tpu_custom_call" | custom-call | flops 16106127360 | bytes 5242880 | tf_op jit(solution)/shard_map/attention_forward/pallas_call | solution.py:74
  114.8 4.4 all-gather.2.cloned.1.call-done.a
  119.2 1.5 collective-permute-start.10
  120.8 4.4 multiply_convert_fusion
  126.2 2.9 copy.89.t
  130.4 14.6 %attention_forward.5 = (bf16[2048,256]{1,0:T(8,128)(2,1)}, bf16[2048,256]{1,0:T(8,128)(2,1)}) custom-call(bf16[2048,1536]{1,0:T(8,128)(2,1)} %get-tuple-element.47.x_ref.x, bf16[768,3456]{1,0:T(8,128)(2,1)} %tie.8.refs_0_.mine.back_mine), custom_call_target="tpu_custom_call" | custom-call | flops 16106127360 | bytes 5242880 | tf_op jit(solution)/shard_map/attention_forward/pallas_call | solution.py:74
  144.9 119.4 %feed_forward.1 = (bf16[2048,768]{1,0:T(8,128)(2,1)}, f32[2048,768]{1,0:T(8,128)}, bf16[2048,768]{1,0:T(8,128)(2,1)}, bf16[8,480,384]{2,1,0:T(8,128)(2,1)}, bf16...) custom-call(s32[1]{0:T(128)} %bitcast.at, ...), custom_call_target="tpu_custom_call" | custom-call | flops 115964116992 | bytes 53477376 | tf_op jit(solution)/shard_map/feed_forward/pallas_call | solution.py:428
  265.2 30.8 %attention_backward.3 = (bf16[2048,768]{1,0:T(8,128)(2,1)}, bf16[768,384]{1,0:T(8,128)(2,1)}, bf16[768,384]{1,0:T(8,128)(2,1)}, f32[8,768]{1,0:T(8,128)}) custom-call(s32[1]{0:T(128)} %bitcast.at, bf16[2048,1536]{1,0:T(8,128)(2,1)} %get-tuple-element.47.x_ref.x, bf16[2048,256]{1,0:T(8,128)(2,1)} %get-tuple-element.49.m2_any.o, ...), custom_call_target="tpu_custom_call" | custom-call | flops 30064771072 | bytes 9437184 | tf_op jit(solution)/shard_map/attention_backward/pallas_call | solution.py:176
  301.4 4.5 add_convert_fusion.3
  306.2 2.4 add_convert_fusion.1.refs_0_
  308.6 31.0 %attention_backward.4 = (bf16[2048,768]{1,0:T(8,128)(2,1)}, bf16[768,384]{1,0:T(8,128)(2,1)}, bf16[768,384]{1,0:T(8,128)(2,1)}, f32[8,768]{1,0:T(8,128)}) custom-call(s32[1]{0:T(128)} %bitcast.at, bf16[2048,1536]{1,0:T(8,128)(2,1)} %get-tuple-element.47.x_ref.x, bf16[2048,256]{1,0:T(8,128)(2,1)} %get-tuple-element.48.b.m1_any.o, ...), custom_call_target="tpu_custom_call" | custom-call | flops 30064771072 | bytes 9437184 | tf_op jit(solution)/shard_map/attention_backward/pallas_call | solution.py:176
  341.7 2.2 fusion.10
  343.9 1.2 collective-permute-start.16
  345.0 2.4 fusion.3
  348.3 31.0 %attention_backward.5 = (bf16[2048,768]{1,0:T(8,128)(2,1)}, bf16[768,384]{1,0:T(8,128)(2,1)}, bf16[768,384]{1,0:T(8,128)(2,1)}, f32[8,768]{1,0:T(8,128)}) custom-call(s32[1]{0:T(128)} %bitcast.at, bf16[2048,768]{1,0:T(8,128)(2,1)} %get-tuple-element.45.x_ref.x, bf16[2048,256]{1,0:T(8,128)(2,1)} %get-tuple-element.46.refs_0_.m0_any.o, ...), custom_call_target="tpu_custom_call" | custom-call | flops 30064771072 | bytes 9437184 | tf_op jit(solution)/shard_map/attention_backward/pallas_call | solution.py:176
  381.6 1.7 fusion.16.refs_8_
  384.1 1.6 add_convert_fusion.19
  386.6 1.9 fusion.4
  388.5 1.3 collective-permute-start.20
  390.6 16.4 %input_gradient.1 = (f32[2048,768]{1,0:T(8,128)}, f32[2,768]{1,0:T(2,128)}) custom-call(bf16[2048,768]{1,0:T(8,128)(2,1)} %bitcast.142, f32[2048,768]{1,0:T(8,128)} %get-tuple-element.51.gh_ref, f32[1,768]{1,0:T(1,128)} %slice.253.gain_ref, bf16[2048,768]{1,0:T(8,128)(2,1)} %get-tuple-element.63.refs_0_, bf16[2048,768]{1,0:T(8,128)(2,1)} %get-tuple-element.64.refs_1_, ...), custom_call_target="tpu_custom_call" | custom-call | flops 14495514624 | bytes 25165824 | tf_op jit(solution)/shard_map/input_gradient/pallas_call | solution.py:505
  407.8 1.1 fusion.13
  410.0 1.3 collective-permute-start.21
  411.2 1.2 add_convert_fusion.13
  414.4 11.6 %collective-permute-done.21 = bf16[864,384]{1,0:T(8,128)(2,1)} collective-permute-done((bf16[864,384]{1,0:T(8,128)(2,1)S(1)}, bf16[864,384]{1,0:T(8,128)(2,1)}, u32[]{:S(2)}, u32[]{:S(2)}) %collective-permute-start.21) | collective-permute-done | bytes 663584 | tf_op jit(solution)/shard_map/ppermute | solution.py:583
  426.0 1.3 add_convert_fusion.4.b
  427.3 1.5 collective-permute-start.23
  429.8 1.2 collective-permute-start.26
  432.1 4.2 collective-permute-done.26
  436.3 1.5 fusion.19
  437.9 2.0 copy.105.a
  439.8 1.3 add_convert_fusion.8
  442.1 7.4 %collective-permute-done.22.a = bf16[2,98,768]{2,1,0:T(8,128)(2,1)S(1)} collective-permute-done((bf16[2,98,768]{2,1,0:T(8,128)(2,1)S(1)}, bf16[2,98,768]{2,1,0:T(8,128)(2,1)S(1)}, u32[]{:S(2)}, u32[]{:S(2)}) %collective-permute-start.22) | collective-permute-done | bytes 301088 | tf_op jit(solution)/shard_map/ppermute | solution.py:583
  451.6 10.1 %collective-permute-done.24 = bf16[1,98,768]{2,1,0:T(8,128)(2,1)S(1)} collective-permute-done((bf16[1,98,768]{2,1,0:T(8,128)(2,1)S(1)}, bf16[1,98,768]{2,1,0:T(8,128)(2,1)S(1)}, u32[]{:S(2)}, u32[]{:S(2)}) %collective-permute-start.24) | collective-permute-done | bytes 150560 | tf_op jit(solution)/shard_map/ppermute | solution.py:583
  461.8 1.2 collective-permute-start.27
  463.1 5.6 %collective-permute-done.27 = bf16[98,1152]{1,0:T(8,128)(2,1)S(1)} collective-permute-done((bf16[98,1152]{1,0:T(8,128)(2,1)S(1)}, bf16[98,1152]{1,0:T(8,128)(2,1)S(1)}, u32[]{:S(2)}, u32[]{:S(2)}) %collective-permute-start.27) | collective-permute-done | bytes 225824 | tf_op jit(solution)/shard_map/ppermute | solution.py:583
  468.8 1.5 collective-permute-start.28
  470.3 1.4 copy.110
  471.7 1.1 convert_element_type.549
  476.6 1.1 reshape.425
  (269 shorter events, 42.7 us)
Async XLA Ops:
  7.2 112.0 %all-gather.2.cloned.1.call-start = ((), (), s32[]{:S(2)}) async-start(), calls=%async_computation.1 | async-start | bytes 5971968 | tf_op jit(solution)/shard_map/all_gather | solution.py:692
  9.0 10.1 %copy-start.29 = (bf16[96,768]{1,0:T(8,128)(2,1)S(1)}, bf16[96,768]{1,0:T(8,128)(2,1)}, u32[]{:S(2)}) copy-start(bf16[96,768]{1,0:T(8,128)(2,1)} %param.18) | copy-start | bytes 442372
  10.4 23.1 %collective-permute-start = (bf16[1,112,384]{2,1,0:T(8,128)(2,1)}, bf16[1,112,384]{2,1,0:T(8,128)(2,1)}, u32[]{:S(2)}, u32[]{:S(2)}) collective-permute-start(bf16[1,112,384]{2,1,0:T(8,128)(2,1)} %maximum_bitcast_fusion), channel_id=1, source_target_pairs={{0,8},{4,12},{8,0},{12,4},{16,24},{20,28},{24,16},{28,20},{1,9},{5... | collective-permute-start | bytes 258056 | tf_op jit(solution)/shard_map/ppermute | solution.py:583
  12.5 21.0 %collective-permute-start.1 = (bf16[1,112,384]{2,1,0:T(8,128)(2,1)}, bf16[1,112,384]{2,1,0:T(8,128)(2,1)}, u32[]{:S(2)}, u32[]{:S(2)}) collective-permute-start(bf16[1,112,384]{2,1,0:T(8,128)(2,1)} %maximum_bitcast_fusion), channel_id=1, source_target_pairs={{0,16},{4,20},{8,24},{12,28},{16,0},{20,4},{24,8},{28,12},{1,17},{... | collective-permute-start | bytes 258056 | tf_op jit(solution)/shard_map/ppermute | solution.py:583
  14.8 18.7 %collective-permute-start.2 = (bf16[1,112,384]{2,1,0:T(8,128)(2,1)}, bf16[1,112,384]{2,1,0:T(8,128)(2,1)}, u32[]{:S(2)}, u32[]{:S(2)}) collective-permute-start(bf16[1,112,384]{2,1,0:T(8,128)(2,1)} %maximum_bitcast_fusion), channel_id=1, source_target_pairs={{0,24},{4,28},{8,16},{12,20},{16,8},{20,12},{24,0},{28,4},{1,25},{... | collective-permute-start | bytes 258056 | tf_op jit(solution)/shard_map/ppermute | solution.py:583
  15.6 24.9 %collective-permute-start.5 = (bf16[1,96,768]{2,1,0:T(8,128)(2,1)}, bf16[1,96,768]{2,1,0:T(8,128)(2,1)S(1)}, u32[]{:S(2)}, u32[]{:S(2)}) collective-permute-start(bf16[1,96,768]{2,1,0:T(8,128)(2,1)} %get-tuple-element.123), channel_id=1, source_target_pairs={{0,8},{4,12},{8,0},{12,4},{16,24},{20,28},{24,16},{28,20},{1,9},{5... | collective-permute-start | bytes 442376 | tf_op jit(solution)/shard_map/ppermute | solution.py:583
  15.9 24.5 %collective-permute-start.6 = (bf16[1,96,768]{2,1,0:T(8,128)(2,1)}, bf16[1,96,768]{2,1,0:T(8,128)(2,1)S(1)}, u32[]{:S(2)}, u32[]{:S(2)}) collective-permute-start(bf16[1,96,768]{2,1,0:T(8,128)(2,1)} %get-tuple-element.123), channel_id=1, source_target_pairs={{0,16},{4,20},{8,24},{12,28},{16,0},{20,4},{24,8},{28,12},{1,17},{... | collective-permute-start | bytes 442376 | tf_op jit(solution)/shard_map/ppermute | solution.py:583
  19.8 10.1 %copy-start = (s32[8]{0:T(128)S(1)}, s32[8]{0:T(128)}, u32[]{:S(2)}) copy-start(s32[8]{0:T(128)} %constant.176) | copy-start | bytes 100
  19.8 11.5 %copy-start.1 = (bf16[2,1024,768]{2,1,0:T(8,128)(2,1)S(1)}, bf16[2,1024,768]{2,1,0:T(8,128)(2,1)}, u32[]{:S(2)}) copy-start(bf16[2,1024,768]{2,1,0:T(8,128)(2,1)} %param.13) | copy-start | bytes 9437188
  29.8 379.1 %reduce-scatter.2.cloned.1.call-start = ((), (), s32[]{:S(2)}) async-start(), calls=%async_computation.2 | async-start | bytes 3317760 | tf_op jit(solution)/shard_map/reduce_scatter | solution.py:745
  33.4 7.0 %collective-permute-start.7 = (bf16[1,96,768]{2,1,0:T(8,128)(2,1)}, bf16[1,96,768]{2,1,0:T(8,128)(2,1)S(1)}, u32[]{:S(2)}, u32[]{:S(2)}) collective-permute-start(bf16[1,96,768]{2,1,0:T(8,128)(2,1)} %get-tuple-element.123), channel_id=1, source_target_pairs={{0,24},{4,28},{8,16},{12,20},{16,8},{20,12},{24,0},{28,4},{1,25},{... | collective-permute-start | bytes 442376 | tf_op jit(solution)/shard_map/ppermute | solution.py:583
  34.5 10.0 %collective-permute-start.3 = (bf16[4,112,384]{2,1,0:T(8,128)(2,1)S(1)}, bf16[4,112,384]{2,1,0:T(8,128)(2,1)S(1)}, u32[]{:S(2)}, u32[]{:S(2)}) collective-permute-start(bf16[4,112,384]{2,1,0:T(8,128)(2,1)S(1)} %pad_maximum_fusion.4), channel_id=1, source_target_pairs={{0,4},{4,0},{8,12},{12,8},{16,20},{20,16},{24,28},{28,24},{1,5},{5... | collective-permute-start | bytes 1032200 | tf_op jit(solution)/shard_map/ppermute | solution.py:583
  42.3 20.2 %collective-permute-start.8 = (bf16[4,96,768]{2,1,0:T(8,128)(2,1)}, bf16[4,96,768]{2,1,0:T(8,128)(2,1)}, u32[]{:S(2)}, u32[]{:S(2)}) collective-permute-start(bf16[4,96,768]{2,1,0:T(8,128)(2,1)} %pad_maximum_fusion.3), channel_id=1, source_target_pairs={{0,4},{4,0},{8,12},{12,8},{16,20},{20,16},{24,28},{28,24},{1,5},{5... | collective-permute-start | bytes 1769480 | tf_op jit(solution)/shard_map/ppermute | solution.py:583
  46.3 19.9 %collective-permute-start.4 = (bf16[8,112,384]{2,1,0:T(8,128)(2,1)}, bf16[8,112,384]{2,1,0:T(8,128)(2,1)}, u32[]{:S(2)}, u32[]{:S(2)}) collective-permute-start(bf16[8,112,384]{2,1,0:T(8,128)(2,1)} %constant_dynamic-update-slice_fusion.mine), channel_id=1, source_target_pairs={{0,1},{1,0},{2,3},{3,2},{4,5},{5,4},{6,7},{7,6},{8,9},{9,8},{10,11... | collective-permute-start | bytes 2064392 | tf_op jit(solution)/shard_map/ppermute | solution.py:583
  58.1 4.4 copy-start.30
  63.6 10.2 %copy-start.31 = (bf16[8,96,768]{2,1,0:T(8,128)(2,1)}, bf16[8,96,768]{2,1,0:T(8,128)(2,1)S(1)}, u32[]{:S(2)}) copy-start(bf16[8,96,768]{2,1,0:T(8,128)(2,1)S(1)} %constant_dynamic-update-slice_fusion.5.mine) | copy-start | bytes 3538948
  63.6 24.8 %collective-permute-start.9 = (bf16[8,96,768]{2,1,0:T(8,128)(2,1)S(1)}, bf16[8,96,768]{2,1,0:T(8,128)(2,1)S(1)}, u32[]{:S(2)}, u32[]{:S(2)}) collective-permute-start(bf16[8,96,768]{2,1,0:T(8,128)(2,1)S(1)} %constant_dynamic-update-slice_fusion.5.mine), channel_id=1, source_target_pairs={{0,1},{1,0},{2,3},{3,2},{4,5},{5,4},{6,7},{7,6},{8,9},{9,8},{10,11... | collective-permute-start | bytes 3538952 | tf_op jit(solution)/shard_map/ppermute | solution.py:583
  88.3 1.1 copy-start.41
  119.2 1.5 copy-start.42
  119.2 1.5 copy-start.35
  119.2 25.8 %collective-permute-start.10 = (bf16[768,3456]{1,0:T(8,128)(2,1)}, bf16[768,3456]{1,0:T(8,128)(2,1)}, u32[]{:S(2)}, u32[]{:S(2)}) collective-permute-start(bf16[768,3456]{1,0:T(8,128)(2,1)} %tie.8.refs_0_.mine.back_mine), channel_id=1, source_target_pairs={{0,1},{1,0},{2,3},{3,2},{4,5},{5,4},{6,7},{7,6},{8,9},{9,8},{10,11... | collective-permute-start | bytes 15925256 | tf_op jit(solution)/shard_map/ppermute | solution.py:583
  120.8 5.4 %copy-start.2 = (bf16[2048,768]{1,0:T(8,128)(2,1)S(1)}, bf16[2048,768]{1,0:T(8,128)(2,1)}, u32[]{:S(2)}) copy-start(bf16[2048,768]{1,0:T(8,128)(2,1)} %add_convert_fusion.n1) | copy-start | bytes 9437188
  264.3 41.9 %collective-permute-start.14 = (bf16[8,480,384]{2,1,0:T(8,128)(2,1)}, bf16[8,480,384]{2,1,0:T(8,128)(2,1)S(1)}, u32[]{:S(2)}, u32[]{:S(2)}) collective-permute-start(bf16[8,480,384]{2,1,0:T(8,128)(2,1)} %get-tuple-element.61), channel_id=1, source_target_pairs={{0,1},{1,0},{2,3},{3,2},{4,5},{5,4},{6,7},{7,6},{8,9},{9,8},{10,11... | collective-permute-start | bytes 8847368 | tf_op jit(solution)/shard_map/ppermute | solution.py:583
  265.1 36.3 %collective-permute-start.11 = (bf16[8,384,384]{2,1,0:T(8,128)(2,1)}, bf16[8,384,384]{2,1,0:T(8,128)(2,1)}, u32[]{:S(2)}, u32[]{:S(2)}) collective-permute-start(bf16[8,384,384]{2,1,0:T(8,128)(2,1)} %get-tuple-element.55), channel_id=1, source_target_pairs={{0,1},{1,0},{2,3},{3,2},{4,5},{5,4},{6,7},{7,6},{8,9},{9,8},{10,11... | collective-permute-start | bytes 7077896 | tf_op jit(solution)/shard_map/ppermute | solution.py:583
  296.0 44.9 %collective-permute-start.13 = (bf16[768,384]{1,0:T(8,128)(2,1)}, bf16[768,384]{1,0:T(8,128)(2,1)S(1)}, u32[]{:S(2)}, u32[]{:S(2)}) collective-permute-start(bf16[768,384]{1,0:T(8,128)(2,1)} %get-tuple-element.58), channel_id=1, source_target_pairs={{0,1},{1,0},{2,3},{3,2},{4,5},{5,4},{6,7},{7,6},{8,9},{9,8},{10,11... | collective-permute-start | bytes 1769480 | tf_op jit(solution)/shard_map/ppermute | solution.py:583
  301.4 4.8 copy-start.7
  305.9 39.1 %collective-permute-start.12 = (bf16[4,384,384]{2,1,0:T(8,128)(2,1)}, bf16[4,384,384]{2,1,0:T(8,128)(2,1)}, u32[]{:S(2)}, u32[]{:S(2)}) collective-permute-start(bf16[4,384,384]{2,1,0:T(8,128)(2,1)} %get-tuple-element.125.refs_3_), channel_id=1, source_target_pairs={{0,4},{4,0},{8,12},{12,8},{16,20},{20,16},{24,28},{28,24},{1,5},{5... | collective-permute-start | bytes 3538952 | tf_op jit(solution)/shard_map/ppermute | solution.py:583
  339.7 2.0 copy-start.23
  339.7 50.1 %collective-permute-start.17 = (bf16[768,384]{1,0:T(8,128)(2,1)}, bf16[768,384]{1,0:T(8,128)(2,1)S(1)}, u32[]{:S(2)}, u32[]{:S(2)}) collective-permute-start(bf16[768,384]{1,0:T(8,128)(2,1)} %get-tuple-element.69), channel_id=1, source_target_pairs={{0,1},{1,0},{2,3},{3,2},{4,5},{5,4},{6,7},{7,6},{8,9},{9,8},{10,11... | collective-permute-start | bytes 1769480 | tf_op jit(solution)/shard_map/ppermute | solution.py:583
  340.9 0.8 copy-start.10
  341.7 3.4 copy-start.6
  343.9 37.0 %collective-permute-start.16 = (bf16[4,96,384]{2,1,0:T(8,128)(2,1)}, bf16[4,96,384]{2,1,0:T(8,128)(2,1)S(1)}, u32[]{:S(2)}, u32[]{:S(2)}) collective-permute-start(bf16[4,96,384]{2,1,0:T(8,128)(2,1)} %get-tuple-element.136.refs_3_), channel_id=1, source_target_pairs={{0,4},{4,0},{8,12},{12,8},{16,20},{20,16},{24,28},{28,24},{1,5},{5... | collective-permute-start | bytes 884744 | tf_op jit(solution)/shard_map/ppermute | solution.py:583
  347.4 38.3 %collective-permute-start.15 = (bf16[2,384,384]{2,1,0:T(8,128)(2,1)S(1)}, bf16[2,384,384]{2,1,0:T(8,128)(2,1)S(1)}, u32[]{:S(2)}, u32[]{:S(2)}) collective-permute-start(bf16[2,384,384]{2,1,0:T(8,128)(2,1)S(1)} %get-tuple-element.126.refs_1_), channel_id=1, source_target_pairs={{0,8},{4,12},{8,0},{12,4},{16,24},{20,28},{24,16},{28,20},{1,9},{5... | collective-permute-start | bytes 1769480 | tf_op jit(solution)/shard_map/ppermute | solution.py:583
  348.3 32.3 %copy-start.36 = (bf16[2,3,128]{2,1,0:T(4,128)(2,1)S(1)}, bf16[2,3,128]{2,1,0:T(4,128)(2,1)}, u32[]{:S(2)}) copy-start(bf16[2,3,128]{2,1,0:T(4,128)(2,1)} %concatenate.82) | copy-start | bytes 4612
  379.3 2.3 copy-start.18
  379.3 33.6 %collective-permute-start.18 = (bf16[768,384]{1,0:T(8,128)(2,1)}, bf16[768,384]{1,0:T(8,128)(2,1)S(1)}, u32[]{:S(2)}, u32[]{:S(2)}) collective-permute-start(bf16[768,384]{1,0:T(8,128)(2,1)} %get-tuple-element.71), channel_id=1, source_target_pairs={{0,1},{1,0},{2,3},{3,2},{4,5},{5,4},{6,7},{7,6},{8,9},{9,8},{10,11... | collective-permute-start | bytes 1769480 | tf_op jit(solution)/shard_map/ppermute | solution.py:583
  381.6 5.0 %copy-start.12 = (bf16[2,1,384,384]{3,2,1,0:T(8,128)(2,1)S(1)}, bf16[2,1,384,384]{3,2,1,0:T(8,128)(2,1)}, u32[]{:S(2)}) copy-start(bf16[2,1,384,384]{3,2,1,0:T(8,128)(2,1)} %get-tuple-element.127) | copy-start | bytes 1769476
  383.2 31.2 %collective-permute-start.25 = (bf16[2,96,384]{2,1,0:T(8,128)(2,1)}, bf16[2,96,384]{2,1,0:T(8,128)(2,1)}, u32[]{:S(2)}, u32[]{:S(2)}) collective-permute-start(bf16[2,96,384]{2,1,0:T(8,128)(2,1)} %fusion.16.refs_8_), channel_id=1, source_target_pairs={{0,8},{4,12},{8,0},{12,4},{16,24},{20,28},{24,16},{28,20},{1,9},{5... | collective-permute-start | bytes 442376 | tf_op jit(solution)/shard_map/ppermute | solution.py:583
  388.5 1.3 copy-start.26
  388.5 18.5 %collective-permute-start.20 = (bf16[1,384,384]{2,1,0:T(8,128)(2,1)S(1)}, bf16[1,384,384]{2,1,0:T(8,128)(2,1)S(1)}, u32[]{:S(2)}, u32[]{:S(2)}) collective-permute-start(bf16[1,384,384]{2,1,0:T(8,128)(2,1)S(1)} %get-tuple-element.134.refs_6_), channel_id=1, source_target_pairs={{0,16},{4,20},{8,24},{12,28},{16,0},{20,4},{24,8},{28,12},{1,17},{... | collective-permute-start | bytes 884744 | tf_op jit(solution)/shard_map/ppermute | solution.py:583
  390.6 17.2 %copy-start.17 = (bf16[1,384,384]{2,1,0:T(8,128)(2,1)S(1)}, bf16[1,384,384]{2,1,0:T(8,128)(2,1)}, u32[]{:S(2)}) copy-start(bf16[1,384,384]{2,1,0:T(8,128)(2,1)} %get-tuple-element.135.refs_5_) | copy-start | bytes 884740
  407.7 3.5 copy-start.9
  408.9 3.6 copy-start.27
  408.9 3.8 copy-start.32
  408.9 3.8 copy-start.33
  408.9 3.8 copy-start.34
  410.0 3.0 copy-start.5
  410.0 16.0 %collective-permute-start.21 = (bf16[864,384]{1,0:T(8,128)(2,1)S(1)}, bf16[864,384]{1,0:T(8,128)(2,1)}, u32[]{:S(2)}, u32[]{:S(2)}) collective-permute-start(bf16[864,384]{1,0:T(8,128)(2,1)S(1)} %pad_maximum_fusion), channel_id=1, source_target_pairs={{0,2},{1,3},{2,0},{3,1},{4,6},{5,7},{6,4},{7,5},{8,10},{9,11},{10,... | collective-permute-start | bytes 1990664 | tf_op jit(solution)/shard_map/ppermute | solution.py:583
  412.9 0.8 copy-start.21
  413.7 12.3 %copy-start.13 = (bf16[480,384]{1,0:T(8,128)(2,1)S(1)}, bf16[480,384]{1,0:T(8,128)(2,1)}, u32[]{:S(2)}) copy-start(bf16[480,384]{1,0:T(8,128)(2,1)} %reduce-scatter.2.cloned.1.call-done) | copy-start | bytes 1105924
  414.0 23.8 %collective-permute-start.19 = (bf16[4,98,768]{2,0,1:T(4,128)(2,1)S(1)}, bf16[4,98,768]{2,0,1:T(4,128)(2,1)}, u32[]{:S(2)}, u32[]{:S(2)}) collective-permute-start(bf16[4,98,768]{2,0,1:T(4,128)(2,1)S(1)} %copy.104), channel_id=1, source_target_pairs={{0,4},{4,0},{8,12},{12,8},{16,20},{20,16},{24,28},{28,24},{1,5},{5... | collective-permute-start | bytes 1806344 | tf_op jit(solution)/shard_map/ppermute | solution.py:583
  414.4 17.6 %copy-start.28 = (bf16[4,1,2,768]{3,2,1,0:T(2,128)(2,1)S(1)}, bf16[4,1,2,768]{3,2,1,0:T(2,128)(2,1)}, u32[]{:S(2)}) copy-start(bf16[4,1,2,768]{3,2,1,0:T(2,128)(2,1)} %get-tuple-element.155) | copy-start | bytes 36868
  427.3 12.6 %copy-start.3 = (bf16[864,384]{1,0:T(8,128)(2,1)}, bf16[864,384]{1,0:T(8,128)(2,1)S(1)}, u32[]{:S(2)}) copy-start(bf16[864,384]{1,0:T(8,128)(2,1)S(1)} %add_convert_fusion.4.b) | copy-start | bytes 1990660
  427.3 9.0 %copy-start.24 = (bf16[2,1,96,384]{3,2,1,0:T(8,128)(2,1)S(1)}, bf16[2,1,96,384]{3,2,1,0:T(8,128)(2,1)}, u32[]{:S(2)}) copy-start(bf16[2,1,96,384]{3,2,1,0:T(8,128)(2,1)} %add_convert_fusion.19) | copy-start | bytes 442372
  427.3 13.9 %collective-permute-start.23 = (bf16[864,384]{1,0:T(8,128)(2,1)S(1)}, bf16[864,384]{1,0:T(8,128)(2,1)S(1)}, u32[]{:S(2)}, u32[]{:S(2)}) collective-permute-start(bf16[864,384]{1,0:T(8,128)(2,1)S(1)} %add_convert_fusion.4.b), channel_id=1, source_target_pairs={{0,1},{1,0},{2,3},{3,2},{4,5},{5,4},{6,7},{7,6},{8,9},{9,8},{10,11... | collective-permute-start | bytes 1990664 | tf_op jit(solution)/shard_map/ppermute | solution.py:583
  429.8 6.5 %collective-permute-start.26 = (bf16[1,96,384]{2,1,0:T(8,128)(2,1)S(1)}, bf16[1,96,384]{2,1,0:T(8,128)(2,1)S(1)}, u32[]{:S(2)}, u32[]{:S(2)}) collective-permute-start(bf16[1,96,384]{2,1,0:T(8,128)(2,1)S(1)} %fusion.17), channel_id=1, source_target_pairs={{0,16},{4,20},{8,24},{12,28},{16,0},{20,4},{24,8},{28,12},{1,17},{... | collective-permute-start | bytes 221192 | tf_op jit(solution)/shard_map/ppermute | solution.py:583
  439.8 1.4 copy-start.4
  441.1 8.4 %collective-permute-start.22 = (bf16[2,98,768]{2,1,0:T(8,128)(2,1)S(1)}, bf16[2,98,768]{2,1,0:T(8,128)(2,1)S(1)}, u32[]{:S(2)}, u32[]{:S(2)}) collective-permute-start(bf16[2,98,768]{2,1,0:T(8,128)(2,1)S(1)} %get-tuple-element.131), channel_id=1, source_target_pairs={{0,8},{4,12},{8,0},{12,4},{16,24},{20,28},{24,16},{28,20},{1,9},{5... | collective-permute-start | bytes 903176 | tf_op jit(solution)/shard_map/ppermute | solution.py:583
  441.2 0.8 copy-start.8
  450.3 11.4 %copy-start.15 = (bf16[2,98,768]{2,1,0:T(8,128)(2,1)S(1)}, bf16[2,98,768]{2,1,0:T(8,128)(2,1)}, u32[]{:S(2)}) copy-start(bf16[2,98,768]{2,1,0:T(8,128)(2,1)} %tie.14) | copy-start | bytes 903172
  450.3 11.5 %copy-start.20 = (bf16[96,384]{1,0:T(8,128)(2,1)S(1)}, bf16[96,384]{1,0:T(8,128)(2,1)}, u32[]{:S(2)}) copy-start(bf16[96,384]{1,0:T(8,128)(2,1)} %fusion.19) | copy-start | bytes 221188
  451.3 10.4 %collective-permute-start.24 = (bf16[1,98,768]{2,1,0:T(8,128)(2,1)S(1)}, bf16[1,98,768]{2,1,0:T(8,128)(2,1)S(1)}, u32[]{:S(2)}, u32[]{:S(2)}) collective-permute-start(bf16[1,98,768]{2,1,0:T(8,128)(2,1)S(1)} %fusion.8), channel_id=1, source_target_pairs={{0,16},{4,20},{8,24},{12,28},{16,0},{20,4},{24,8},{28,12},{1,17},{... | collective-permute-start | bytes 451592 | tf_op jit(solution)/shard_map/ppermute | solution.py:583
  461.8 6.9 %collective-permute-start.27 = (bf16[98,1152]{1,0:T(8,128)(2,1)S(1)}, bf16[98,1152]{1,0:T(8,128)(2,1)S(1)}, u32[]{:S(2)}, u32[]{:S(2)}) collective-permute-start(bf16[98,1152]{1,0:T(8,128)(2,1)S(1)} %fusion.14), channel_id=1, source_target_pairs={{0,2},{1,3},{2,0},{3,1},{4,6},{5,7},{6,4},{7,5},{8,10},{9,11},{10,... | collective-permute-start | bytes 677384 | tf_op jit(solution)/shard_map/ppermute | solution.py:583
  468.8 4.8 collective-permute-start.28
  (10 other events, 7.6 us)
Sparse Core Ops, SparseCore 0:
  29.9 89.2 all-gather.1
  308.8 80.4 reduce-scatter.1

commit v4 on v3

--- a/solution.py
+++ b/solution.py
@@ -414,7 +414,7 @@
         settle(last_ones)
 
 
-def middle(core, x, mixed, g, mine, other, back_mine, back_other, direct, vec, fb, F=768, T=256):
+def middle(core, x, mixed, g, mine, other, back_mine, back_other, direct, vec, fb, F=768, T=512):
     n, D = x.shape
     FF = fb.shape[1]
     one = pl.Buffered(1)

time: 484 us -> 469 us (0.969); the launches traced: 485 us -> 464 us
  Pallas kernels: 291 us -> 270 us
    pallas_call x1, Pallas kernels: 119 us -> 98.5 us  [middle(): pl.pallas_call(functools.partial(mid_kernel, T, direct), grid=(FF // F,),...]
  transfers between devices with their start and end apart: 31 -> 31, of which waited for: 7 -> 7; matrix products, arithmetic and copies ran while one was open for 17% -> 18% of each run, Pallas kernels for 35% -> 37%
where the time goes in v4:
time: 469 us; the launch traced here: 464 us
  Pallas kernels  270 us (58%)
  local copies, waits for them, and re-layouts  52.1 us (11%)
  other arithmetic  45.9 us (10%)
  waiting for transfers between devices  44.8 us (10%)
  starting transfers between devices  36.3 us (8%)
  between operations  15.1 us (3%)
    pallas_call x1, Pallas kernels, middle(): pl.pallas_call(functools.partial(mid_kernel, T, direct), grid=(FF // F,),...  98.5 us
    pallas_call x3, Pallas kernels, attn_bwd(): pl.pallas_call(kernel, grid=(pairs, rows), in_specs=[pl.BlockSpec(memory_...  92.6 us
    pallas_call x3, Pallas kernels, attn_fwd(): pl.pallas_call(kernel, grid=(rows, pairs), in_specs=[pl.BlockSpec((length...  43.8 us
    ppermute x29, waiting for transfers between devices, swap(): return lax.ppermute(x, axis, [(i, i ^ mask) for i in range(size)])  40.3 us
    ppermute x29, starting transfers between devices, swap(): return lax.ppermute(x, axis, [(i, i ^ mask) for i in range(size)])  36.2 us
    convert_element_type x15, other arithmetic, add(): return total.astype(BF)  23.6 us
    unnamed x112, local copies, waits for them, and re-layouts  23.4 us
    pallas_call x2, Pallas kernels, project(): pl.pallas_call(functools.partial(project_kernel, order, rows, half), grid...  18.3 us
  transfers between devices with their start and end apart: 31, of which 7 were waited for; matrix products, arithmetic and copies ran while one was open for 18% of the time, Pallas kernels for 37%

profile of v4, /device:TPU:1, one launch (start us, length us, event | category | flops | bytes accessed | tf_op | source)
XLA Modules:
  0.0 463.7 jit_solution(4440145323493919658)
XLA Ops:
  7.2 1.5 reshape.401
  10.4 2.1 collective-permute-start
  12.5 2.3 collective-permute-start.1
  15.9 3.2 collective-permute-start.6
  19.8 2.1 fusion.26
  21.9 1.7 dynamic-slice_dynamic-update-slice_fusion
  23.6 1.6 dynamic-slice_dynamic-update-slice_fusion.4
  25.1 1.5 dynamic-slice_dynamic-update-slice_fusion.3
  26.7 1.5 dynamic-slice_dynamic-update-slice_fusion.2
  28.2 1.5 dynamic-slice_dynamic-update-slice_fusion.1
  33.5 1.1 pad_maximum_fusion.4
  34.5 1.3 collective-permute-start.3
  35.8 1.5 constant_dynamic-update-slice_fusion.3
  37.3 1.5 constant_dynamic-update-slice_fusion.2
  38.9 1.6 constant_dynamic-update-slice_fusion.1
  40.5 1.8 pad_maximum_fusion.3
  46.3 9.3 %collective-permute-start.4 = (bf16[8,112,384]{2,1,0:T(8,128)(2,1)}, bf16[8,112,384]{2,1,0:T(8,128)(2,1)}, u32[]{:S(2)}, u32[]{:S(2)}) collective-permute-start(bf16[8,112,384]{2,1,0:T(8,128)(2,1)} %constant_dynamic-update-slice_fusion.mine), channel_id=1, source_target_pairs={{0,1},{1,0},{2,3},{3,2},{4,5},{5,4},{6,7},{7,6},{8,9},{9,8},{10,11... | collective-permute-start | bytes 2064392 | tf_op jit(solution)/shard_map/ppermute | solution.py:583
  58.1 3.2 add_convert_fusion.n1
  61.2 1.2 collective-permute-done.8
  62.5 1.1 constant_dynamic-update-slice_fusion.5.mine
  63.6 2.5 collective-permute-start.9
  66.1 7.6 %project.2 = (bf16[2048,768]{1,0:T(8,128)(2,1)}, bf16[768,768]{1,0:T(8,128)(2,1)}) custom-call(s32[2]{0:T(128)} %pad_add_fusion.at, bf16[2048,768]{1,0:T(8,128)(2,1)} %add_convert_fusion.n1, bf16[8,112,384]{2,1,0:T(8,128)(2,1)} %constant_dynamic-update-slice_fusion.mine, bf16[8,112,384]{2,1,0:T(8,128)(2,1)} %collective-permute-done.4.other, ...), custom_call_target="tpu_custom_call" | custom-call | flops 4831838208 | bytes 9437184 | tf_op jit(solution)/shard_map/project/pallas_call | solution.py:553
  73.7 14.6 %attention_forward.3 = (bf16[2048,256]{1,0:T(8,128)(2,1)}, bf16[2048,256]{1,0:T(8,128)(2,1)}) custom-call(bf16[2048,768]{1,0:T(8,128)(2,1)} %get-tuple-element.45.x_ref.x), custom_call_target="tpu_custom_call" | custom-call | flops 16106127360 | bytes 5242880 | tf_op jit(solution)/shard_map/attention_forward/pallas_call | solution.py:74
  88.3 1.1 copy-done.41
  89.4 10.7 %project.3 = (bf16[2048,1536]{1,0:T(8,128)(2,1)}, bf16[768,1536]{1,0:T(8,128)(2,1)}) custom-call(s32[2]{0:T(128)} %pad_add_fusion.at, bf16[2048,768]{1,0:T(8,128)(2,1)} %add_convert_fusion.n1, bf16[8,96,768]{2,1,0:T(8,128)(2,1)} %copy-done.31, bf16[8,96,768]{2,1,0:T(8,128)(2,1)} %copy-done.41, f32[1,1536]{1,0:T(1,128)} %slice.305.bias, ...), custom_call_target="tpu_custom_call" | custom-call | flops 9663676416 | bytes 12582912 | tf_op jit(solution)/shard_map/project/pallas_call | solution.py:553
  100.1 14.6 %attention_forward.4 = (bf16[2048,256]{1,0:T(8,128)(2,1)}, bf16[2048,256]{1,0:T(8,128)(2,1)}) custom-call(bf16[2048,1536]{1,0:T(8,128)(2,1)} %get-tuple-element.47.x_ref.x), custom_call_target="tpu_custom_call" | custom-call | flops 16106127360 | bytes 5242880 | tf_op jit(solution)/shard_map/attention_forward/pallas_call | solution.py:74
  114.8 4.4 all-gather.2.cloned.1.call-done.a
  119.2 1.5 collective-permute-start.10
  120.8 4.4 multiply_convert_fusion
  126.2 2.9 copy.89.t
  130.4 14.6 %attention_forward.5 = (bf16[2048,256]{1,0:T(8,128)(2,1)}, bf16[2048,256]{1,0:T(8,128)(2,1)}) custom-call(bf16[2048,1536]{1,0:T(8,128)(2,1)} %get-tuple-element.47.x_ref.x, bf16[768,3456]{1,0:T(8,128)(2,1)} %tie.8.refs_0_.mine.back_mine), custom_call_target="tpu_custom_call" | custom-call | flops 16106127360 | bytes 5242880 | tf_op jit(solution)/shard_map/attention_forward/pallas_call | solution.py:74
  144.9 98.5 %feed_forward.1 = (bf16[2048,768]{1,0:T(8,128)(2,1)}, f32[2048,768]{1,0:T(8,128)}, bf16[2048,768]{1,0:T(8,128)(2,1)}, bf16[8,480,384]{2,1,0:T(8,128)(2,1)}, bf16...) custom-call(s32[1]{0:T(128)} %bitcast.at, ...), custom_call_target="tpu_custom_call" | custom-call | flops 115964116992 | bytes 53477376 | tf_op jit(solution)/shard_map/feed_forward/pallas_call | solution.py:428
  244.3 30.8 %attention_backward.3 = (bf16[2048,768]{1,0:T(8,128)(2,1)}, bf16[768,384]{1,0:T(8,128)(2,1)}, bf16[768,384]{1,0:T(8,128)(2,1)}, f32[8,768]{1,0:T(8,128)}) custom-call(s32[1]{0:T(128)} %bitcast.at, bf16[2048,1536]{1,0:T(8,128)(2,1)} %get-tuple-element.47.x_ref.x, bf16[2048,256]{1,0:T(8,128)(2,1)} %get-tuple-element.49.m2_any.o, ...), custom_call_target="tpu_custom_call" | custom-call | flops 30064771072 | bytes 9437184 | tf_op jit(solution)/shard_map/attention_backward/pallas_call | solution.py:176
  280.6 4.5 add_convert_fusion.3
  285.4 2.4 add_convert_fusion.1.refs_0_
  287.8 30.8 %attention_backward.4 = (bf16[2048,768]{1,0:T(8,128)(2,1)}, bf16[768,384]{1,0:T(8,128)(2,1)}, bf16[768,384]{1,0:T(8,128)(2,1)}, f32[8,768]{1,0:T(8,128)}) custom-call(s32[1]{0:T(128)} %bitcast.at, bf16[2048,1536]{1,0:T(8,128)(2,1)} %get-tuple-element.47.x_ref.x, bf16[2048,256]{1,0:T(8,128)(2,1)} %get-tuple-element.48.b.m1_any.o, ...), custom_call_target="tpu_custom_call" | custom-call | flops 30064771072 | bytes 9437184 | tf_op jit(solution)/shard_map/attention_backward/pallas_call | solution.py:176
  320.7 2.2 fusion.10
  322.8 1.2 collective-permute-start.16
  324.1 2.4 fusion.3
  327.3 31.0 %attention_backward.5 = (bf16[2048,768]{1,0:T(8,128)(2,1)}, bf16[768,384]{1,0:T(8,128)(2,1)}, bf16[768,384]{1,0:T(8,128)(2,1)}, f32[8,768]{1,0:T(8,128)}) custom-call(s32[1]{0:T(128)} %bitcast.at, bf16[2048,768]{1,0:T(8,128)(2,1)} %get-tuple-element.45.x_ref.x, bf16[2048,256]{1,0:T(8,128)(2,1)} %get-tuple-element.46.refs_0_.m0_any.o, ...), custom_call_target="tpu_custom_call" | custom-call | flops 30064771072 | bytes 9437184 | tf_op jit(solution)/shard_map/attention_backward/pallas_call | solution.py:176
  360.5 1.7 fusion.16.refs_8_
  363.1 1.6 add_convert_fusion.19
  365.5 1.9 fusion.4
  367.5 1.3 collective-permute-start.20
  369.5 16.4 %input_gradient.1 = (f32[2048,768]{1,0:T(8,128)}, f32[2,768]{1,0:T(2,128)}) custom-call(bf16[2048,768]{1,0:T(8,128)(2,1)} %bitcast.142, f32[2048,768]{1,0:T(8,128)} %get-tuple-element.51.gh_ref, f32[1,768]{1,0:T(1,128)} %slice.253.gain_ref, bf16[2048,768]{1,0:T(8,128)(2,1)} %get-tuple-element.63.refs_0_, bf16[2048,768]{1,0:T(8,128)(2,1)} %get-tuple-element.64.refs_1_, ...), custom_call_target="tpu_custom_call" | custom-call | flops 14495514624 | bytes 25165824 | tf_op jit(solution)/shard_map/input_gradient/pallas_call | solution.py:505
  386.7 1.1 fusion.13
  388.9 1.3 collective-permute-start.21
  390.2 1.2 add_convert_fusion.13
  393.4 11.6 %collective-permute-done.21 = bf16[864,384]{1,0:T(8,128)(2,1)} collective-permute-done((bf16[864,384]{1,0:T(8,128)(2,1)S(1)}, bf16[864,384]{1,0:T(8,128)(2,1)}, u32[]{:S(2)}, u32[]{:S(2)}) %collective-permute-start.21) | collective-permute-done | bytes 663584 | tf_op jit(solution)/shard_map/ppermute | solution.py:583
  405.0 1.3 add_convert_fusion.4.b
  406.2 1.5 collective-permute-start.23
  408.7 1.2 collective-permute-start.26
  411.0 4.2 collective-permute-done.26
  415.2 1.5 fusion.19
  416.8 2.0 copy.105.a
  418.8 1.3 add_convert_fusion.8
  421.1 7.4 %collective-permute-done.22.a = bf16[2,98,768]{2,1,0:T(8,128)(2,1)S(1)} collective-permute-done((bf16[2,98,768]{2,1,0:T(8,128)(2,1)S(1)}, bf16[2,98,768]{2,1,0:T(8,128)(2,1)S(1)}, u32[]{:S(2)}, u32[]{:S(2)}) %collective-permute-start.22) | collective-permute-done | bytes 301088 | tf_op jit(solution)/shard_map/ppermute | solution.py:583
  430.5 10.1 %collective-permute-done.24 = bf16[1,98,768]{2,1,0:T(8,128)(2,1)S(1)} collective-permute-done((bf16[1,98,768]{2,1,0:T(8,128)(2,1)S(1)}, bf16[1,98,768]{2,1,0:T(8,128)(2,1)S(1)}, u32[]{:S(2)}, u32[]{:S(2)}) %collective-permute-start.24) | collective-permute-done | bytes 150560 | tf_op jit(solution)/shard_map/ppermute | solution.py:583
  440.7 1.2 collective-permute-start.27
  442.0 5.7 %collective-permute-done.27 = bf16[98,1152]{1,0:T(8,128)(2,1)S(1)} collective-permute-done((bf16[98,1152]{1,0:T(8,128)(2,1)S(1)}, bf16[98,1152]{1,0:T(8,128)(2,1)S(1)}, u32[]{:S(2)}, u32[]{:S(2)}) %collective-permute-start.27) | collective-permute-done | bytes 225824 | tf_op jit(solution)/shard_map/ppermute | solution.py:583
  447.7 1.5 collective-permute-start.28
  449.3 1.4 copy.110
  450.6 1.1 convert_element_type.549
  455.6 1.1 reshape.425
  (269 shorter events, 42.7 us)
Async XLA Ops:
  7.2 112.0 %all-gather.2.cloned.1.call-start = ((), (), s32[]{:S(2)}) async-start(), calls=%async_computation.1 | async-start | bytes 5971968 | tf_op jit(solution)/shard_map/all_gather | solution.py:692
  9.0 10.1 %copy-start.29 = (bf16[96,768]{1,0:T(8,128)(2,1)S(1)}, bf16[96,768]{1,0:T(8,128)(2,1)}, u32[]{:S(2)}) copy-start(bf16[96,768]{1,0:T(8,128)(2,1)} %param.18) | copy-start | bytes 442372
  10.4 23.1 %collective-permute-start = (bf16[1,112,384]{2,1,0:T(8,128)(2,1)}, bf16[1,112,384]{2,1,0:T(8,128)(2,1)}, u32[]{:S(2)}, u32[]{:S(2)}) collective-permute-start(bf16[1,112,384]{2,1,0:T(8,128)(2,1)} %maximum_bitcast_fusion), channel_id=1, source_target_pairs={{0,8},{4,12},{8,0},{12,4},{16,24},{20,28},{24,16},{28,20},{1,9},{5... | collective-permute-start | bytes 258056 | tf_op jit(solution)/shard_map/ppermute | solution.py:583
  12.5 21.0 %collective-permute-start.1 = (bf16[1,112,384]{2,1,0:T(8,128)(2,1)}, bf16[1,112,384]{2,1,0:T(8,128)(2,1)}, u32[]{:S(2)}, u32[]{:S(2)}) collective-permute-start(bf16[1,112,384]{2,1,0:T(8,128)(2,1)} %maximum_bitcast_fusion), channel_id=1, source_target_pairs={{0,16},{4,20},{8,24},{12,28},{16,0},{20,4},{24,8},{28,12},{1,17},{... | collective-permute-start | bytes 258056 | tf_op jit(solution)/shard_map/ppermute | solution.py:583
  14.8 18.7 %collective-permute-start.2 = (bf16[1,112,384]{2,1,0:T(8,128)(2,1)}, bf16[1,112,384]{2,1,0:T(8,128)(2,1)}, u32[]{:S(2)}, u32[]{:S(2)}) collective-permute-start(bf16[1,112,384]{2,1,0:T(8,128)(2,1)} %maximum_bitcast_fusion), channel_id=1, source_target_pairs={{0,24},{4,28},{8,16},{12,20},{16,8},{20,12},{24,0},{28,4},{1,25},{... | collective-permute-start | bytes 258056 | tf_op jit(solution)/shard_map/ppermute | solution.py:583
  15.6 24.9 %collective-permute-start.5 = (bf16[1,96,768]{2,1,0:T(8,128)(2,1)}, bf16[1,96,768]{2,1,0:T(8,128)(2,1)S(1)}, u32[]{:S(2)}, u32[]{:S(2)}) collective-permute-start(bf16[1,96,768]{2,1,0:T(8,128)(2,1)} %get-tuple-element.123), channel_id=1, source_target_pairs={{0,8},{4,12},{8,0},{12,4},{16,24},{20,28},{24,16},{28,20},{1,9},{5... | collective-permute-start | bytes 442376 | tf_op jit(solution)/shard_map/ppermute | solution.py:583
  15.9 24.5 %collective-permute-start.6 = (bf16[1,96,768]{2,1,0:T(8,128)(2,1)}, bf16[1,96,768]{2,1,0:T(8,128)(2,1)S(1)}, u32[]{:S(2)}, u32[]{:S(2)}) collective-permute-start(bf16[1,96,768]{2,1,0:T(8,128)(2,1)} %get-tuple-element.123), channel_id=1, source_target_pairs={{0,16},{4,20},{8,24},{12,28},{16,0},{20,4},{24,8},{28,12},{1,17},{... | collective-permute-start | bytes 442376 | tf_op jit(solution)/shard_map/ppermute | solution.py:583
  19.8 10.1 %copy-start = (s32[8]{0:T(128)S(1)}, s32[8]{0:T(128)}, u32[]{:S(2)}) copy-start(s32[8]{0:T(128)} %constant.176) | copy-start | bytes 100
  19.8 11.5 %copy-start.1 = (bf16[2,1024,768]{2,1,0:T(8,128)(2,1)S(1)}, bf16[2,1024,768]{2,1,0:T(8,128)(2,1)}, u32[]{:S(2)}) copy-start(bf16[2,1024,768]{2,1,0:T(8,128)(2,1)} %param.13) | copy-start | bytes 9437188
  29.8 358.1 %reduce-scatter.2.cloned.1.call-start = ((), (), s32[]{:S(2)}) async-start(), calls=%async_computation.2 | async-start | bytes 3317760 | tf_op jit(solution)/shard_map/reduce_scatter | solution.py:745
  33.4 7.0 %collective-permute-start.7 = (bf16[1,96,768]{2,1,0:T(8,128)(2,1)}, bf16[1,96,768]{2,1,0:T(8,128)(2,1)S(1)}, u32[]{:S(2)}, u32[]{:S(2)}) collective-permute-start(bf16[1,96,768]{2,1,0:T(8,128)(2,1)} %get-tuple-element.123), channel_id=1, source_target_pairs={{0,24},{4,28},{8,16},{12,20},{16,8},{20,12},{24,0},{28,4},{1,25},{... | collective-permute-start | bytes 442376 | tf_op jit(solution)/shard_map/ppermute | solution.py:583
  34.5 10.0 %collective-permute-start.3 = (bf16[4,112,384]{2,1,0:T(8,128)(2,1)S(1)}, bf16[4,112,384]{2,1,0:T(8,128)(2,1)S(1)}, u32[]{:S(2)}, u32[]{:S(2)}) collective-permute-start(bf16[4,112,384]{2,1,0:T(8,128)(2,1)S(1)} %pad_maximum_fusion.4), channel_id=1, source_target_pairs={{0,4},{4,0},{8,12},{12,8},{16,20},{20,16},{24,28},{28,24},{1,5},{5... | collective-permute-start | bytes 1032200 | tf_op jit(solution)/shard_map/ppermute | solution.py:583
  42.3 20.2 %collective-permute-start.8 = (bf16[4,96,768]{2,1,0:T(8,128)(2,1)}, bf16[4,96,768]{2,1,0:T(8,128)(2,1)}, u32[]{:S(2)}, u32[]{:S(2)}) collective-permute-start(bf16[4,96,768]{2,1,0:T(8,128)(2,1)} %pad_maximum_fusion.3), channel_id=1, source_target_pairs={{0,4},{4,0},{8,12},{12,8},{16,20},{20,16},{24,28},{28,24},{1,5},{5... | collective-permute-start | bytes 1769480 | tf_op jit(solution)/shard_map/ppermute | solution.py:583
  46.3 19.9 %collective-permute-start.4 = (bf16[8,112,384]{2,1,0:T(8,128)(2,1)}, bf16[8,112,384]{2,1,0:T(8,128)(2,1)}, u32[]{:S(2)}, u32[]{:S(2)}) collective-permute-start(bf16[8,112,384]{2,1,0:T(8,128)(2,1)} %constant_dynamic-update-slice_fusion.mine), channel_id=1, source_target_pairs={{0,1},{1,0},{2,3},{3,2},{4,5},{5,4},{6,7},{7,6},{8,9},{9,8},{10,11... | collective-permute-start | bytes 2064392 | tf_op jit(solution)/shard_map/ppermute | solution.py:583
  58.1 4.4 copy-start.30
  63.6 10.2 %copy-start.31 = (bf16[8,96,768]{2,1,0:T(8,128)(2,1)}, bf16[8,96,768]{2,1,0:T(8,128)(2,1)S(1)}, u32[]{:S(2)}) copy-start(bf16[8,96,768]{2,1,0:T(8,128)(2,1)S(1)} %constant_dynamic-update-slice_fusion.5.mine) | copy-start | bytes 3538948
  63.6 24.8 %collective-permute-start.9 = (bf16[8,96,768]{2,1,0:T(8,128)(2,1)S(1)}, bf16[8,96,768]{2,1,0:T(8,128)(2,1)S(1)}, u32[]{:S(2)}, u32[]{:S(2)}) collective-permute-start(bf16[8,96,768]{2,1,0:T(8,128)(2,1)S(1)} %constant_dynamic-update-slice_fusion.5.mine), channel_id=1, source_target_pairs={{0,1},{1,0},{2,3},{3,2},{4,5},{5,4},{6,7},{7,6},{8,9},{9,8},{10,11... | collective-permute-start | bytes 3538952 | tf_op jit(solution)/shard_map/ppermute | solution.py:583
  88.3 1.1 copy-start.41
  119.2 1.5 copy-start.42
  119.2 1.5 copy-start.35
  119.2 25.8 %collective-permute-start.10 = (bf16[768,3456]{1,0:T(8,128)(2,1)}, bf16[768,3456]{1,0:T(8,128)(2,1)}, u32[]{:S(2)}, u32[]{:S(2)}) collective-permute-start(bf16[768,3456]{1,0:T(8,128)(2,1)} %tie.8.refs_0_.mine.back_mine), channel_id=1, source_target_pairs={{0,1},{1,0},{2,3},{3,2},{4,5},{5,4},{6,7},{7,6},{8,9},{9,8},{10,11... | collective-permute-start | bytes 15925256 | tf_op jit(solution)/shard_map/ppermute | solution.py:583
  120.8 5.4 %copy-start.2 = (bf16[2048,768]{1,0:T(8,128)(2,1)S(1)}, bf16[2048,768]{1,0:T(8,128)(2,1)}, u32[]{:S(2)}) copy-start(bf16[2048,768]{1,0:T(8,128)(2,1)} %add_convert_fusion.n1) | copy-start | bytes 9437188
  243.5 41.9 %collective-permute-start.14 = (bf16[8,480,384]{2,1,0:T(8,128)(2,1)}, bf16[8,480,384]{2,1,0:T(8,128)(2,1)S(1)}, u32[]{:S(2)}, u32[]{:S(2)}) collective-permute-start(bf16[8,480,384]{2,1,0:T(8,128)(2,1)} %get-tuple-element.61), channel_id=1, source_target_pairs={{0,1},{1,0},{2,3},{3,2},{4,5},{5,4},{6,7},{7,6},{8,9},{9,8},{10,11... | collective-permute-start | bytes 8847368 | tf_op jit(solution)/shard_map/ppermute | solution.py:583
  244.3 36.3 %collective-permute-start.11 = (bf16[8,384,384]{2,1,0:T(8,128)(2,1)}, bf16[8,384,384]{2,1,0:T(8,128)(2,1)}, u32[]{:S(2)}, u32[]{:S(2)}) collective-permute-start(bf16[8,384,384]{2,1,0:T(8,128)(2,1)} %get-tuple-element.55), channel_id=1, source_target_pairs={{0,1},{1,0},{2,3},{3,2},{4,5},{5,4},{6,7},{7,6},{8,9},{9,8},{10,11... | collective-permute-start | bytes 7077896 | tf_op jit(solution)/shard_map/ppermute | solution.py:583
  275.1 44.7 %collective-permute-start.13 = (bf16[768,384]{1,0:T(8,128)(2,1)}, bf16[768,384]{1,0:T(8,128)(2,1)S(1)}, u32[]{:S(2)}, u32[]{:S(2)}) collective-permute-start(bf16[768,384]{1,0:T(8,128)(2,1)} %get-tuple-element.58), channel_id=1, source_target_pairs={{0,1},{1,0},{2,3},{3,2},{4,5},{5,4},{6,7},{7,6},{8,9},{9,8},{10,11... | collective-permute-start | bytes 1769480 | tf_op jit(solution)/shard_map/ppermute | solution.py:583
  280.6 4.8 %copy-start.7 = (bf16[8,480,384]{2,1,0:T(8,128)(2,1)S(1)}, bf16[8,480,384]{2,1,0:T(8,128)(2,1)}, u32[]{:S(2)}) copy-start(bf16[8,480,384]{2,1,0:T(8,128)(2,1)} %get-tuple-element.60) | copy-start | bytes 8847364
  285.1 39.0 %collective-permute-start.12 = (bf16[4,384,384]{2,1,0:T(8,128)(2,1)}, bf16[4,384,384]{2,1,0:T(8,128)(2,1)}, u32[]{:S(2)}, u32[]{:S(2)}) collective-permute-start(bf16[4,384,384]{2,1,0:T(8,128)(2,1)} %get-tuple-element.125.refs_3_), channel_id=1, source_target_pairs={{0,4},{4,0},{8,12},{12,8},{16,20},{20,16},{24,28},{28,24},{1,5},{5... | collective-permute-start | bytes 3538952 | tf_op jit(solution)/shard_map/ppermute | solution.py:583
  318.6 2.0 copy-start.23
  318.6 50.1 %collective-permute-start.17 = (bf16[768,384]{1,0:T(8,128)(2,1)}, bf16[768,384]{1,0:T(8,128)(2,1)S(1)}, u32[]{:S(2)}, u32[]{:S(2)}) collective-permute-start(bf16[768,384]{1,0:T(8,128)(2,1)} %get-tuple-element.69), channel_id=1, source_target_pairs={{0,1},{1,0},{2,3},{3,2},{4,5},{5,4},{6,7},{7,6},{8,9},{9,8},{10,11... | collective-permute-start | bytes 1769480 | tf_op jit(solution)/shard_map/ppermute | solution.py:583
  319.8 0.8 copy-start.10
  320.7 3.4 copy-start.6
  322.8 37.0 %collective-permute-start.16 = (bf16[4,96,384]{2,1,0:T(8,128)(2,1)}, bf16[4,96,384]{2,1,0:T(8,128)(2,1)S(1)}, u32[]{:S(2)}, u32[]{:S(2)}) collective-permute-start(bf16[4,96,384]{2,1,0:T(8,128)(2,1)} %get-tuple-element.136.refs_3_), channel_id=1, source_target_pairs={{0,4},{4,0},{8,12},{12,8},{16,20},{20,16},{24,28},{28,24},{1,5},{5... | collective-permute-start | bytes 884744 | tf_op jit(solution)/shard_map/ppermute | solution.py:583
  326.5 38.3 %collective-permute-start.15 = (bf16[2,384,384]{2,1,0:T(8,128)(2,1)S(1)}, bf16[2,384,384]{2,1,0:T(8,128)(2,1)S(1)}, u32[]{:S(2)}, u32[]{:S(2)}) collective-permute-start(bf16[2,384,384]{2,1,0:T(8,128)(2,1)S(1)} %get-tuple-element.126.refs_1_), channel_id=1, source_target_pairs={{0,8},{4,12},{8,0},{12,4},{16,24},{20,28},{24,16},{28,20},{1,9},{5... | collective-permute-start | bytes 1769480 | tf_op jit(solution)/shard_map/ppermute | solution.py:583
  327.3 32.3 %copy-start.36 = (bf16[2,3,128]{2,1,0:T(4,128)(2,1)S(1)}, bf16[2,3,128]{2,1,0:T(4,128)(2,1)}, u32[]{:S(2)}) copy-start(bf16[2,3,128]{2,1,0:T(4,128)(2,1)} %concatenate.82) | copy-start | bytes 4612
  358.2 2.3 copy-start.18
  358.2 33.6 %collective-permute-start.18 = (bf16[768,384]{1,0:T(8,128)(2,1)}, bf16[768,384]{1,0:T(8,128)(2,1)S(1)}, u32[]{:S(2)}, u32[]{:S(2)}) collective-permute-start(bf16[768,384]{1,0:T(8,128)(2,1)} %get-tuple-element.71), channel_id=1, source_target_pairs={{0,1},{1,0},{2,3},{3,2},{4,5},{5,4},{6,7},{7,6},{8,9},{9,8},{10,11... | collective-permute-start | bytes 1769480 | tf_op jit(solution)/shard_map/ppermute | solution.py:583
  360.5 5.0 %copy-start.12 = (bf16[2,1,384,384]{3,2,1,0:T(8,128)(2,1)S(1)}, bf16[2,1,384,384]{3,2,1,0:T(8,128)(2,1)}, u32[]{:S(2)}) copy-start(bf16[2,1,384,384]{3,2,1,0:T(8,128)(2,1)} %get-tuple-element.127) | copy-start | bytes 1769476
  362.2 31.2 %collective-permute-start.25 = (bf16[2,96,384]{2,1,0:T(8,128)(2,1)}, bf16[2,96,384]{2,1,0:T(8,128)(2,1)}, u32[]{:S(2)}, u32[]{:S(2)}) collective-permute-start(bf16[2,96,384]{2,1,0:T(8,128)(2,1)} %fusion.16.refs_8_), channel_id=1, source_target_pairs={{0,8},{4,12},{8,0},{12,4},{16,24},{20,28},{24,16},{28,20},{1,9},{5... | collective-permute-start | bytes 442376 | tf_op jit(solution)/shard_map/ppermute | solution.py:583
  367.5 1.3 copy-start.26
  367.5 18.5 %collective-permute-start.20 = (bf16[1,384,384]{2,1,0:T(8,128)(2,1)S(1)}, bf16[1,384,384]{2,1,0:T(8,128)(2,1)S(1)}, u32[]{:S(2)}, u32[]{:S(2)}) collective-permute-start(bf16[1,384,384]{2,1,0:T(8,128)(2,1)S(1)} %get-tuple-element.134.refs_6_), channel_id=1, source_target_pairs={{0,16},{4,20},{8,24},{12,28},{16,0},{20,4},{24,8},{28,12},{1,17},{... | collective-permute-start | bytes 884744 | tf_op jit(solution)/shard_map/ppermute | solution.py:583
  369.5 17.1 %copy-start.17 = (bf16[1,384,384]{2,1,0:T(8,128)(2,1)S(1)}, bf16[1,384,384]{2,1,0:T(8,128)(2,1)}, u32[]{:S(2)}) copy-start(bf16[1,384,384]{2,1,0:T(8,128)(2,1)} %get-tuple-element.135.refs_5_) | copy-start | bytes 884740
  386.7 3.5 copy-start.9
  387.8 3.6 copy-start.27
  387.8 3.8 copy-start.32
  387.8 3.8 copy-start.33
  387.8 3.8 copy-start.34
  388.9 2.9 copy-start.5
  388.9 16.0 %collective-permute-start.21 = (bf16[864,384]{1,0:T(8,128)(2,1)S(1)}, bf16[864,384]{1,0:T(8,128)(2,1)}, u32[]{:S(2)}, u32[]{:S(2)}) collective-permute-start(bf16[864,384]{1,0:T(8,128)(2,1)S(1)} %pad_maximum_fusion), channel_id=1, source_target_pairs={{0,2},{1,3},{2,0},{3,1},{4,6},{5,7},{6,4},{7,5},{8,10},{9,11},{10,... | collective-permute-start | bytes 1990664 | tf_op jit(solution)/shard_map/ppermute | solution.py:583
  391.8 0.8 copy-start.21
  392.7 12.3 %copy-start.13 = (bf16[480,384]{1,0:T(8,128)(2,1)S(1)}, bf16[480,384]{1,0:T(8,128)(2,1)}, u32[]{:S(2)}) copy-start(bf16[480,384]{1,0:T(8,128)(2,1)} %reduce-scatter.2.cloned.1.call-done) | copy-start | bytes 1105924
  393.0 23.8 %collective-permute-start.19 = (bf16[4,98,768]{2,0,1:T(4,128)(2,1)S(1)}, bf16[4,98,768]{2,0,1:T(4,128)(2,1)}, u32[]{:S(2)}, u32[]{:S(2)}) collective-permute-start(bf16[4,98,768]{2,0,1:T(4,128)(2,1)S(1)} %copy.104), channel_id=1, source_target_pairs={{0,4},{4,0},{8,12},{12,8},{16,20},{20,16},{24,28},{28,24},{1,5},{5... | collective-permute-start | bytes 1806344 | tf_op jit(solution)/shard_map/ppermute | solution.py:583
  393.4 17.6 %copy-start.28 = (bf16[4,1,2,768]{3,2,1,0:T(2,128)(2,1)S(1)}, bf16[4,1,2,768]{3,2,1,0:T(2,128)(2,1)}, u32[]{:S(2)}) copy-start(bf16[4,1,2,768]{3,2,1,0:T(2,128)(2,1)} %get-tuple-element.155) | copy-start | bytes 36868
  406.2 12.5 %copy-start.3 = (bf16[864,384]{1,0:T(8,128)(2,1)}, bf16[864,384]{1,0:T(8,128)(2,1)S(1)}, u32[]{:S(2)}) copy-start(bf16[864,384]{1,0:T(8,128)(2,1)S(1)} %add_convert_fusion.4.b) | copy-start | bytes 1990660
  406.2 9.0 %copy-start.24 = (bf16[2,1,96,384]{3,2,1,0:T(8,128)(2,1)S(1)}, bf16[2,1,96,384]{3,2,1,0:T(8,128)(2,1)}, u32[]{:S(2)}) copy-start(bf16[2,1,96,384]{3,2,1,0:T(8,128)(2,1)} %add_convert_fusion.19) | copy-start | bytes 442372
  406.2 13.9 %collective-permute-start.23 = (bf16[864,384]{1,0:T(8,128)(2,1)S(1)}, bf16[864,384]{1,0:T(8,128)(2,1)S(1)}, u32[]{:S(2)}, u32[]{:S(2)}) collective-permute-start(bf16[864,384]{1,0:T(8,128)(2,1)S(1)} %add_convert_fusion.4.b), channel_id=1, source_target_pairs={{0,1},{1,0},{2,3},{3,2},{4,5},{5,4},{6,7},{7,6},{8,9},{9,8},{10,11... | collective-permute-start | bytes 1990664 | tf_op jit(solution)/shard_map/ppermute | solution.py:583
  408.7 6.5 %collective-permute-start.26 = (bf16[1,96,384]{2,1,0:T(8,128)(2,1)S(1)}, bf16[1,96,384]{2,1,0:T(8,128)(2,1)S(1)}, u32[]{:S(2)}, u32[]{:S(2)}) collective-permute-start(bf16[1,96,384]{2,1,0:T(8,128)(2,1)S(1)} %fusion.17), channel_id=1, source_target_pairs={{0,16},{4,20},{8,24},{12,28},{16,0},{20,4},{24,8},{28,12},{1,17},{... | collective-permute-start | bytes 221192 | tf_op jit(solution)/shard_map/ppermute | solution.py:583
  418.8 1.4 copy-start.4
  420.1 8.4 %collective-permute-start.22 = (bf16[2,98,768]{2,1,0:T(8,128)(2,1)S(1)}, bf16[2,98,768]{2,1,0:T(8,128)(2,1)S(1)}, u32[]{:S(2)}, u32[]{:S(2)}) collective-permute-start(bf16[2,98,768]{2,1,0:T(8,128)(2,1)S(1)} %get-tuple-element.131), channel_id=1, source_target_pairs={{0,8},{4,12},{8,0},{12,4},{16,24},{20,28},{24,16},{28,20},{1,9},{5... | collective-permute-start | bytes 903176 | tf_op jit(solution)/shard_map/ppermute | solution.py:583
  420.2 0.8 copy-start.8
  429.2 11.4 %copy-start.15 = (bf16[2,98,768]{2,1,0:T(8,128)(2,1)S(1)}, bf16[2,98,768]{2,1,0:T(8,128)(2,1)}, u32[]{:S(2)}) copy-start(bf16[2,98,768]{2,1,0:T(8,128)(2,1)} %tie.14) | copy-start | bytes 903172
  429.2 11.5 %copy-start.20 = (bf16[96,384]{1,0:T(8,128)(2,1)S(1)}, bf16[96,384]{1,0:T(8,128)(2,1)}, u32[]{:S(2)}) copy-start(bf16[96,384]{1,0:T(8,128)(2,1)} %fusion.19) | copy-start | bytes 221188
  430.3 10.4 %collective-permute-start.24 = (bf16[1,98,768]{2,1,0:T(8,128)(2,1)S(1)}, bf16[1,98,768]{2,1,0:T(8,128)(2,1)S(1)}, u32[]{:S(2)}, u32[]{:S(2)}) collective-permute-start(bf16[1,98,768]{2,1,0:T(8,128)(2,1)S(1)} %fusion.8), channel_id=1, source_target_pairs={{0,16},{4,20},{8,24},{12,28},{16,0},{20,4},{24,8},{28,12},{1,17},{... | collective-permute-start | bytes 451592 | tf_op jit(solution)/shard_map/ppermute | solution.py:583
  440.7 6.9 %collective-permute-start.27 = (bf16[98,1152]{1,0:T(8,128)(2,1)S(1)}, bf16[98,1152]{1,0:T(8,128)(2,1)S(1)}, u32[]{:S(2)}, u32[]{:S(2)}) collective-permute-start(bf16[98,1152]{1,0:T(8,128)(2,1)S(1)} %fusion.14), channel_id=1, source_target_pairs={{0,2},{1,3},{2,0},{3,1},{4,6},{5,7},{6,4},{7,5},{8,10},{9,11},{10,... | collective-permute-start | bytes 677384 | tf_op jit(solution)/shard_map/ppermute | solution.py:583
  447.7 4.8 %collective-permute-start.28 = (bf16[98,1152]{1,0:T(8,128)(2,1)S(1)}, bf16[98,1152]{1,0:T(8,128)(2,1)S(1)}, u32[]{:S(2)}, u32[]{:S(2)}) collective-permute-start(bf16[98,1152]{1,0:T(8,128)(2,1)S(1)} %add_convert_fusion.16), channel_id=1, source_target_pairs={{0,1},{1,0},{2,3},{3,2},{4,5},{5,4},{6,7},{7,6},{8,9},{9,8},{10,11... | collective-permute-start | bytes 677384 | tf_op jit(solution)/shard_map/ppermute | solution.py:583
  (10 other events, 7.6 us)
Sparse Core Ops, SparseCore 0:
  29.9 89.2 all-gather.1
  287.9 80.5 reduce-scatter.1

commit v5 on v4

--- a/solution.py
+++ b/solution.py
@@ -768,7 +768,7 @@
     by_column = by_column.reshape(8, size, share).transpose(1, 0, 2)
     small = jnp.concatenate([by_column, ffn_sum.reshape(size, -1, share)], axis=1).astype(BF).reshape(size, -1)
     count = small.shape[1]
-    extra = -(-count // 768)
+    extra = -(-count // 6144) * 8
     small = jnp.pad(small, ((0, 0), (0, extra * 768 - count))).reshape(size, extra, 768)
     halves = [pick([t.reshape(size, share, -1) for t in ts], *groups[0]) for ts in ((keep_d, from_core_d), (keep_e, from_core_e))]
     picked = [

time: 469 us -> 468 us (level)
    convert_element_type x15 -> x16, other arithmetic: 23.6 us -> 22.5 us  [add(): return total.astype(BF)]
    unnamed x112 -> x117, local copies, waits for them, and re-layouts: 23.4 us -> 23.9 us
  transfers between devices with their start and end apart: 31 -> 31, of which waited for: 7 -> 7; matrix products, arithmetic and copies ran while one was open for 18% -> 17% of each run, Pallas kernels for 37% -> 37%
where the time goes in v5:
time: 468 us; the launch traced here: 463 us
  Pallas kernels  270 us (58%)
  local copies, waits for them, and re-layouts  49.7 us (11%)
  other arithmetic  46.5 us (10%)
  waiting for transfers between devices  44.6 us (10%)
  starting transfers between devices  36.9 us (8%)
  between operations  15.2 us (3%)
    pallas_call x1, Pallas kernels, middle(): pl.pallas_call(functools.partial(mid_kernel, T, direct), grid=(FF // F,),...  98.6 us
    pallas_call x3, Pallas kernels, attn_bwd(): pl.pallas_call(kernel, grid=(pairs, rows), in_specs=[pl.BlockSpec(memory_...  92.6 us
    pallas_call x3, Pallas kernels, attn_fwd(): pl.pallas_call(kernel, grid=(rows, pairs), in_specs=[pl.BlockSpec((length...  43.8 us
    ppermute x29, waiting for transfers between devices, swap(): return lax.ppermute(x, axis, [(i, i ^ mask) for i in range(size)])  40.2 us
    ppermute x29, starting transfers between devices, swap(): return lax.ppermute(x, axis, [(i, i ^ mask) for i in range(size)])  36.8 us
    unnamed x117, local copies, waits for them, and re-layouts  23.9 us
    convert_element_type x16, other arithmetic, add(): return total.astype(BF)  22.5 us
    pallas_call x2, Pallas kernels, project(): pl.pallas_call(functools.partial(project_kernel, order, rows, half), grid...  18.3 us
  transfers between devices with their start and end apart: 31, of which 7 were waited for; matrix products, arithmetic and copies ran while one was open for 17% of the time, Pallas kernels for 37%

profile of v5, /device:TPU:1, one launch (start us, length us, event | category | flops | bytes accessed | tf_op | source)
XLA Modules:
  0.0 462.6 jit_solution(4413110877161210150)
XLA Ops:
  7.2 1.5 reshape.401
  10.4 2.1 collective-permute-start
  12.5 2.3 collective-permute-start.1
  15.9 3.2 collective-permute-start.6
  19.8 2.1 fusion.25
  21.9 1.7 dynamic-slice_dynamic-update-slice_fusion
  23.6 1.5 dynamic-slice_dynamic-update-slice_fusion.4
  25.1 1.5 dynamic-slice_dynamic-update-slice_fusion.3
  26.6 1.5 dynamic-slice_dynamic-update-slice_fusion.2
  28.2 1.5 dynamic-slice_dynamic-update-slice_fusion.1
  31.7 1.1 fusion.1
  33.4 1.1 pad_maximum_fusion.4
  34.5 1.3 collective-permute-start.3
  35.8 1.5 constant_dynamic-update-slice_fusion.3
  37.3 1.5 constant_dynamic-update-slice_fusion.2
  38.9 1.6 constant_dynamic-update-slice_fusion.1
  40.4 1.8 pad_maximum_fusion.3
  46.2 9.3 %collective-permute-start.4 = (bf16[8,112,384]{2,1,0:T(8,128)(2,1)}, bf16[8,112,384]{2,1,0:T(8,128)(2,1)}, u32[]{:S(2)}, u32[]{:S(2)}) collective-permute-start(bf16[8,112,384]{2,1,0:T(8,128)(2,1)} %constant_dynamic-update-slice_fusion.mine), channel_id=1, source_target_pairs={{0,1},{1,0},{2,3},{3,2},{4,5},{5,4},{6,7},{7,6},{8,9},{9,8},{10,11... | collective-permute-start | bytes 2064392 | tf_op jit(solution)/shard_map/ppermute | solution.py:583
  58.0 3.2 add_convert_fusion.n1
  61.2 1.2 collective-permute-done.8
  62.4 1.1 constant_dynamic-update-slice_fusion.5.mine
  63.5 2.5 collective-permute-start.9
  66.1 7.6 %project.2 = (bf16[2048,768]{1,0:T(8,128)(2,1)}, bf16[768,768]{1,0:T(8,128)(2,1)}) custom-call(s32[2]{0:T(128)} %pad_add_fusion.at, bf16[2048,768]{1,0:T(8,128)(2,1)} %add_convert_fusion.n1, bf16[8,112,384]{2,1,0:T(8,128)(2,1)} %constant_dynamic-update-slice_fusion.mine, bf16[8,112,384]{2,1,0:T(8,128)(2,1)} %collective-permute-done.4.other, ...), custom_call_target="tpu_custom_call" | custom-call | flops 4831838208 | bytes 9437184 | tf_op jit(solution)/shard_map/project/pallas_call | solution.py:553
  73.7 14.6 %attention_forward.3 = (bf16[2048,256]{1,0:T(8,128)(2,1)}, bf16[2048,256]{1,0:T(8,128)(2,1)}) custom-call(bf16[2048,768]{1,0:T(8,128)(2,1)} %get-tuple-element.45.x_ref.x), custom_call_target="tpu_custom_call" | custom-call | flops 16106127360 | bytes 5242880 | tf_op jit(solution)/shard_map/attention_forward/pallas_call | solution.py:74
  88.3 1.1 copy-done.43
  89.4 10.7 %project.3 = (bf16[2048,1536]{1,0:T(8,128)(2,1)}, bf16[768,1536]{1,0:T(8,128)(2,1)}) custom-call(s32[2]{0:T(128)} %pad_add_fusion.at, bf16[2048,768]{1,0:T(8,128)(2,1)} %add_convert_fusion.n1, bf16[8,96,768]{2,1,0:T(8,128)(2,1)} %copy-done.33, bf16[8,96,768]{2,1,0:T(8,128)(2,1)} %copy-done.43, f32[1,1536]{1,0:T(1,128)} %slice.305.bias, ...), custom_call_target="tpu_custom_call" | custom-call | flops 9663676416 | bytes 12582912 | tf_op jit(solution)/shard_map/project/pallas_call | solution.py:553
  100.2 14.6 %attention_forward.4 = (bf16[2048,256]{1,0:T(8,128)(2,1)}, bf16[2048,256]{1,0:T(8,128)(2,1)}) custom-call(bf16[2048,1536]{1,0:T(8,128)(2,1)} %get-tuple-element.47.x_ref.x), custom_call_target="tpu_custom_call" | custom-call | flops 16106127360 | bytes 5242880 | tf_op jit(solution)/shard_map/attention_forward/pallas_call | solution.py:74
  114.8 4.3 all-gather.2.cloned.1.call-done.a
  119.1 1.5 collective-permute-start.10
  120.7 4.4 multiply_convert_fusion
  126.1 2.9 copy.55.t
  130.3 14.6 %attention_forward.5 = (bf16[2048,256]{1,0:T(8,128)(2,1)}, bf16[2048,256]{1,0:T(8,128)(2,1)}) custom-call(bf16[2048,1536]{1,0:T(8,128)(2,1)} %get-tuple-element.47.x_ref.x, bf16[768,3456]{1,0:T(8,128)(2,1)} %tie.8.refs_0_.mine.back_mine), custom_call_target="tpu_custom_call" | custom-call | flops 16106127360 | bytes 5242880 | tf_op jit(solution)/shard_map/attention_forward/pallas_call | solution.py:74
  144.9 98.6 %feed_forward.1 = (bf16[2048,768]{1,0:T(8,128)(2,1)}, f32[2048,768]{1,0:T(8,128)}, bf16[2048,768]{1,0:T(8,128)(2,1)}, bf16[8,480,384]{2,1,0:T(8,128)(2,1)}, bf16...) custom-call(s32[1]{0:T(128)} %bitcast.at, ...), custom_call_target="tpu_custom_call" | custom-call | flops 115964116992 | bytes 53477376 | tf_op jit(solution)/shard_map/feed_forward/pallas_call | solution.py:428
  244.4 30.8 %attention_backward.3 = (bf16[2048,768]{1,0:T(8,128)(2,1)}, bf16[768,384]{1,0:T(8,128)(2,1)}, bf16[768,384]{1,0:T(8,128)(2,1)}, f32[8,768]{1,0:T(8,128)}) custom-call(s32[1]{0:T(128)} %bitcast.at, bf16[2048,1536]{1,0:T(8,128)(2,1)} %get-tuple-element.47.x_ref.x, bf16[2048,256]{1,0:T(8,128)(2,1)} %get-tuple-element.49.m2_any.o, ...), custom_call_target="tpu_custom_call" | custom-call | flops 30064771072 | bytes 9437184 | tf_op jit(solution)/shard_map/attention_backward/pallas_call | solution.py:176
  280.6 4.5 add_convert_fusion.3
  285.4 2.4 add_convert_fusion.1.refs_0_
  287.8 30.9 %attention_backward.4 = (bf16[2048,768]{1,0:T(8,128)(2,1)}, bf16[768,384]{1,0:T(8,128)(2,1)}, bf16[768,384]{1,0:T(8,128)(2,1)}, f32[8,768]{1,0:T(8,128)}) custom-call(s32[1]{0:T(128)} %bitcast.at, bf16[2048,1536]{1,0:T(8,128)(2,1)} %get-tuple-element.47.x_ref.x, bf16[2048,256]{1,0:T(8,128)(2,1)} %get-tuple-element.48.b.m1_any.o, ...), custom_call_target="tpu_custom_call" | custom-call | flops 30064771072 | bytes 9437184 | tf_op jit(solution)/shard_map/attention_backward/pallas_call | solution.py:176
  320.7 2.0 fusion.10
  322.8 1.2 collective-permute-start.16
  324.0 2.6 fusion.3
  326.7 30.9 %attention_backward.5 = (bf16[2048,768]{1,0:T(8,128)(2,1)}, bf16[768,384]{1,0:T(8,128)(2,1)}, bf16[768,384]{1,0:T(8,128)(2,1)}, f32[8,768]{1,0:T(8,128)}) custom-call(s32[1]{0:T(128)} %bitcast.at, bf16[2048,768]{1,0:T(8,128)(2,1)} %get-tuple-element.45.x_ref.x, bf16[2048,256]{1,0:T(8,128)(2,1)} %get-tuple-element.46.refs_0_.m0_any.o, ...), custom_call_target="tpu_custom_call" | custom-call | flops 30064771072 | bytes 9437184 | tf_op jit(solution)/shard_map/attention_backward/pallas_call | solution.py:176
  360.2 1.6 fusion.16.refs_8_
  361.8 1.3 collective-permute-start.25
  363.1 1.6 add_convert_fusion.19
  366.2 1.9 fusion.4
  368.1 1.3 collective-permute-start.20
  369.4 16.4 %input_gradient.1 = (f32[2048,768]{1,0:T(8,128)}, f32[2,768]{1,0:T(2,128)}) custom-call(bf16[2048,768]{1,0:T(8,128)(2,1)} %bitcast.149, f32[2048,768]{1,0:T(8,128)} %get-tuple-element.51.gh_ref, f32[1,768]{1,0:T(1,128)} %slice.253.gain_ref, bf16[2048,768]{1,0:T(8,128)(2,1)} %get-tuple-element.63.refs_0_, bf16[2048,768]{1,0:T(8,128)(2,1)} %get-tuple-element.64.refs_1_, ...), custom_call_target="tpu_custom_call" | custom-call | flops 14495514624 | bytes 25165824 | tf_op jit(solution)/shard_map/input_gradient/pallas_call | solution.py:505
  387.7 1.9 pad_maximum_fusion
  389.6 1.2 collective-permute-start.21
  390.8 1.0 fusion.11
  394.4 11.4 %collective-permute-done.21 = bf16[864,384]{1,0:T(8,128)(2,1)} collective-permute-done((bf16[864,384]{1,0:T(8,128)(2,1)}, bf16[864,384]{1,0:T(8,128)(2,1)}, u32[]{:S(2)}, u32[]{:S(2)}) %collective-permute-start.21) | collective-permute-done | bytes 663584 | tf_op jit(solution)/shard_map/ppermute | solution.py:583
  405.8 1.3 add_convert_fusion.4.b
  407.1 1.6 collective-permute-start.23
  409.6 1.2 collective-permute-start.26
  410.9 5.4 %collective-permute-done.26 = bf16[1,96,384]{2,1,0:T(8,128)(2,1)S(1)} collective-permute-done((bf16[1,96,384]{2,1,0:T(8,128)(2,1)S(1)}, bf16[1,96,384]{2,1,0:T(8,128)(2,1)S(1)}, u32[]{:S(2)}, u32[]{:S(2)}) %collective-permute-start.26) | collective-permute-done | bytes 73760 | tf_op jit(solution)/shard_map/ppermute | solution.py:583
  418.0 1.3 add_convert_fusion.8
  420.3 7.7 %collective-permute-done.22.a = bf16[2,104,768]{2,1,0:T(8,128)(2,1)S(1)} collective-permute-done((bf16[2,104,768]{2,1,0:T(8,128)(2,1)S(1)}, bf16[2,104,768]{2,1,0:T(8,128)(2,1)S(1)}, u32[]{:S(2)}, u32[]{:S(2)}) %collective-permute-start.22) | collective-permute-done | bytes 319520 | tf_op jit(solution)/shard_map/ppermute | solution.py:583
  430.0 10.1 %collective-permute-done.24 = bf16[1,104,768]{2,1,0:T(8,128)(2,1)S(1)} collective-permute-done((bf16[1,104,768]{2,1,0:T(8,128)(2,1)S(1)}, bf16[1,104,768]{2,1,0:T(8,128)(2,1)S(1)}, u32[]{:S(2)}, u32[]{:S(2)}) %collective-permute-start.24) | collective-permute-done | bytes 159776 | tf_op jit(solution)/shard_map/ppermute | solution.py:583
  440.9 1.2 collective-permute-start.27
  442.2 1.4 copy.76
  443.7 4.3 collective-permute-done.27
  448.0 1.5 collective-permute-start.28
  449.5 1.1 convert_element_type.549
  454.4 1.1 reshape.425
  (272 shorter events, 42.1 us)
Async XLA Ops:
  7.2 111.9 %all-gather.2.cloned.1.call-start = ((), (), s32[]{:S(2)}) async-start(), calls=%async_computation.1 | async-start | bytes 5971968 | tf_op jit(solution)/shard_map/all_gather | solution.py:692
  9.0 10.1 %copy-start.31 = (bf16[96,768]{1,0:T(8,128)(2,1)S(1)}, bf16[96,768]{1,0:T(8,128)(2,1)}, u32[]{:S(2)}) copy-start(bf16[96,768]{1,0:T(8,128)(2,1)} %param.18) | copy-start | bytes 442372
  10.4 23.0 %collective-permute-start = (bf16[1,112,384]{2,1,0:T(8,128)(2,1)}, bf16[1,112,384]{2,1,0:T(8,128)(2,1)}, u32[]{:S(2)}, u32[]{:S(2)}) collective-permute-start(bf16[1,112,384]{2,1,0:T(8,128)(2,1)} %maximum_bitcast_fusion), channel_id=1, source_target_pairs={{0,8},{4,12},{8,0},{12,4},{16,24},{20,28},{24,16},{28,20},{1,9},{5... | collective-permute-start | bytes 258056 | tf_op jit(solution)/shard_map/ppermute | solution.py:583
  12.5 20.9 %collective-permute-start.1 = (bf16[1,112,384]{2,1,0:T(8,128)(2,1)}, bf16[1,112,384]{2,1,0:T(8,128)(2,1)}, u32[]{:S(2)}, u32[]{:S(2)}) collective-permute-start(bf16[1,112,384]{2,1,0:T(8,128)(2,1)} %maximum_bitcast_fusion), channel_id=1, source_target_pairs={{0,16},{4,20},{8,24},{12,28},{16,0},{20,4},{24,8},{28,12},{1,17},{... | collective-permute-start | bytes 258056 | tf_op jit(solution)/shard_map/ppermute | solution.py:583
  14.8 18.6 %collective-permute-start.2 = (bf16[1,112,384]{2,1,0:T(8,128)(2,1)}, bf16[1,112,384]{2,1,0:T(8,128)(2,1)}, u32[]{:S(2)}, u32[]{:S(2)}) collective-permute-start(bf16[1,112,384]{2,1,0:T(8,128)(2,1)} %maximum_bitcast_fusion), channel_id=1, source_target_pairs={{0,24},{4,28},{8,16},{12,20},{16,8},{20,12},{24,0},{28,4},{1,25},{... | collective-permute-start | bytes 258056 | tf_op jit(solution)/shard_map/ppermute | solution.py:583
  15.6 24.8 %collective-permute-start.5 = (bf16[1,96,768]{2,1,0:T(8,128)(2,1)}, bf16[1,96,768]{2,1,0:T(8,128)(2,1)S(1)}, u32[]{:S(2)}, u32[]{:S(2)}) collective-permute-start(bf16[1,96,768]{2,1,0:T(8,128)(2,1)} %get-tuple-element.113), channel_id=1, source_target_pairs={{0,8},{4,12},{8,0},{12,4},{16,24},{20,28},{24,16},{28,20},{1,9},{5... | collective-permute-start | bytes 442376 | tf_op jit(solution)/shard_map/ppermute | solution.py:583
  15.9 24.5 %collective-permute-start.6 = (bf16[1,96,768]{2,1,0:T(8,128)(2,1)}, bf16[1,96,768]{2,1,0:T(8,128)(2,1)S(1)}, u32[]{:S(2)}, u32[]{:S(2)}) collective-permute-start(bf16[1,96,768]{2,1,0:T(8,128)(2,1)} %get-tuple-element.113), channel_id=1, source_target_pairs={{0,16},{4,20},{8,24},{12,28},{16,0},{20,4},{24,8},{28,12},{1,17},{... | collective-permute-start | bytes 442376 | tf_op jit(solution)/shard_map/ppermute | solution.py:583
  19.8 10.0 %copy-start = (s32[8]{0:T(128)S(1)}, s32[8]{0:T(128)}, u32[]{:S(2)}) copy-start(s32[8]{0:T(128)} %constant.176) | copy-start | bytes 100
  19.8 11.4 %copy-start.1 = (bf16[2,1024,768]{2,1,0:T(8,128)(2,1)S(1)}, bf16[2,1024,768]{2,1,0:T(8,128)(2,1)}, u32[]{:S(2)}) copy-start(bf16[2,1024,768]{2,1,0:T(8,128)(2,1)} %param.13) | copy-start | bytes 9437188
  29.7 357.9 %reduce-scatter.2.cloned.1.call-start = ((), (), s32[]{:S(2)}) async-start(), calls=%async_computation.2 | async-start | bytes 3317760 | tf_op jit(solution)/shard_map/reduce_scatter | solution.py:745
  33.4 7.0 %collective-permute-start.7 = (bf16[1,96,768]{2,1,0:T(8,128)(2,1)}, bf16[1,96,768]{2,1,0:T(8,128)(2,1)S(1)}, u32[]{:S(2)}, u32[]{:S(2)}) collective-permute-start(bf16[1,96,768]{2,1,0:T(8,128)(2,1)} %get-tuple-element.113), channel_id=1, source_target_pairs={{0,24},{4,28},{8,16},{12,20},{16,8},{20,12},{24,0},{28,4},{1,25},{... | collective-permute-start | bytes 442376 | tf_op jit(solution)/shard_map/ppermute | solution.py:583
  34.5 10.0 %collective-permute-start.3 = (bf16[4,112,384]{2,1,0:T(8,128)(2,1)S(1)}, bf16[4,112,384]{2,1,0:T(8,128)(2,1)S(1)}, u32[]{:S(2)}, u32[]{:S(2)}) collective-permute-start(bf16[4,112,384]{2,1,0:T(8,128)(2,1)S(1)} %pad_maximum_fusion.4), channel_id=1, source_target_pairs={{0,4},{4,0},{8,12},{12,8},{16,20},{20,16},{24,28},{28,24},{1,5},{5... | collective-permute-start | bytes 1032200 | tf_op jit(solution)/shard_map/ppermute | solution.py:583
  42.2 20.2 %collective-permute-start.8 = (bf16[4,96,768]{2,1,0:T(8,128)(2,1)}, bf16[4,96,768]{2,1,0:T(8,128)(2,1)}, u32[]{:S(2)}, u32[]{:S(2)}) collective-permute-start(bf16[4,96,768]{2,1,0:T(8,128)(2,1)} %pad_maximum_fusion.3), channel_id=1, source_target_pairs={{0,4},{4,0},{8,12},{12,8},{16,20},{20,16},{24,28},{28,24},{1,5},{5... | collective-permute-start | bytes 1769480 | tf_op jit(solution)/shard_map/ppermute | solution.py:583
  46.2 19.9 %collective-permute-start.4 = (bf16[8,112,384]{2,1,0:T(8,128)(2,1)}, bf16[8,112,384]{2,1,0:T(8,128)(2,1)}, u32[]{:S(2)}, u32[]{:S(2)}) collective-permute-start(bf16[8,112,384]{2,1,0:T(8,128)(2,1)} %constant_dynamic-update-slice_fusion.mine), channel_id=1, source_target_pairs={{0,1},{1,0},{2,3},{3,2},{4,5},{5,4},{6,7},{7,6},{8,9},{9,8},{10,11... | collective-permute-start | bytes 2064392 | tf_op jit(solution)/shard_map/ppermute | solution.py:583
  58.0 4.4 copy-start.32
  63.5 10.2 %copy-start.33 = (bf16[8,96,768]{2,1,0:T(8,128)(2,1)}, bf16[8,96,768]{2,1,0:T(8,128)(2,1)S(1)}, u32[]{:S(2)}) copy-start(bf16[8,96,768]{2,1,0:T(8,128)(2,1)S(1)} %constant_dynamic-update-slice_fusion.5.mine) | copy-start | bytes 3538948
  63.5 24.8 %collective-permute-start.9 = (bf16[8,96,768]{2,1,0:T(8,128)(2,1)S(1)}, bf16[8,96,768]{2,1,0:T(8,128)(2,1)S(1)}, u32[]{:S(2)}, u32[]{:S(2)}) collective-permute-start(bf16[8,96,768]{2,1,0:T(8,128)(2,1)S(1)} %constant_dynamic-update-slice_fusion.5.mine), channel_id=1, source_target_pairs={{0,1},{1,0},{2,3},{3,2},{4,5},{5,4},{6,7},{7,6},{8,9},{9,8},{10,11... | collective-permute-start | bytes 3538952 | tf_op jit(solution)/shard_map/ppermute | solution.py:583
  88.3 1.1 copy-start.43
  119.1 1.5 copy-start.44
  119.1 1.5 copy-start.37
  119.1 25.8 %collective-permute-start.10 = (bf16[768,3456]{1,0:T(8,128)(2,1)}, bf16[768,3456]{1,0:T(8,128)(2,1)}, u32[]{:S(2)}, u32[]{:S(2)}) collective-permute-start(bf16[768,3456]{1,0:T(8,128)(2,1)} %tie.8.refs_0_.mine.back_mine), channel_id=1, source_target_pairs={{0,1},{1,0},{2,3},{3,2},{4,5},{5,4},{6,7},{7,6},{8,9},{9,8},{10,11... | collective-permute-start | bytes 15925256 | tf_op jit(solution)/shard_map/ppermute | solution.py:583
  120.7 5.4 %copy-start.2 = (bf16[2048,768]{1,0:T(8,128)(2,1)S(1)}, bf16[2048,768]{1,0:T(8,128)(2,1)}, u32[]{:S(2)}) copy-start(bf16[2048,768]{1,0:T(8,128)(2,1)} %add_convert_fusion.n1) | copy-start | bytes 9437188
  243.5 41.9 %collective-permute-start.14 = (bf16[8,480,384]{2,1,0:T(8,128)(2,1)}, bf16[8,480,384]{2,1,0:T(8,128)(2,1)S(1)}, u32[]{:S(2)}, u32[]{:S(2)}) collective-permute-start(bf16[8,480,384]{2,1,0:T(8,128)(2,1)} %get-tuple-element.61), channel_id=1, source_target_pairs={{0,1},{1,0},{2,3},{3,2},{4,5},{5,4},{6,7},{7,6},{8,9},{9,8},{10,11... | collective-permute-start | bytes 8847368 | tf_op jit(solution)/shard_map/ppermute | solution.py:583
  244.3 36.3 %collective-permute-start.11 = (bf16[8,384,384]{2,1,0:T(8,128)(2,1)}, bf16[8,384,384]{2,1,0:T(8,128)(2,1)}, u32[]{:S(2)}, u32[]{:S(2)}) collective-permute-start(bf16[8,384,384]{2,1,0:T(8,128)(2,1)} %get-tuple-element.55), channel_id=1, source_target_pairs={{0,1},{1,0},{2,3},{3,2},{4,5},{5,4},{6,7},{7,6},{8,9},{9,8},{10,11... | collective-permute-start | bytes 7077896 | tf_op jit(solution)/shard_map/ppermute | solution.py:583
  275.1 44.8 %collective-permute-start.13 = (bf16[768,384]{1,0:T(8,128)(2,1)}, bf16[768,384]{1,0:T(8,128)(2,1)S(1)}, u32[]{:S(2)}, u32[]{:S(2)}) collective-permute-start(bf16[768,384]{1,0:T(8,128)(2,1)} %get-tuple-element.58), channel_id=1, source_target_pairs={{0,1},{1,0},{2,3},{3,2},{4,5},{5,4},{6,7},{7,6},{8,9},{9,8},{10,11... | collective-permute-start | bytes 1769480 | tf_op jit(solution)/shard_map/ppermute | solution.py:583
  280.6 4.8 %copy-start.7 = (bf16[8,480,384]{2,1,0:T(8,128)(2,1)S(1)}, bf16[8,480,384]{2,1,0:T(8,128)(2,1)}, u32[]{:S(2)}) copy-start(bf16[8,480,384]{2,1,0:T(8,128)(2,1)} %get-tuple-element.60) | copy-start | bytes 8847364
  285.1 38.9 %collective-permute-start.12 = (bf16[4,384,384]{2,1,0:T(8,128)(2,1)}, bf16[4,384,384]{2,1,0:T(8,128)(2,1)}, u32[]{:S(2)}, u32[]{:S(2)}) collective-permute-start(bf16[4,384,384]{2,1,0:T(8,128)(2,1)} %get-tuple-element.115.refs_3_), channel_id=1, source_target_pairs={{0,4},{4,0},{8,12},{12,8},{16,20},{20,16},{24,28},{28,24},{1,5},{5... | collective-permute-start | bytes 3538952 | tf_op jit(solution)/shard_map/ppermute | solution.py:583
  318.7 2.0 copy-start.26
  318.7 46.0 %collective-permute-start.17 = (bf16[768,384]{1,0:T(8,128)(2,1)}, bf16[768,384]{1,0:T(8,128)(2,1)S(1)}, u32[]{:S(2)}, u32[]{:S(2)}) collective-permute-start(bf16[768,384]{1,0:T(8,128)(2,1)} %get-tuple-element.69), channel_id=1, source_target_pairs={{0,1},{1,0},{2,3},{3,2},{4,5},{5,4},{6,7},{7,6},{8,9},{9,8},{10,11... | collective-permute-start | bytes 1769480 | tf_op jit(solution)/shard_map/ppermute | solution.py:583
  320.7 3.2 copy-start.6
  322.8 3.8 copy-start.28
  322.8 36.7 %collective-permute-start.16 = (bf16[4,96,384]{2,1,0:T(8,128)(2,1)S(1)}, bf16[4,96,384]{2,1,0:T(8,128)(2,1)S(1)}, u32[]{:S(2)}, u32[]{:S(2)}) collective-permute-start(bf16[4,96,384]{2,1,0:T(8,128)(2,1)S(1)} %get-tuple-element.124.refs_3_), channel_id=1, source_target_pairs={{0,4},{4,0},{8,12},{12,8},{16,20},{20,16},{24,28},{28,24},{1,5},{5... | collective-permute-start | bytes 884744 | tf_op jit(solution)/shard_map/ppermute | solution.py:583
  326.6 38.3 %collective-permute-start.15 = (bf16[2,384,384]{2,1,0:T(8,128)(2,1)}, bf16[2,384,384]{2,1,0:T(8,128)(2,1)S(1)}, u32[]{:S(2)}, u32[]{:S(2)}) collective-permute-start(bf16[2,384,384]{2,1,0:T(8,128)(2,1)} %get-tuple-element.116.refs_1_), channel_id=1, source_target_pairs={{0,8},{4,12},{8,0},{12,4},{16,24},{20,28},{24,16},{28,20},{1,9},{5... | collective-permute-start | bytes 1769480 | tf_op jit(solution)/shard_map/ppermute | solution.py:583
  326.7 32.5 %copy-start.38 = (bf16[2,3,128]{2,1,0:T(4,128)(2,1)S(1)}, bf16[2,3,128]{2,1,0:T(4,128)(2,1)}, u32[]{:S(2)}) copy-start(bf16[2,3,128]{2,1,0:T(4,128)(2,1)} %concatenate.82) | copy-start | bytes 4612
  357.6 2.6 copy-start.19
  357.6 7.1 %copy-start.10 = (bf16[768,384]{1,0:T(8,128)(2,1)S(1)}, bf16[768,384]{1,0:T(8,128)(2,1)}, u32[]{:S(2)}) copy-start(bf16[768,384]{1,0:T(8,128)(2,1)} %get-tuple-element.62.b.refs_4_) | copy-start | bytes 1769476
  357.6 34.7 %collective-permute-start.18 = (bf16[768,384]{1,0:T(8,128)(2,1)}, bf16[768,384]{1,0:T(8,128)(2,1)S(1)}, u32[]{:S(2)}, u32[]{:S(2)}) collective-permute-start(bf16[768,384]{1,0:T(8,128)(2,1)} %get-tuple-element.71), channel_id=1, source_target_pairs={{0,1},{1,0},{2,3},{3,2},{4,5},{5,4},{6,7},{7,6},{8,9},{9,8},{10,11... | collective-permute-start | bytes 1769480 | tf_op jit(solution)/shard_map/ppermute | solution.py:583
  361.8 32.5 %collective-permute-start.25 = (bf16[2,96,384]{2,1,0:T(8,128)(2,1)}, bf16[2,96,384]{2,1,0:T(8,128)(2,1)}, u32[]{:S(2)}, u32[]{:S(2)}) collective-permute-start(bf16[2,96,384]{2,1,0:T(8,128)(2,1)} %fusion.16.refs_8_), channel_id=1, source_target_pairs={{0,8},{4,12},{8,0},{12,4},{16,24},{20,28},{24,16},{28,20},{1,9},{5... | collective-permute-start | bytes 442376 | tf_op jit(solution)/shard_map/ppermute | solution.py:583
  364.7 1.0 copy-start.25
  364.7 1.5 copy-start.13
  368.1 1.3 copy-start.29
  368.1 17.7 %collective-permute-start.20 = (bf16[1,384,384]{2,1,0:T(8,128)(2,1)S(1)}, bf16[1,384,384]{2,1,0:T(8,128)(2,1)S(1)}, u32[]{:S(2)}, u32[]{:S(2)}) collective-permute-start(bf16[1,384,384]{2,1,0:T(8,128)(2,1)S(1)} %get-tuple-element.122.refs_6_), channel_id=1, source_target_pairs={{0,16},{4,20},{8,24},{12,28},{16,0},{20,4},{24,8},{28,12},{1,17},{... | collective-permute-start | bytes 884744 | tf_op jit(solution)/shard_map/ppermute | solution.py:583
  369.4 17.1 %copy-start.18 = (bf16[1,384,384]{2,1,0:T(8,128)(2,1)S(1)}, bf16[1,384,384]{2,1,0:T(8,128)(2,1)}, u32[]{:S(2)}) copy-start(bf16[1,384,384]{2,1,0:T(8,128)(2,1)} %get-tuple-element.123.refs_5_) | copy-start | bytes 884740
  387.6 4.3 copy-start.30
  387.6 4.5 copy-start.34
  387.6 4.5 copy-start.35
  387.6 4.5 copy-start.36
  387.6 4.7 %copy-start.5 = (bf16[768,384]{1,0:T(8,128)(2,1)S(1)}, bf16[768,384]{1,0:T(8,128)(2,1)}, u32[]{:S(2)}) copy-start(bf16[768,384]{1,0:T(8,128)(2,1)} %get-tuple-element.68.b) | copy-start | bytes 1769476
  389.6 16.1 %collective-permute-start.21 = (bf16[864,384]{1,0:T(8,128)(2,1)}, bf16[864,384]{1,0:T(8,128)(2,1)}, u32[]{:S(2)}, u32[]{:S(2)}) collective-permute-start(bf16[864,384]{1,0:T(8,128)(2,1)} %pad_maximum_fusion), channel_id=1, source_target_pairs={{0,2},{1,3},{2,0},{3,1},{4,6},{5,7},{6,4},{7,5},{8,10},{9,11},{10,... | collective-permute-start | bytes 1990664 | tf_op jit(solution)/shard_map/ppermute | solution.py:583
  392.4 13.4 %copy-start.14 = (bf16[480,384]{1,0:T(8,128)(2,1)S(1)}, bf16[480,384]{1,0:T(8,128)(2,1)}, u32[]{:S(2)}) copy-start(bf16[480,384]{1,0:T(8,128)(2,1)} %reduce-scatter.2.cloned.1.call-done) | copy-start | bytes 1105924
  394.0 16.7 %copy-start.24 = (bf16[768,384]{1,0:T(8,128)(2,1)S(1)}, bf16[768,384]{1,0:T(8,128)(2,1)}, u32[]{:S(2)}) copy-start(bf16[768,384]{1,0:T(8,128)(2,1)} %copy-done.23) | copy-start | bytes 1769476
  394.0 23.1 %collective-permute-start.19 = (bf16[4,104,768]{2,1,0:T(8,128)(2,1)}, bf16[4,104,768]{2,1,0:T(8,128)(2,1)S(1)}, u32[]{:S(2)}, u32[]{:S(2)}) collective-permute-start(bf16[4,104,768]{2,1,0:T(8,128)(2,1)} %pad_maximum_fusion.2), channel_id=1, source_target_pairs={{0,4},{4,0},{8,12},{12,8},{16,20},{20,16},{24,28},{28,24},{1,5},{5... | collective-permute-start | bytes 1916936 | tf_op jit(solution)/shard_map/ppermute | solution.py:583
  407.0 10.1 %copy-start.3 = (bf16[864,384]{1,0:T(8,128)(2,1)}, bf16[864,384]{1,0:T(8,128)(2,1)S(1)}, u32[]{:S(2)}) copy-start(bf16[864,384]{1,0:T(8,128)(2,1)S(1)} %add_convert_fusion.4.b) | copy-start | bytes 1990660
  407.0 9.2 %copy-start.27 = (bf16[2,1,96,384]{3,2,1,0:T(8,128)(2,1)S(1)}, bf16[2,1,96,384]{3,2,1,0:T(8,128)(2,1)}, u32[]{:S(2)}) copy-start(bf16[2,1,96,384]{3,2,1,0:T(8,128)(2,1)} %add_convert_fusion.19) | copy-start | bytes 442372
  407.1 12.3 %collective-permute-start.23 = (bf16[864,384]{1,0:T(8,128)(2,1)S(1)}, bf16[864,384]{1,0:T(8,128)(2,1)S(1)}, u32[]{:S(2)}, u32[]{:S(2)}) collective-permute-start(bf16[864,384]{1,0:T(8,128)(2,1)S(1)} %add_convert_fusion.4.b), channel_id=1, source_target_pairs={{0,1},{1,0},{2,3},{3,2},{4,5},{5,4},{6,7},{7,6},{8,9},{9,8},{10,11... | collective-permute-start | bytes 1990664 | tf_op jit(solution)/shard_map/ppermute | solution.py:583
  409.6 6.7 %collective-permute-start.26 = (bf16[1,96,384]{2,1,0:T(8,128)(2,1)S(1)}, bf16[1,96,384]{2,1,0:T(8,128)(2,1)S(1)}, u32[]{:S(2)}, u32[]{:S(2)}) collective-permute-start(bf16[1,96,384]{2,1,0:T(8,128)(2,1)S(1)} %fusion.17), channel_id=1, source_target_pairs={{0,16},{4,20},{8,24},{12,28},{16,0},{20,4},{24,8},{28,12},{1,17},{... | collective-permute-start | bytes 221192 | tf_op jit(solution)/shard_map/ppermute | solution.py:583
  418.0 1.4 copy-start.4
  419.3 8.7 %collective-permute-start.22 = (bf16[2,104,768]{2,1,0:T(8,128)(2,1)S(1)}, bf16[2,104,768]{2,1,0:T(8,128)(2,1)S(1)}, u32[]{:S(2)}, u32[]{:S(2)}) collective-permute-start(bf16[2,104,768]{2,1,0:T(8,128)(2,1)S(1)} %get-tuple-element.121), channel_id=1, source_target_pairs={{0,8},{4,12},{8,0},{12,4},{16,24},{20,28},{24,16},{28,20},{1,9},{5... | collective-permute-start | bytes 958472 | tf_op jit(solution)/shard_map/ppermute | solution.py:583
  428.7 11.4 %copy-start.16 = (bf16[2,104,768]{2,1,0:T(8,128)(2,1)S(1)}, bf16[2,104,768]{2,1,0:T(8,128)(2,1)}, u32[]{:S(2)}) copy-start(bf16[2,104,768]{2,1,0:T(8,128)(2,1)} %tie.14) | copy-start | bytes 958468
  429.8 10.4 %collective-permute-start.24 = (bf16[1,104,768]{2,1,0:T(8,128)(2,1)S(1)}, bf16[1,104,768]{2,1,0:T(8,128)(2,1)S(1)}, u32[]{:S(2)}, u32[]{:S(2)}) collective-permute-start(bf16[1,104,768]{2,1,0:T(8,128)(2,1)S(1)} %fusion.8), channel_id=1, source_target_pairs={{0,16},{4,20},{8,24},{12,28},{16,0},{20,4},{24,8},{28,12},{1,17},{... | collective-permute-start | bytes 479240 | tf_op jit(solution)/shard_map/ppermute | solution.py:583
  430.0 10.9 %copy-start.21 = (bf16[96,3072]{1,0:T(8,128)(2,1)}, bf16[96,3072]{1,0:T(8,128)(2,1)S(1)}, u32[]{:S(2)}) copy-start(bf16[96,3072]{1,0:T(8,128)(2,1)S(1)} %slice_dynamic-update-slice_fusion.2) | copy-start | bytes 1769476
  440.9 7.0 %collective-permute-start.27 = (bf16[104,1152]{1,0:T(8,128)(2,1)}, bf16[104,1152]{1,0:T(8,128)(2,1)S(1)}, u32[]{:S(2)}, u32[]{:S(2)}) collective-permute-start(bf16[104,1152]{1,0:T(8,128)(2,1)} %fusion.14), channel_id=1, source_target_pairs={{0,2},{1,3},{2,0},{3,1},{4,6},{5,7},{6,4},{7,5},{8,10},{9,11},{10,... | collective-permute-start | bytes 718856 | tf_op jit(solution)/shard_map/ppermute | solution.py:583
  442.2 1.4 copy-start.22
  448.0 3.3 collective-permute-start.28
  (12 other events, 9.3 us)
Sparse Core Ops, SparseCore 0:
  29.9 89.2 all-gather.1
  287.9 80.5 reduce-scatter.1
